TPU v7x, 256 devices: a whole 4x4x8 slice. The times are simulated.
256 devices in a mesh: tm: 16 (over z, y_lo), space: 16 (over y_hi, x, core).
Axes of the slice: x: 4, y: 4 (y_hi: 2, y_lo: 2; y = y_hi * 2 + y_lo), z: 8, core: 2. Of those that a mesh axis runs over, the one named last changes fastest.
Arguments:
- initial: float32 [64, 128, 128], P('space'), may hold values from -6 to 8
- guess: float32 [32, 64, 128, 128], P('tm', 'space'), may hold values from -6 to 8
- conductivity: float32 [64, 128, 128], P('space'), may hold values from 0.1 to 1
- source: float32 [64, 128, 128], P('space'), may hold values from -1.2 to 1.2
Outputs:
- updated: float32 [32, 64, 128, 128], P('tm', 'space')
All inputs are finite; a program needn't handle non-finite values.
Results may differ from a plain program's by a relative error of at most 0.00002.
Values sent between devices are 32-bit elements; how exact they have to be, the bound alone decides.
No kernel may reach another device: no remote copies, remote signals or barrier semaphores. Data moves between devices by JAX's collectives and lax.ppermute only.
A program may use at most 64 MiB of HBM per device.

v0:
```python
import jax
import jax.numpy as jnp
from jax import lax
from jax.sharding import PartitionSpec as P

fine_rate = 0.04
coarse_rate = 0.16


def with_halo(cells, sides, width):
    for axis, dim in sides:
        count = lax.axis_size(axis)
        ends = count - 1
        head = lax.slice_in_dim(cells, 0, width, axis=dim)
        tail = lax.slice_in_dim(cells, cells.shape[dim] - width, cells.shape[dim], axis=dim)
        cells = jnp.concatenate(
            [
                lax.ppermute(tail, axis, [(i, (i + 1) % count) for i in range(ends)]),
                cells,
                lax.ppermute(head, axis, [((i + 1) % count, i) for i in range(ends)]),
            ],
            axis=dim,
        )
    return cells


def passed_along(x, axis, by):
    size = lax.axis_size(axis)
    pairs = [(i, i + by) for i in range(size) if 0 <= i + by < size]
    return lax.ppermute(x, axis, pairs)


def divergence(padded_state, padded_cond):
    lead = padded_state.ndim - 3
    state = jnp.pad(padded_state, [(0, 0)] * lead + [(0, 0), (1, 1), (1, 1)])
    cond = jnp.pad(padded_cond, [(0, 0), (1, 1), (1, 1)])
    centre = state[..., 1:-1, 1:-1, 1:-1]
    cond_centre = cond[1:-1, 1:-1, 1:-1]
    pairs = [
        (state[..., 2:, 1:-1, 1:-1], cond[2:, 1:-1, 1:-1]),
        (state[..., :-2, 1:-1, 1:-1], cond[:-2, 1:-1, 1:-1]),
        (state[..., 1:-1, 2:, 1:-1], cond[1:-1, 2:, 1:-1]),
        (state[..., 1:-1, :-2, 1:-1], cond[1:-1, :-2, 1:-1]),
        (state[..., 1:-1, 1:-1, 2:], cond[1:-1, 1:-1, 2:]),
        (state[..., 1:-1, 1:-1, :-2], cond[1:-1, 1:-1, :-2]),
    ]
    total = jnp.zeros(centre.shape, jnp.float32)
    for neighbour, cond_next in pairs:
        total = total + 0.5 * (cond_centre + cond_next) * (neighbour - centre)
    return total


def fine_step(state, fields):
    width = state.shape[1]
    padded = with_halo(state, (("space", 1),), 1)
    cond = fields[0, 2 : width + 4]
    heat = fields[1, 3 : width + 3]
    return state + fine_rate * divergence(padded, cond) + heat


def relax(starts, fields):
    state = starts
    for turn in range(3):
        state = fine_step(state, fields)
    return state


def coarse_step(state, fields):
    width = state.shape[0]
    padded = with_halo(state, (("space", 0),), 1)
    return state + coarse_rate * divergence(padded, fields[0, 2 : width + 4])


def body(initial, guess, conductivity, source):
    fields = with_halo(jnp.stack([conductivity, source]), (("space", 1),), 3)
    leading = lax.axis_index("tm") == 0

    def starts_of(values):
        previous = passed_along(values[-1], "tm", 1)
        previous = jnp.where(leading, initial, previous)
        return jnp.concatenate([previous[None], values[:-1]], 0)

    lastf = relax(starts_of(guess), fields)
    cvals = fine_step(lastf, fields)
    lastf = relax(starts_of(cvals), fields)
    resid = fine_step(lastf, fields) - cvals
    count = resid.shape[0]

    def round_body(turn, carry):
        state = passed_along(carry[-1], "tm", 1)
        result = []
        for index in range(count):
            state = coarse_step(state, fields) + resid[index]
            result.append(state)
        return jnp.stack(result, 0)

    corr = lax.fori_loop(0, lax.axis_size("tm"), round_body, jnp.zeros_like(resid))
    return cvals + corr


def solution(mesh):
    placed = (
        P("space", None, None),
        P("tm", "space", None, None),
        P("space", None, None),
        P("space", None, None),
    )
    return jax.shard_map(
        body, mesh=mesh, in_specs=placed, out_specs=P("tm", "space", None, None), check_vma=False
    )
```

profile of v0, /device:TPU:144, one launch (start us, length us, event | category | flops | bytes accessed | tf_op | source)
XLA Modules:
  0.0 692.8 jit_solution(13491018574507436532)
XLA Ops:
  1.1 3.2 collective-permute-start.5
  4.3 8.8 %collective-permute-done.5 = f32[4,128,128]{2,1,0:T(8,128)S(1)} collective-permute-done((f32[4,128,128]{2,1,0:T(8,128)S(1)}, f32[4,128,128]{2,1,0:T(8,128)S(1)}, u32[]{:S(2)}, u32[]{:S(2)}) %collective-permute-start.5) | collective-permute-done | bytes 262176 | tf_op jit(solution)/shard_map/ppermute | solution.py:30
  13.2 3.0 collective-permute-start.7
  18.3 7.3 %collective-permute-start.6 = (f32[2,3,128,128]{3,2,1,0:T(8,128)S(1)}, f32[2,3,128,128]{3,2,1,0:T(8,128)S(1)}, u32[]{:S(2)}, u32[]{:S(2)}) collective-permute-start(f32[2,3,128,128]{3,2,1,0:T(8,128)S(1)} %get-tuple-element.113), channel_id=1, source_target_pairs={{1,0},{2,1},{3,2},{4,3},{5,4},{6,5},{7,6},{8,7},{9,8},{10,9},{11,1... | collective-permute-start | bytes 1179656 | tf_op jit(solution)/shard_map/ppermute | solution.py:20
  28.0 2.8 collective-permute-done.6
  30.8 7.4 %collective-permute-done.8 = f32[2,3,128,128]{3,2,1,0:T(8,128)S(1)} collective-permute-done((f32[2,3,128,128]{3,2,1,0:T(8,128)S(1)}, f32[2,3,128,128]{3,2,1,0:T(8,128)S(1)}, u32[]{:S(2)}, u32[]{:S(2)}) %collective-permute-start.8) | collective-permute-done | bytes 393248 | tf_op jit(solution)/shard_map/ppermute | solution.py:18
  43.8 7.4 %collective-permute-done.11 = f32[2,1,128,128]{3,2,1,0:T(8,128)S(1)} collective-permute-done((f32[2,1,128,128]{3,2,1,0:T(8,128)S(1)}, f32[2,1,128,128]{3,2,1,0:T(8,128)S(1)}, u32[]{:S(2)}, u32[]{:S(2)}) %collective-permute-start.11) | collective-permute-done | bytes 131104 | tf_op jit(solution)/shard_map/ppermute | solution.py:18
  56.7 7.5 %collective-permute-done.13 = f32[2,1,128,128]{3,2,1,0:T(8,128)S(1)} collective-permute-done((f32[2,1,128,128]{3,2,1,0:T(8,128)S(1)}, f32[2,1,128,128]{3,2,1,0:T(8,128)S(1)}, u32[]{:S(2)}, u32[]{:S(2)}) %collective-permute-start.13) | collective-permute-done | bytes 131104 | tf_op jit(solution)/shard_map/ppermute | solution.py:18
  69.8 7.4 %collective-permute-done.15 = f32[2,1,128,128]{3,2,1,0:T(8,128)S(1)} collective-permute-done((f32[2,1,128,128]{3,2,1,0:T(8,128)S(1)}, f32[2,1,128,128]{3,2,1,0:T(8,128)S(1)}, u32[]{:S(2)}, u32[]{:S(2)}) %collective-permute-start.15) | collective-permute-done | bytes 131104 | tf_op jit(solution)/shard_map/ppermute | solution.py:18
  78.3 2.7 collective-permute-start.16
  81.1 7.7 %collective-permute-done.16 = f32[4,128,128]{2,1,0:T(8,128)S(1)} collective-permute-done((f32[4,128,128]{2,1,0:T(8,128)S(1)}, f32[4,128,128]{2,1,0:T(8,128)S(1)}, u32[]{:S(2)}, u32[]{:S(2)}) %collective-permute-start.16) | collective-permute-done | bytes 262176 | tf_op jit(solution)/shard_map/ppermute | solution.py:30
  93.2 7.4 %collective-permute-done.18 = f32[2,1,128,128]{3,2,1,0:T(8,128)S(1)} collective-permute-done((f32[2,1,128,128]{3,2,1,0:T(8,128)S(1)}, f32[2,1,128,128]{3,2,1,0:T(8,128)S(1)}, u32[]{:S(2)}, u32[]{:S(2)}) %collective-permute-start.18) | collective-permute-done | bytes 131104 | tf_op jit(solution)/shard_map/ppermute | solution.py:18
  106.2 7.5 %collective-permute-done.20 = f32[2,1,128,128]{3,2,1,0:T(8,128)S(1)} collective-permute-done((f32[2,1,128,128]{3,2,1,0:T(8,128)S(1)}, f32[2,1,128,128]{3,2,1,0:T(8,128)S(1)}, u32[]{:S(2)}, u32[]{:S(2)}) %collective-permute-start.20) | collective-permute-done | bytes 131104 | tf_op jit(solution)/shard_map/ppermute | solution.py:18
  119.2 7.4 %collective-permute-done.22 = f32[2,1,128,128]{3,2,1,0:T(8,128)S(1)} collective-permute-done((f32[2,1,128,128]{3,2,1,0:T(8,128)S(1)}, f32[2,1,128,128]{3,2,1,0:T(8,128)S(1)}, u32[]{:S(2)}, u32[]{:S(2)}) %collective-permute-start.22) | collective-permute-done | bytes 131104 | tf_op jit(solution)/shard_map/ppermute | solution.py:18
  132.3 7.4 %collective-permute-done.24 = f32[2,1,128,128]{3,2,1,0:T(8,128)S(1)} collective-permute-done((f32[2,1,128,128]{3,2,1,0:T(8,128)S(1)}, f32[2,1,128,128]{3,2,1,0:T(8,128)S(1)}, u32[]{:S(2)}, u32[]{:S(2)}) %collective-permute-start.24) | collective-permute-done | bytes 131104 | tf_op jit(solution)/shard_map/ppermute | solution.py:18
  140.8 550.1 %while.12 = (s32[]{:T(128)}, f32[2,4,128,128]{3,2,1,0:T(8,128)S(1)}, f32[4,128,128]{2,1,0:T(8,128)S(1)}, f32[4,128,128]{2,1,0:T(8,128)S(1)}, f32[2,10,128,128]{3...) while((s32[]{:T(128)}, f32[2,4,128,128]{3,2,1,0:T(8,128)S(1)}, f32[4,128,128]{2,1,0:T(8,128)S(1)}, ...), condition=%wide.region_1.2_spmd, body=%wide.region_0.1_spmd.sunk | while | flops 7367378 | bytes 12870101 | solution.py:97
  142.8 8.4 %collective-permute-done = f32[4,128,128]{2,1,0:T(8,128)S(1)} collective-permute-done((f32[4,128,128]{2,1,0:T(8,128)S(1)}, f32[4,128,128]{2,1,0:T(8,128)S(1)}, u32[]{:S(2)}, u32[]{:S(2)}) %collective-permute-start) | collective-permute-done | bytes 262176 | tf_op jit(solution)/shard_map/while/body/eval_jaxpr/ppermute | solution.py:30
  155.6 6.7 collective-permute-done.2
  167.5 6.8 collective-permute-done.4
  177.1 8.4 %collective-permute-done = f32[4,128,128]{2,1,0:T(8,128)S(1)} collective-permute-done((f32[4,128,128]{2,1,0:T(8,128)S(1)}, f32[4,128,128]{2,1,0:T(8,128)S(1)}, u32[]{:S(2)}, u32[]{:S(2)}) %collective-permute-start) | collective-permute-done | bytes 262176 | tf_op jit(solution)/shard_map/while/body/eval_jaxpr/ppermute | solution.py:30
  190.0 6.7 collective-permute-done.2
  201.9 6.9 collective-permute-done.4
  211.5 8.4 %collective-permute-done = f32[4,128,128]{2,1,0:T(8,128)S(1)} collective-permute-done((f32[4,128,128]{2,1,0:T(8,128)S(1)}, f32[4,128,128]{2,1,0:T(8,128)S(1)}, u32[]{:S(2)}, u32[]{:S(2)}) %collective-permute-start) | collective-permute-done | bytes 262176 | tf_op jit(solution)/shard_map/while/body/eval_jaxpr/ppermute | solution.py:30
  224.4 6.7 collective-permute-done.2
  236.3 6.9 collective-permute-done.4
  245.9 8.4 %collective-permute-done = f32[4,128,128]{2,1,0:T(8,128)S(1)} collective-permute-done((f32[4,128,128]{2,1,0:T(8,128)S(1)}, f32[4,128,128]{2,1,0:T(8,128)S(1)}, u32[]{:S(2)}, u32[]{:S(2)}) %collective-permute-start) | collective-permute-done | bytes 262176 | tf_op jit(solution)/shard_map/while/body/eval_jaxpr/ppermute | solution.py:30
  258.8 6.7 collective-permute-done.2
  270.7 6.9 collective-permute-done.4
  280.3 8.4 %collective-permute-done = f32[4,128,128]{2,1,0:T(8,128)S(1)} collective-permute-done((f32[4,128,128]{2,1,0:T(8,128)S(1)}, f32[4,128,128]{2,1,0:T(8,128)S(1)}, u32[]{:S(2)}, u32[]{:S(2)}) %collective-permute-start) | collective-permute-done | bytes 262176 | tf_op jit(solution)/shard_map/while/body/eval_jaxpr/ppermute | solution.py:30
  293.2 6.7 collective-permute-done.2
  305.1 6.9 collective-permute-done.4
  314.7 8.4 %collective-permute-done = f32[4,128,128]{2,1,0:T(8,128)S(1)} collective-permute-done((f32[4,128,128]{2,1,0:T(8,128)S(1)}, f32[4,128,128]{2,1,0:T(8,128)S(1)}, u32[]{:S(2)}, u32[]{:S(2)}) %collective-permute-start) | collective-permute-done | bytes 262176 | tf_op jit(solution)/shard_map/while/body/eval_jaxpr/ppermute | solution.py:30
  327.6 6.7 collective-permute-done.2
  339.5 6.9 collective-permute-done.4
  349.1 8.4 %collective-permute-done = f32[4,128,128]{2,1,0:T(8,128)S(1)} collective-permute-done((f32[4,128,128]{2,1,0:T(8,128)S(1)}, f32[4,128,128]{2,1,0:T(8,128)S(1)}, u32[]{:S(2)}, u32[]{:S(2)}) %collective-permute-start) | collective-permute-done | bytes 262176 | tf_op jit(solution)/shard_map/while/body/eval_jaxpr/ppermute | solution.py:30
  362.0 6.7 collective-permute-done.2
  373.9 6.9 collective-permute-done.4
  383.5 8.4 %collective-permute-done = f32[4,128,128]{2,1,0:T(8,128)S(1)} collective-permute-done((f32[4,128,128]{2,1,0:T(8,128)S(1)}, f32[4,128,128]{2,1,0:T(8,128)S(1)}, u32[]{:S(2)}, u32[]{:S(2)}) %collective-permute-start) | collective-permute-done | bytes 262176 | tf_op jit(solution)/shard_map/while/body/eval_jaxpr/ppermute | solution.py:30
  396.4 6.7 collective-permute-done.2
  408.3 6.9 collective-permute-done.4
  417.9 8.4 %collective-permute-done = f32[4,128,128]{2,1,0:T(8,128)S(1)} collective-permute-done((f32[4,128,128]{2,1,0:T(8,128)S(1)}, f32[4,128,128]{2,1,0:T(8,128)S(1)}, u32[]{:S(2)}, u32[]{:S(2)}) %collective-permute-start) | collective-permute-done | bytes 262176 | tf_op jit(solution)/shard_map/while/body/eval_jaxpr/ppermute | solution.py:30
  430.8 6.7 collective-permute-done.2
  442.7 6.9 collective-permute-done.4
  452.3 8.4 %collective-permute-done = f32[4,128,128]{2,1,0:T(8,128)S(1)} collective-permute-done((f32[4,128,128]{2,1,0:T(8,128)S(1)}, f32[4,128,128]{2,1,0:T(8,128)S(1)}, u32[]{:S(2)}, u32[]{:S(2)}) %collective-permute-start) | collective-permute-done | bytes 262176 | tf_op jit(solution)/shard_map/while/body/eval_jaxpr/ppermute | solution.py:30
  465.2 6.7 collective-permute-done.2
  477.1 6.9 collective-permute-done.4
  486.7 8.4 %collective-permute-done = f32[4,128,128]{2,1,0:T(8,128)S(1)} collective-permute-done((f32[4,128,128]{2,1,0:T(8,128)S(1)}, f32[4,128,128]{2,1,0:T(8,128)S(1)}, u32[]{:S(2)}, u32[]{:S(2)}) %collective-permute-start) | collective-permute-done | bytes 262176 | tf_op jit(solution)/shard_map/while/body/eval_jaxpr/ppermute | solution.py:30
  499.6 6.7 collective-permute-done.2
  511.5 6.9 collective-permute-done.4
  521.1 8.4 %collective-permute-done = f32[4,128,128]{2,1,0:T(8,128)S(1)} collective-permute-done((f32[4,128,128]{2,1,0:T(8,128)S(1)}, f32[4,128,128]{2,1,0:T(8,128)S(1)}, u32[]{:S(2)}, u32[]{:S(2)}) %collective-permute-start) | collective-permute-done | bytes 262176 | tf_op jit(solution)/shard_map/while/body/eval_jaxpr/ppermute | solution.py:30
  534.0 6.7 collective-permute-done.2
  545.9 6.9 collective-permute-done.4
  555.5 8.4 %collective-permute-done = f32[4,128,128]{2,1,0:T(8,128)S(1)} collective-permute-done((f32[4,128,128]{2,1,0:T(8,128)S(1)}, f32[4,128,128]{2,1,0:T(8,128)S(1)}, u32[]{:S(2)}, u32[]{:S(2)}) %collective-permute-start) | collective-permute-done | bytes 262176 | tf_op jit(solution)/shard_map/while/body/eval_jaxpr/ppermute | solution.py:30
  568.4 6.7 collective-permute-done.2
  580.3 6.9 collective-permute-done.4
  589.9 8.4 %collective-permute-done = f32[4,128,128]{2,1,0:T(8,128)S(1)} collective-permute-done((f32[4,128,128]{2,1,0:T(8,128)S(1)}, f32[4,128,128]{2,1,0:T(8,128)S(1)}, u32[]{:S(2)}, u32[]{:S(2)}) %collective-permute-start) | collective-permute-done | bytes 262176 | tf_op jit(solution)/shard_map/while/body/eval_jaxpr/ppermute | solution.py:30
  602.8 6.7 collective-permute-done.2
  614.7 6.9 collective-permute-done.4
  624.3 8.4 %collective-permute-done = f32[4,128,128]{2,1,0:T(8,128)S(1)} collective-permute-done((f32[4,128,128]{2,1,0:T(8,128)S(1)}, f32[4,128,128]{2,1,0:T(8,128)S(1)}, u32[]{:S(2)}, u32[]{:S(2)}) %collective-permute-start) | collective-permute-done | bytes 262176 | tf_op jit(solution)/shard_map/while/body/eval_jaxpr/ppermute | solution.py:30
  637.2 6.7 collective-permute-done.2
  649.1 6.8 collective-permute-done.4
  658.6 8.4 %collective-permute-done = f32[4,128,128]{2,1,0:T(8,128)S(1)} collective-permute-done((f32[4,128,128]{2,1,0:T(8,128)S(1)}, f32[4,128,128]{2,1,0:T(8,128)S(1)}, u32[]{:S(2)}, u32[]{:S(2)}) %collective-permute-start) | collective-permute-done | bytes 262176 | tf_op jit(solution)/shard_map/while/body/eval_jaxpr/ppermute | solution.py:30
  671.5 6.7 collective-permute-done.2
  683.4 6.8 collective-permute-done.4
  (323 shorter events, 242.8 us)
Async XLA Ops:
  1.1 12.0 %collective-permute-start.5 = (f32[4,128,128]{2,1,0:T(8,128)S(1)}, f32[4,128,128]{2,1,0:T(8,128)S(1)}, u32[]{:S(2)}, u32[]{:S(2)}) collective-permute-start(f32[4,128,128]{2,1,0:T(8,128)S(1)} %get-tuple-element.117), channel_id=1, source_target_pairs={{0,16},{16,32},{32,48},{48,64},{64,80},{80,96},{96,112},{112,128},... | collective-permute-start | bytes 786440 | tf_op jit(solution)/shard_map/ppermute | solution.py:30
  13.2 14.2 %collective-permute-start.7 = (f32[2,1,128,128]{3,2,1,0:T(8,128)S(1)}, f32[2,1,128,128]{3,2,1,0:T(8,128)S(1)}, u32[]{:S(2)}, u32[]{:S(2)}) collective-permute-start(f32[2,1,128,128]{3,2,1,0:T(8,128)S(1)} %get-tuple-element.115), channel_id=1, source_target_pairs={{1,0},{2,1},{3,2},{4,3},{5,4},{6,5},{7,6},{8,7},{9,8},{10,9},{11,1... | collective-permute-start | bytes 393224 | tf_op jit(solution)/shard_map/ppermute | solution.py:20
  16.3 11.2 %collective-permute-start.9 = (f32[2,1,128,128]{3,2,1,0:T(8,128)S(1)}, f32[2,1,128,128]{3,2,1,0:T(8,128)S(1)}, u32[]{:S(2)}, u32[]{:S(2)}) collective-permute-start(f32[2,1,128,128]{3,2,1,0:T(8,128)S(1)} %get-tuple-element.114), channel_id=1, source_target_pairs={{0,1},{1,2},{2,3},{3,4},{4,5},{5,6},{6,7},{7,8},{8,9},{9,10},{10,1... | collective-permute-start | bytes 393224 | tf_op jit(solution)/shard_map/ppermute | solution.py:18
  18.3 12.5 %collective-permute-start.6 = (f32[2,3,128,128]{3,2,1,0:T(8,128)S(1)}, f32[2,3,128,128]{3,2,1,0:T(8,128)S(1)}, u32[]{:S(2)}, u32[]{:S(2)}) collective-permute-start(f32[2,3,128,128]{3,2,1,0:T(8,128)S(1)} %get-tuple-element.113), channel_id=1, source_target_pairs={{1,0},{2,1},{3,2},{4,3},{5,4},{6,5},{7,6},{8,7},{9,8},{10,9},{11,1... | collective-permute-start | bytes 1179656 | tf_op jit(solution)/shard_map/ppermute | solution.py:20
  25.5 12.7 %collective-permute-start.8 = (f32[2,3,128,128]{3,2,1,0:T(8,128)S(1)}, f32[2,3,128,128]{3,2,1,0:T(8,128)S(1)}, u32[]{:S(2)}, u32[]{:S(2)}) collective-permute-start(f32[2,3,128,128]{3,2,1,0:T(8,128)S(1)} %get-tuple-element.112), channel_id=1, source_target_pairs={{0,1},{1,2},{2,3},{3,4},{4,5},{5,6},{6,7},{7,8},{8,9},{9,10},{10,1... | collective-permute-start | bytes 1179656 | tf_op jit(solution)/shard_map/ppermute | solution.py:18
  39.3 4.4 collective-permute-start.10
  41.3 9.9 %collective-permute-start.11 = (f32[2,1,128,128]{3,2,1,0:T(8,128)S(1)}, f32[2,1,128,128]{3,2,1,0:T(8,128)S(1)}, u32[]{:S(2)}, u32[]{:S(2)}) collective-permute-start(f32[2,1,128,128]{3,2,1,0:T(8,128)S(1)} %get-tuple-element.110), channel_id=1, source_target_pairs={{0,1},{1,2},{2,3},{3,4},{4,5},{5,6},{6,7},{7,8},{8,9},{9,10},{10,1... | collective-permute-start | bytes 393224 | tf_op jit(solution)/shard_map/ppermute | solution.py:18
  52.3 4.4 collective-permute-start.12
  54.2 10.0 %collective-permute-start.13 = (f32[2,1,128,128]{3,2,1,0:T(8,128)S(1)}, f32[2,1,128,128]{3,2,1,0:T(8,128)S(1)}, u32[]{:S(2)}, u32[]{:S(2)}) collective-permute-start(f32[2,1,128,128]{3,2,1,0:T(8,128)S(1)} %get-tuple-element.108), channel_id=1, source_target_pairs={{0,1},{1,2},{2,3},{3,4},{4,5},{5,6},{6,7},{7,8},{8,9},{9,10},{10,1... | collective-permute-start | bytes 393224 | tf_op jit(solution)/shard_map/ppermute | solution.py:18
  67.3 9.9 %collective-permute-start.15 = (f32[2,1,128,128]{3,2,1,0:T(8,128)S(1)}, f32[2,1,128,128]{3,2,1,0:T(8,128)S(1)}, u32[]{:S(2)}, u32[]{:S(2)}) collective-permute-start(f32[2,1,128,128]{3,2,1,0:T(8,128)S(1)} %get-tuple-element.106), channel_id=1, source_target_pairs={{0,1},{1,2},{2,3},{3,4},{4,5},{5,6},{6,7},{7,8},{8,9},{9,10},{10,1... | collective-permute-start | bytes 393224 | tf_op jit(solution)/shard_map/ppermute | solution.py:18
  78.3 10.4 %collective-permute-start.16 = (f32[4,128,128]{2,1,0:T(8,128)S(1)}, f32[4,128,128]{2,1,0:T(8,128)S(1)}, u32[]{:S(2)}, u32[]{:S(2)}) collective-permute-start(f32[4,128,128]{2,1,0:T(8,128)S(1)} %get-tuple-element.105), channel_id=1, source_target_pairs={{0,16},{16,32},{32,48},{48,64},{64,80},{80,96},{96,112},{112,128},... | collective-permute-start | bytes 786440 | tf_op jit(solution)/shard_map/ppermute | solution.py:30
  90.7 9.9 %collective-permute-start.18 = (f32[2,1,128,128]{3,2,1,0:T(8,128)S(1)}, f32[2,1,128,128]{3,2,1,0:T(8,128)S(1)}, u32[]{:S(2)}, u32[]{:S(2)}) collective-permute-start(f32[2,1,128,128]{3,2,1,0:T(8,128)S(1)} %get-tuple-element.102), channel_id=1, source_target_pairs={{0,1},{1,2},{2,3},{3,4},{4,5},{5,6},{6,7},{7,8},{8,9},{9,10},{10,1... | collective-permute-start | bytes 393224 | tf_op jit(solution)/shard_map/ppermute | solution.py:18
  103.7 10.0 %collective-permute-start.20 = (f32[2,1,128,128]{3,2,1,0:T(8,128)S(1)}, f32[2,1,128,128]{3,2,1,0:T(8,128)S(1)}, u32[]{:S(2)}, u32[]{:S(2)}) collective-permute-start(f32[2,1,128,128]{3,2,1,0:T(8,128)S(1)} %get-tuple-element.100), channel_id=1, source_target_pairs={{0,1},{1,2},{2,3},{3,4},{4,5},{5,6},{6,7},{7,8},{8,9},{9,10},{10,1... | collective-permute-start | bytes 393224 | tf_op jit(solution)/shard_map/ppermute | solution.py:18
  116.7 9.9 %collective-permute-start.22 = (f32[2,1,128,128]{3,2,1,0:T(8,128)S(1)}, f32[2,1,128,128]{3,2,1,0:T(8,128)S(1)}, u32[]{:S(2)}, u32[]{:S(2)}) collective-permute-start(f32[2,1,128,128]{3,2,1,0:T(8,128)S(1)} %get-tuple-element.98), channel_id=1, source_target_pairs={{0,1},{1,2},{2,3},{3,4},{4,5},{5,6},{6,7},{7,8},{8,9},{9,10},{10,1... | collective-permute-start | bytes 393224 | tf_op jit(solution)/shard_map/ppermute | solution.py:18
  127.8 4.5 collective-permute-start.23
  129.7 10.0 %collective-permute-start.24 = (f32[2,1,128,128]{3,2,1,0:T(8,128)S(1)}, f32[2,1,128,128]{3,2,1,0:T(8,128)S(1)}, u32[]{:S(2)}, u32[]{:S(2)}) collective-permute-start(f32[2,1,128,128]{3,2,1,0:T(8,128)S(1)} %get-tuple-element.96), channel_id=1, source_target_pairs={{0,1},{1,2},{2,3},{3,4},{4,5},{5,6},{6,7},{7,8},{8,9},{9,10},{10,1... | collective-permute-start | bytes 393224 | tf_op jit(solution)/shard_map/ppermute | solution.py:18
  140.9 10.4 %collective-permute-start = (f32[4,128,128]{2,1,0:T(8,128)S(1)}, f32[4,128,128]{2,1,0:T(8,128)S(1)}, u32[]{:S(2)}, u32[]{:S(2)}) collective-permute-start(f32[4,128,128]{2,1,0:T(8,128)S(1)} %slice_bitcast_fusion.7), channel_id=1, source_target_pairs={{0,16},{16,32},{32,48},{48,64},{64,80},{80,96},{96,112},{112,128},... | collective-permute-start | bytes 786440 | tf_op jit(solution)/shard_map/while/body/eval_jaxpr/ppermute | solution.py:30
  153.2 9.2 %collective-permute-start.2 = (f32[1,128,128]{2,1,0:T(8,128)S(1)}, f32[1,128,128]{2,1,0:T(8,128)S(1)}, u32[]{:S(2)}, u32[]{:S(2)}) collective-permute-start(f32[1,128,128]{2,1,0:T(8,128)S(1)} %get-tuple-element.164), channel_id=1, source_target_pairs={{0,1},{1,2},{2,3},{3,4},{4,5},{5,6},{6,7},{7,8},{8,9},{9,10},{10,1... | collective-permute-start | bytes 196616 | tf_op jit(solution)/shard_map/while/body/eval_jaxpr/ppermute | solution.py:18
  165.1 9.2 %collective-permute-start.4 = (f32[1,128,128]{2,1,0:T(8,128)S(1)}, f32[1,128,128]{2,1,0:T(8,128)S(1)}, u32[]{:S(2)}, u32[]{:S(2)}) collective-permute-start(f32[1,128,128]{2,1,0:T(8,128)S(1)} %get-tuple-element.166), channel_id=1, source_target_pairs={{0,1},{1,2},{2,3},{3,4},{4,5},{5,6},{6,7},{7,8},{8,9},{9,10},{10,1... | collective-permute-start | bytes 196616 | tf_op jit(solution)/shard_map/while/body/eval_jaxpr/ppermute | solution.py:18
  175.2 10.4 %collective-permute-start = (f32[4,128,128]{2,1,0:T(8,128)S(1)}, f32[4,128,128]{2,1,0:T(8,128)S(1)}, u32[]{:S(2)}, u32[]{:S(2)}) collective-permute-start(f32[4,128,128]{2,1,0:T(8,128)S(1)} %slice_bitcast_fusion.7), channel_id=1, source_target_pairs={{0,16},{16,32},{32,48},{48,64},{64,80},{80,96},{96,112},{112,128},... | collective-permute-start | bytes 786440 | tf_op jit(solution)/shard_map/while/body/eval_jaxpr/ppermute | solution.py:30
  187.5 9.2 %collective-permute-start.2 = (f32[1,128,128]{2,1,0:T(8,128)S(1)}, f32[1,128,128]{2,1,0:T(8,128)S(1)}, u32[]{:S(2)}, u32[]{:S(2)}) collective-permute-start(f32[1,128,128]{2,1,0:T(8,128)S(1)} %get-tuple-element.164), channel_id=1, source_target_pairs={{0,1},{1,2},{2,3},{3,4},{4,5},{5,6},{6,7},{7,8},{8,9},{9,10},{10,1... | collective-permute-start | bytes 196616 | tf_op jit(solution)/shard_map/while/body/eval_jaxpr/ppermute | solution.py:18
  199.4 9.3 %collective-permute-start.4 = (f32[1,128,128]{2,1,0:T(8,128)S(1)}, f32[1,128,128]{2,1,0:T(8,128)S(1)}, u32[]{:S(2)}, u32[]{:S(2)}) collective-permute-start(f32[1,128,128]{2,1,0:T(8,128)S(1)} %get-tuple-element.166), channel_id=1, source_target_pairs={{0,1},{1,2},{2,3},{3,4},{4,5},{5,6},{6,7},{7,8},{8,9},{9,10},{10,1... | collective-permute-start | bytes 196616 | tf_op jit(solution)/shard_map/while/body/eval_jaxpr/ppermute | solution.py:18
  209.6 10.4 %collective-permute-start = (f32[4,128,128]{2,1,0:T(8,128)S(1)}, f32[4,128,128]{2,1,0:T(8,128)S(1)}, u32[]{:S(2)}, u32[]{:S(2)}) collective-permute-start(f32[4,128,128]{2,1,0:T(8,128)S(1)} %slice_bitcast_fusion.7), channel_id=1, source_target_pairs={{0,16},{16,32},{32,48},{48,64},{64,80},{80,96},{96,112},{112,128},... | collective-permute-start | bytes 786440 | tf_op jit(solution)/shard_map/while/body/eval_jaxpr/ppermute | solution.py:30
  221.9 9.2 %collective-permute-start.2 = (f32[1,128,128]{2,1,0:T(8,128)S(1)}, f32[1,128,128]{2,1,0:T(8,128)S(1)}, u32[]{:S(2)}, u32[]{:S(2)}) collective-permute-start(f32[1,128,128]{2,1,0:T(8,128)S(1)} %get-tuple-element.164), channel_id=1, source_target_pairs={{0,1},{1,2},{2,3},{3,4},{4,5},{5,6},{6,7},{7,8},{8,9},{9,10},{10,1... | collective-permute-start | bytes 196616 | tf_op jit(solution)/shard_map/while/body/eval_jaxpr/ppermute | solution.py:18
  233.8 9.3 %collective-permute-start.4 = (f32[1,128,128]{2,1,0:T(8,128)S(1)}, f32[1,128,128]{2,1,0:T(8,128)S(1)}, u32[]{:S(2)}, u32[]{:S(2)}) collective-permute-start(f32[1,128,128]{2,1,0:T(8,128)S(1)} %get-tuple-element.166), channel_id=1, source_target_pairs={{0,1},{1,2},{2,3},{3,4},{4,5},{5,6},{6,7},{7,8},{8,9},{9,10},{10,1... | collective-permute-start | bytes 196616 | tf_op jit(solution)/shard_map/while/body/eval_jaxpr/ppermute | solution.py:18
  244.0 10.4 %collective-permute-start = (f32[4,128,128]{2,1,0:T(8,128)S(1)}, f32[4,128,128]{2,1,0:T(8,128)S(1)}, u32[]{:S(2)}, u32[]{:S(2)}) collective-permute-start(f32[4,128,128]{2,1,0:T(8,128)S(1)} %slice_bitcast_fusion.7), channel_id=1, source_target_pairs={{0,16},{16,32},{32,48},{48,64},{64,80},{80,96},{96,112},{112,128},... | collective-permute-start | bytes 786440 | tf_op jit(solution)/shard_map/while/body/eval_jaxpr/ppermute | solution.py:30
  256.3 9.2 %collective-permute-start.2 = (f32[1,128,128]{2,1,0:T(8,128)S(1)}, f32[1,128,128]{2,1,0:T(8,128)S(1)}, u32[]{:S(2)}, u32[]{:S(2)}) collective-permute-start(f32[1,128,128]{2,1,0:T(8,128)S(1)} %get-tuple-element.164), channel_id=1, source_target_pairs={{0,1},{1,2},{2,3},{3,4},{4,5},{5,6},{6,7},{7,8},{8,9},{9,10},{10,1... | collective-permute-start | bytes 196616 | tf_op jit(solution)/shard_map/while/body/eval_jaxpr/ppermute | solution.py:18
  268.2 9.3 %collective-permute-start.4 = (f32[1,128,128]{2,1,0:T(8,128)S(1)}, f32[1,128,128]{2,1,0:T(8,128)S(1)}, u32[]{:S(2)}, u32[]{:S(2)}) collective-permute-start(f32[1,128,128]{2,1,0:T(8,128)S(1)} %get-tuple-element.166), channel_id=1, source_target_pairs={{0,1},{1,2},{2,3},{3,4},{4,5},{5,6},{6,7},{7,8},{8,9},{9,10},{10,1... | collective-permute-start | bytes 196616 | tf_op jit(solution)/shard_map/while/body/eval_jaxpr/ppermute | solution.py:18
  278.4 10.4 %collective-permute-start = (f32[4,128,128]{2,1,0:T(8,128)S(1)}, f32[4,128,128]{2,1,0:T(8,128)S(1)}, u32[]{:S(2)}, u32[]{:S(2)}) collective-permute-start(f32[4,128,128]{2,1,0:T(8,128)S(1)} %slice_bitcast_fusion.7), channel_id=1, source_target_pairs={{0,16},{16,32},{32,48},{48,64},{64,80},{80,96},{96,112},{112,128},... | collective-permute-start | bytes 786440 | tf_op jit(solution)/shard_map/while/body/eval_jaxpr/ppermute | solution.py:30
  290.7 9.2 %collective-permute-start.2 = (f32[1,128,128]{2,1,0:T(8,128)S(1)}, f32[1,128,128]{2,1,0:T(8,128)S(1)}, u32[]{:S(2)}, u32[]{:S(2)}) collective-permute-start(f32[1,128,128]{2,1,0:T(8,128)S(1)} %get-tuple-element.164), channel_id=1, source_target_pairs={{0,1},{1,2},{2,3},{3,4},{4,5},{5,6},{6,7},{7,8},{8,9},{9,10},{10,1... | collective-permute-start | bytes 196616 | tf_op jit(solution)/shard_map/while/body/eval_jaxpr/ppermute | solution.py:18
  302.6 9.3 %collective-permute-start.4 = (f32[1,128,128]{2,1,0:T(8,128)S(1)}, f32[1,128,128]{2,1,0:T(8,128)S(1)}, u32[]{:S(2)}, u32[]{:S(2)}) collective-permute-start(f32[1,128,128]{2,1,0:T(8,128)S(1)} %get-tuple-element.166), channel_id=1, source_target_pairs={{0,1},{1,2},{2,3},{3,4},{4,5},{5,6},{6,7},{7,8},{8,9},{9,10},{10,1... | collective-permute-start | bytes 196616 | tf_op jit(solution)/shard_map/while/body/eval_jaxpr/ppermute | solution.py:18
  312.8 10.4 %collective-permute-start = (f32[4,128,128]{2,1,0:T(8,128)S(1)}, f32[4,128,128]{2,1,0:T(8,128)S(1)}, u32[]{:S(2)}, u32[]{:S(2)}) collective-permute-start(f32[4,128,128]{2,1,0:T(8,128)S(1)} %slice_bitcast_fusion.7), channel_id=1, source_target_pairs={{0,16},{16,32},{32,48},{48,64},{64,80},{80,96},{96,112},{112,128},... | collective-permute-start | bytes 786440 | tf_op jit(solution)/shard_map/while/body/eval_jaxpr/ppermute | solution.py:30
  325.1 9.2 %collective-permute-start.2 = (f32[1,128,128]{2,1,0:T(8,128)S(1)}, f32[1,128,128]{2,1,0:T(8,128)S(1)}, u32[]{:S(2)}, u32[]{:S(2)}) collective-permute-start(f32[1,128,128]{2,1,0:T(8,128)S(1)} %get-tuple-element.164), channel_id=1, source_target_pairs={{0,1},{1,2},{2,3},{3,4},{4,5},{5,6},{6,7},{7,8},{8,9},{9,10},{10,1... | collective-permute-start | bytes 196616 | tf_op jit(solution)/shard_map/while/body/eval_jaxpr/ppermute | solution.py:18
  337.0 9.3 %collective-permute-start.4 = (f32[1,128,128]{2,1,0:T(8,128)S(1)}, f32[1,128,128]{2,1,0:T(8,128)S(1)}, u32[]{:S(2)}, u32[]{:S(2)}) collective-permute-start(f32[1,128,128]{2,1,0:T(8,128)S(1)} %get-tuple-element.166), channel_id=1, source_target_pairs={{0,1},{1,2},{2,3},{3,4},{4,5},{5,6},{6,7},{7,8},{8,9},{9,10},{10,1... | collective-permute-start | bytes 196616 | tf_op jit(solution)/shard_map/while/body/eval_jaxpr/ppermute | solution.py:18
  347.2 10.4 %collective-permute-start = (f32[4,128,128]{2,1,0:T(8,128)S(1)}, f32[4,128,128]{2,1,0:T(8,128)S(1)}, u32[]{:S(2)}, u32[]{:S(2)}) collective-permute-start(f32[4,128,128]{2,1,0:T(8,128)S(1)} %slice_bitcast_fusion.7), channel_id=1, source_target_pairs={{0,16},{16,32},{32,48},{48,64},{64,80},{80,96},{96,112},{112,128},... | collective-permute-start | bytes 786440 | tf_op jit(solution)/shard_map/while/body/eval_jaxpr/ppermute | solution.py:30
  359.5 9.2 %collective-permute-start.2 = (f32[1,128,128]{2,1,0:T(8,128)S(1)}, f32[1,128,128]{2,1,0:T(8,128)S(1)}, u32[]{:S(2)}, u32[]{:S(2)}) collective-permute-start(f32[1,128,128]{2,1,0:T(8,128)S(1)} %get-tuple-element.164), channel_id=1, source_target_pairs={{0,1},{1,2},{2,3},{3,4},{4,5},{5,6},{6,7},{7,8},{8,9},{9,10},{10,1... | collective-permute-start | bytes 196616 | tf_op jit(solution)/shard_map/while/body/eval_jaxpr/ppermute | solution.py:18
  371.4 9.3 %collective-permute-start.4 = (f32[1,128,128]{2,1,0:T(8,128)S(1)}, f32[1,128,128]{2,1,0:T(8,128)S(1)}, u32[]{:S(2)}, u32[]{:S(2)}) collective-permute-start(f32[1,128,128]{2,1,0:T(8,128)S(1)} %get-tuple-element.166), channel_id=1, source_target_pairs={{0,1},{1,2},{2,3},{3,4},{4,5},{5,6},{6,7},{7,8},{8,9},{9,10},{10,1... | collective-permute-start | bytes 196616 | tf_op jit(solution)/shard_map/while/body/eval_jaxpr/ppermute | solution.py:18
  381.6 10.4 %collective-permute-start = (f32[4,128,128]{2,1,0:T(8,128)S(1)}, f32[4,128,128]{2,1,0:T(8,128)S(1)}, u32[]{:S(2)}, u32[]{:S(2)}) collective-permute-start(f32[4,128,128]{2,1,0:T(8,128)S(1)} %slice_bitcast_fusion.7), channel_id=1, source_target_pairs={{0,16},{16,32},{32,48},{48,64},{64,80},{80,96},{96,112},{112,128},... | collective-permute-start | bytes 786440 | tf_op jit(solution)/shard_map/while/body/eval_jaxpr/ppermute | solution.py:30
  393.9 9.2 %collective-permute-start.2 = (f32[1,128,128]{2,1,0:T(8,128)S(1)}, f32[1,128,128]{2,1,0:T(8,128)S(1)}, u32[]{:S(2)}, u32[]{:S(2)}) collective-permute-start(f32[1,128,128]{2,1,0:T(8,128)S(1)} %get-tuple-element.164), channel_id=1, source_target_pairs={{0,1},{1,2},{2,3},{3,4},{4,5},{5,6},{6,7},{7,8},{8,9},{9,10},{10,1... | collective-permute-start | bytes 196616 | tf_op jit(solution)/shard_map/while/body/eval_jaxpr/ppermute | solution.py:18
  405.8 9.3 %collective-permute-start.4 = (f32[1,128,128]{2,1,0:T(8,128)S(1)}, f32[1,128,128]{2,1,0:T(8,128)S(1)}, u32[]{:S(2)}, u32[]{:S(2)}) collective-permute-start(f32[1,128,128]{2,1,0:T(8,128)S(1)} %get-tuple-element.166), channel_id=1, source_target_pairs={{0,1},{1,2},{2,3},{3,4},{4,5},{5,6},{6,7},{7,8},{8,9},{9,10},{10,1... | collective-permute-start | bytes 196616 | tf_op jit(solution)/shard_map/while/body/eval_jaxpr/ppermute | solution.py:18
  416.0 10.4 %collective-permute-start = (f32[4,128,128]{2,1,0:T(8,128)S(1)}, f32[4,128,128]{2,1,0:T(8,128)S(1)}, u32[]{:S(2)}, u32[]{:S(2)}) collective-permute-start(f32[4,128,128]{2,1,0:T(8,128)S(1)} %slice_bitcast_fusion.7), channel_id=1, source_target_pairs={{0,16},{16,32},{32,48},{48,64},{64,80},{80,96},{96,112},{112,128},... | collective-permute-start | bytes 786440 | tf_op jit(solution)/shard_map/while/body/eval_jaxpr/ppermute | solution.py:30
  428.3 9.2 %collective-permute-start.2 = (f32[1,128,128]{2,1,0:T(8,128)S(1)}, f32[1,128,128]{2,1,0:T(8,128)S(1)}, u32[]{:S(2)}, u32[]{:S(2)}) collective-permute-start(f32[1,128,128]{2,1,0:T(8,128)S(1)} %get-tuple-element.164), channel_id=1, source_target_pairs={{0,1},{1,2},{2,3},{3,4},{4,5},{5,6},{6,7},{7,8},{8,9},{9,10},{10,1... | collective-permute-start | bytes 196616 | tf_op jit(solution)/shard_map/while/body/eval_jaxpr/ppermute | solution.py:18
  440.2 9.3 %collective-permute-start.4 = (f32[1,128,128]{2,1,0:T(8,128)S(1)}, f32[1,128,128]{2,1,0:T(8,128)S(1)}, u32[]{:S(2)}, u32[]{:S(2)}) collective-permute-start(f32[1,128,128]{2,1,0:T(8,128)S(1)} %get-tuple-element.166), channel_id=1, source_target_pairs={{0,1},{1,2},{2,3},{3,4},{4,5},{5,6},{6,7},{7,8},{8,9},{9,10},{10,1... | collective-permute-start | bytes 196616 | tf_op jit(solution)/shard_map/while/body/eval_jaxpr/ppermute | solution.py:18
  450.4 10.4 %collective-permute-start = (f32[4,128,128]{2,1,0:T(8,128)S(1)}, f32[4,128,128]{2,1,0:T(8,128)S(1)}, u32[]{:S(2)}, u32[]{:S(2)}) collective-permute-start(f32[4,128,128]{2,1,0:T(8,128)S(1)} %slice_bitcast_fusion.7), channel_id=1, source_target_pairs={{0,16},{16,32},{32,48},{48,64},{64,80},{80,96},{96,112},{112,128},... | collective-permute-start | bytes 786440 | tf_op jit(solution)/shard_map/while/body/eval_jaxpr/ppermute | solution.py:30
  462.7 9.2 %collective-permute-start.2 = (f32[1,128,128]{2,1,0:T(8,128)S(1)}, f32[1,128,128]{2,1,0:T(8,128)S(1)}, u32[]{:S(2)}, u32[]{:S(2)}) collective-permute-start(f32[1,128,128]{2,1,0:T(8,128)S(1)} %get-tuple-element.164), channel_id=1, source_target_pairs={{0,1},{1,2},{2,3},{3,4},{4,5},{5,6},{6,7},{7,8},{8,9},{9,10},{10,1... | collective-permute-start | bytes 196616 | tf_op jit(solution)/shard_map/while/body/eval_jaxpr/ppermute | solution.py:18
  474.6 9.3 %collective-permute-start.4 = (f32[1,128,128]{2,1,0:T(8,128)S(1)}, f32[1,128,128]{2,1,0:T(8,128)S(1)}, u32[]{:S(2)}, u32[]{:S(2)}) collective-permute-start(f32[1,128,128]{2,1,0:T(8,128)S(1)} %get-tuple-element.166), channel_id=1, source_target_pairs={{0,1},{1,2},{2,3},{3,4},{4,5},{5,6},{6,7},{7,8},{8,9},{9,10},{10,1... | collective-permute-start | bytes 196616 | tf_op jit(solution)/shard_map/while/body/eval_jaxpr/ppermute | solution.py:18
  484.8 10.4 %collective-permute-start = (f32[4,128,128]{2,1,0:T(8,128)S(1)}, f32[4,128,128]{2,1,0:T(8,128)S(1)}, u32[]{:S(2)}, u32[]{:S(2)}) collective-permute-start(f32[4,128,128]{2,1,0:T(8,128)S(1)} %slice_bitcast_fusion.7), channel_id=1, source_target_pairs={{0,16},{16,32},{32,48},{48,64},{64,80},{80,96},{96,112},{112,128},... | collective-permute-start | bytes 786440 | tf_op jit(solution)/shard_map/while/body/eval_jaxpr/ppermute | solution.py:30
  497.1 9.2 %collective-permute-start.2 = (f32[1,128,128]{2,1,0:T(8,128)S(1)}, f32[1,128,128]{2,1,0:T(8,128)S(1)}, u32[]{:S(2)}, u32[]{:S(2)}) collective-permute-start(f32[1,128,128]{2,1,0:T(8,128)S(1)} %get-tuple-element.164), channel_id=1, source_target_pairs={{0,1},{1,2},{2,3},{3,4},{4,5},{5,6},{6,7},{7,8},{8,9},{9,10},{10,1... | collective-permute-start | bytes 196616 | tf_op jit(solution)/shard_map/while/body/eval_jaxpr/ppermute | solution.py:18
  509.0 9.3 %collective-permute-start.4 = (f32[1,128,128]{2,1,0:T(8,128)S(1)}, f32[1,128,128]{2,1,0:T(8,128)S(1)}, u32[]{:S(2)}, u32[]{:S(2)}) collective-permute-start(f32[1,128,128]{2,1,0:T(8,128)S(1)} %get-tuple-element.166), channel_id=1, source_target_pairs={{0,1},{1,2},{2,3},{3,4},{4,5},{5,6},{6,7},{7,8},{8,9},{9,10},{10,1... | collective-permute-start | bytes 196616 | tf_op jit(solution)/shard_map/while/body/eval_jaxpr/ppermute | solution.py:18
  519.2 10.4 %collective-permute-start = (f32[4,128,128]{2,1,0:T(8,128)S(1)}, f32[4,128,128]{2,1,0:T(8,128)S(1)}, u32[]{:S(2)}, u32[]{:S(2)}) collective-permute-start(f32[4,128,128]{2,1,0:T(8,128)S(1)} %slice_bitcast_fusion.7), channel_id=1, source_target_pairs={{0,16},{16,32},{32,48},{48,64},{64,80},{80,96},{96,112},{112,128},... | collective-permute-start | bytes 786440 | tf_op jit(solution)/shard_map/while/body/eval_jaxpr/ppermute | solution.py:30
  531.5 9.2 %collective-permute-start.2 = (f32[1,128,128]{2,1,0:T(8,128)S(1)}, f32[1,128,128]{2,1,0:T(8,128)S(1)}, u32[]{:S(2)}, u32[]{:S(2)}) collective-permute-start(f32[1,128,128]{2,1,0:T(8,128)S(1)} %get-tuple-element.164), channel_id=1, source_target_pairs={{0,1},{1,2},{2,3},{3,4},{4,5},{5,6},{6,7},{7,8},{8,9},{9,10},{10,1... | collective-permute-start | bytes 196616 | tf_op jit(solution)/shard_map/while/body/eval_jaxpr/ppermute | solution.py:18
  543.4 9.3 %collective-permute-start.4 = (f32[1,128,128]{2,1,0:T(8,128)S(1)}, f32[1,128,128]{2,1,0:T(8,128)S(1)}, u32[]{:S(2)}, u32[]{:S(2)}) collective-permute-start(f32[1,128,128]{2,1,0:T(8,128)S(1)} %get-tuple-element.166), channel_id=1, source_target_pairs={{0,1},{1,2},{2,3},{3,4},{4,5},{5,6},{6,7},{7,8},{8,9},{9,10},{10,1... | collective-permute-start | bytes 196616 | tf_op jit(solution)/shard_map/while/body/eval_jaxpr/ppermute | solution.py:18
  553.6 10.4 %collective-permute-start = (f32[4,128,128]{2,1,0:T(8,128)S(1)}, f32[4,128,128]{2,1,0:T(8,128)S(1)}, u32[]{:S(2)}, u32[]{:S(2)}) collective-permute-start(f32[4,128,128]{2,1,0:T(8,128)S(1)} %slice_bitcast_fusion.7), channel_id=1, source_target_pairs={{0,16},{16,32},{32,48},{48,64},{64,80},{80,96},{96,112},{112,128},... | collective-permute-start | bytes 786440 | tf_op jit(solution)/shard_map/while/body/eval_jaxpr/ppermute | solution.py:30
  565.9 9.2 %collective-permute-start.2 = (f32[1,128,128]{2,1,0:T(8,128)S(1)}, f32[1,128,128]{2,1,0:T(8,128)S(1)}, u32[]{:S(2)}, u32[]{:S(2)}) collective-permute-start(f32[1,128,128]{2,1,0:T(8,128)S(1)} %get-tuple-element.164), channel_id=1, source_target_pairs={{0,1},{1,2},{2,3},{3,4},{4,5},{5,6},{6,7},{7,8},{8,9},{9,10},{10,1... | collective-permute-start | bytes 196616 | tf_op jit(solution)/shard_map/while/body/eval_jaxpr/ppermute | solution.py:18
  577.8 9.3 %collective-permute-start.4 = (f32[1,128,128]{2,1,0:T(8,128)S(1)}, f32[1,128,128]{2,1,0:T(8,128)S(1)}, u32[]{:S(2)}, u32[]{:S(2)}) collective-permute-start(f32[1,128,128]{2,1,0:T(8,128)S(1)} %get-tuple-element.166), channel_id=1, source_target_pairs={{0,1},{1,2},{2,3},{3,4},{4,5},{5,6},{6,7},{7,8},{8,9},{9,10},{10,1... | collective-permute-start | bytes 196616 | tf_op jit(solution)/shard_map/while/body/eval_jaxpr/ppermute | solution.py:18
  588.0 10.4 %collective-permute-start = (f32[4,128,128]{2,1,0:T(8,128)S(1)}, f32[4,128,128]{2,1,0:T(8,128)S(1)}, u32[]{:S(2)}, u32[]{:S(2)}) collective-permute-start(f32[4,128,128]{2,1,0:T(8,128)S(1)} %slice_bitcast_fusion.7), channel_id=1, source_target_pairs={{0,16},{16,32},{32,48},{48,64},{64,80},{80,96},{96,112},{112,128},... | collective-permute-start | bytes 786440 | tf_op jit(solution)/shard_map/while/body/eval_jaxpr/ppermute | solution.py:30
  600.3 9.2 %collective-permute-start.2 = (f32[1,128,128]{2,1,0:T(8,128)S(1)}, f32[1,128,128]{2,1,0:T(8,128)S(1)}, u32[]{:S(2)}, u32[]{:S(2)}) collective-permute-start(f32[1,128,128]{2,1,0:T(8,128)S(1)} %get-tuple-element.164), channel_id=1, source_target_pairs={{0,1},{1,2},{2,3},{3,4},{4,5},{5,6},{6,7},{7,8},{8,9},{9,10},{10,1... | collective-permute-start | bytes 196616 | tf_op jit(solution)/shard_map/while/body/eval_jaxpr/ppermute | solution.py:18
  612.2 9.3 %collective-permute-start.4 = (f32[1,128,128]{2,1,0:T(8,128)S(1)}, f32[1,128,128]{2,1,0:T(8,128)S(1)}, u32[]{:S(2)}, u32[]{:S(2)}) collective-permute-start(f32[1,128,128]{2,1,0:T(8,128)S(1)} %get-tuple-element.166), channel_id=1, source_target_pairs={{0,1},{1,2},{2,3},{3,4},{4,5},{5,6},{6,7},{7,8},{8,9},{9,10},{10,1... | collective-permute-start | bytes 196616 | tf_op jit(solution)/shard_map/while/body/eval_jaxpr/ppermute | solution.py:18
  622.4 10.4 %collective-permute-start = (f32[4,128,128]{2,1,0:T(8,128)S(1)}, f32[4,128,128]{2,1,0:T(8,128)S(1)}, u32[]{:S(2)}, u32[]{:S(2)}) collective-permute-start(f32[4,128,128]{2,1,0:T(8,128)S(1)} %slice_bitcast_fusion.7), channel_id=1, source_target_pairs={{0,16},{16,32},{32,48},{48,64},{64,80},{80,96},{96,112},{112,128},... | collective-permute-start | bytes 786440 | tf_op jit(solution)/shard_map/while/body/eval_jaxpr/ppermute | solution.py:30
  634.7 9.2 %collective-permute-start.2 = (f32[1,128,128]{2,1,0:T(8,128)S(1)}, f32[1,128,128]{2,1,0:T(8,128)S(1)}, u32[]{:S(2)}, u32[]{:S(2)}) collective-permute-start(f32[1,128,128]{2,1,0:T(8,128)S(1)} %get-tuple-element.164), channel_id=1, source_target_pairs={{0,1},{1,2},{2,3},{3,4},{4,5},{5,6},{6,7},{7,8},{8,9},{9,10},{10,1... | collective-permute-start | bytes 196616 | tf_op jit(solution)/shard_map/while/body/eval_jaxpr/ppermute | solution.py:18
  646.6 9.2 %collective-permute-start.4 = (f32[1,128,128]{2,1,0:T(8,128)S(1)}, f32[1,128,128]{2,1,0:T(8,128)S(1)}, u32[]{:S(2)}, u32[]{:S(2)}) collective-permute-start(f32[1,128,128]{2,1,0:T(8,128)S(1)} %get-tuple-element.166), channel_id=1, source_target_pairs={{0,1},{1,2},{2,3},{3,4},{4,5},{5,6},{6,7},{7,8},{8,9},{9,10},{10,1... | collective-permute-start | bytes 196616 | tf_op jit(solution)/shard_map/while/body/eval_jaxpr/ppermute | solution.py:18
  656.7 10.4 %collective-permute-start = (f32[4,128,128]{2,1,0:T(8,128)S(1)}, f32[4,128,128]{2,1,0:T(8,128)S(1)}, u32[]{:S(2)}, u32[]{:S(2)}) collective-permute-start(f32[4,128,128]{2,1,0:T(8,128)S(1)} %slice_bitcast_fusion.7), channel_id=1, source_target_pairs={{0,16},{16,32},{32,48},{48,64},{64,80},{80,96},{96,112},{112,128},... | collective-permute-start | bytes 786440 | tf_op jit(solution)/shard_map/while/body/eval_jaxpr/ppermute | solution.py:30
  669.0 9.2 %collective-permute-start.2 = (f32[1,128,128]{2,1,0:T(8,128)S(1)}, f32[1,128,128]{2,1,0:T(8,128)S(1)}, u32[]{:S(2)}, u32[]{:S(2)}) collective-permute-start(f32[1,128,128]{2,1,0:T(8,128)S(1)} %get-tuple-element.164), channel_id=1, source_target_pairs={{0,1},{1,2},{2,3},{3,4},{4,5},{5,6},{6,7},{7,8},{8,9},{9,10},{10,1... | collective-permute-start | bytes 196616 | tf_op jit(solution)/shard_map/while/body/eval_jaxpr/ppermute | solution.py:18
  680.9 9.2 %collective-permute-start.4 = (f32[1,128,128]{2,1,0:T(8,128)S(1)}, f32[1,128,128]{2,1,0:T(8,128)S(1)}, u32[]{:S(2)}, u32[]{:S(2)}) collective-permute-start(f32[1,128,128]{2,1,0:T(8,128)S(1)} %get-tuple-element.166), channel_id=1, source_target_pairs={{0,1},{1,2},{2,3},{3,4},{4,5},{5,6},{6,7},{7,8},{8,9},{9,10},{10,1... | collective-permute-start | bytes 196616 | tf_op jit(solution)/shard_map/while/body/eval_jaxpr/ppermute | solution.py:18
  (40 other events, 266.6 us)
where the time goes:
time: 696 us; the launch traced here: 693 us
  waiting for transfers between devices  432 us (62%)
  starting transfers between devices  220 us (32%)
  other arithmetic  36.3 us (5%)
    ppermute x41, waiting for transfers between devices, with_halo(): lax.ppermute(tail, axis, [(i, (i + 1) % count) for i in range(ends)])  277 us
    ppermute x18, waiting for transfers between devices, passed_along(): return lax.ppermute(x, axis, pairs)  152 us
    ppermute x41, starting transfers between devices, with_halo(): lax.ppermute(tail, axis, [(i, (i + 1) % count) for i in range(ends)])  97.9 us
    ppermute x41, starting transfers between devices, with_halo(): lax.ppermute(head, axis, [((i + 1) % count, i) for i in range(ends)])  85.2 us
    ppermute x18, starting transfers between devices, passed_along(): return lax.ppermute(x, axis, pairs)  36.6 us
  transfers between devices with their start and end apart: 100, of which 65 were waited for; matrix products, arithmetic and copies ran while one was open for 0% of the time, Pallas kernels for 0%

commit v1 on v0

v1 whole, which is shorter than its diff:
```python
import jax
import jax.numpy as jnp
from jax import lax
from jax.experimental import pallas as pl
from jax.experimental.pallas import tpu as pltpu
from jax.sharding import PartitionSpec as P

FINE = 0.04
COARSE = 0.16
NT = 16
NS = 16
PAD = 5
EXT = 4 + 2 * PAD
EVEN = [(i, i ^ 1) for i in range(NS)]
ODD = [(i, (i + 1) % NS if i % 2 else (i - 1) % NS) for i in range(NS)]
VMEM = pl.BlockSpec(memory_space=pltpu.VMEM)
SMEM = pl.BlockSpec(memory_space=pltpu.SMEM)


def place_of(t):
    return t ^ ((t >> 1) & 1)


def y_pairs():
    at = {place_of(t): t for t in range(NT)}
    pairs = []
    for t in range(NT):
        for s in range(NS):
            step = 1 if s % 2 else -1
            pairs.append((t * NS + s, at[(place_of(t) + step) % NT] * NS + (s ^ 1)))
    return pairs


YODD = y_pairs()


def even(x):
    return lax.ppermute(x, "space", EVEN)


def odd(x):
    return lax.ppermute(x, "space", ODD)


def yodd(x):
    return lax.ppermute(x, ("tm", "space"), YODD)


def struct(*shape):
    return jax.ShapeDtypeStruct(shape, jnp.float32)


def params(mib=48):
    return pltpu.CompilerParams(vmem_limit_bytes=mib * 1024 * 1024)


def set_coefficients(cond, kx, ky, kz, bb, lo, hi):
    row = lax.broadcasted_iota(jnp.int32, (128, 128), 0)
    col = lax.broadcasted_iota(jnp.int32, (128, 128), 1)
    inner_row = row < 127
    inner_col = col < 127
    ghosts = (
        (row == 0).astype(jnp.float32)
        + (row == 127).astype(jnp.float32)
        + (col == 0).astype(jnp.float32)
        + (col == 127).astype(jnp.float32)
    ) * (0.5 * FINE)

    @pl.loop(lo, hi)
    def _(l):
        here = cond[l]
        kx[l] = (0.5 * FINE) * (here + cond[l + 1])
        ky[l] = jnp.where(inner_row, (0.5 * FINE) * (here + pltpu.roll(here, 127, 0)), 0.0)
        kz[l] = jnp.where(inner_col, (0.5 * FINE) * (here + pltpu.roll(here, 127, 1)), 0.0)
        bb[l] = ghosts * here


def sweep(read, write, kx, ky, kz, bb, lo, hi):
    start = kx[lo - 1] * (read(lo) - read(lo - 1))

    def layer(l, behind):
        v = read(l)
        ahead = kx[l] * (read(l + 1) - v)
        fy = ky[l] * (pltpu.roll(v, 127, 0) - v)
        fz = kz[l] * (pltpu.roll(v, 127, 1) - v)
        change = (ahead - behind) + (fy - pltpu.roll(fy, 1, 0)) + (fz - pltpu.roll(fz, 1, 1)) - bb[l] * v
        write(l, v, change)
        return ahead

    lax.fori_loop(lo, hi, layer, start)


def clear_outside(s, store):
    @pl.when(s == 0)
    def _():
        for l in range(PAD):
            store(l)

    @pl.when(s == NS - 1)
    def _():
        for l in range(PAD + 4, EXT):
            store(l)


def fine_steps(states, count, widths, cond_refs, heat, s):
    kx, ky, kz, bb = cond_refs
    for turn in range(count):
        a, b = turn % 2, (turn + 1) % 2
        for f in range(2):
            h = widths[f] - 1 - turn

            def write(l, v, change):
                states[b, f, l] = v + change + heat[l]

            sweep(lambda l: states[a, f, l], write, kx, ky, kz, bb, PAD - h, PAD + 4 + h)

        def store(l):
            for f in range(2):
                states[b, f, l] = jnp.zeros((128, 128), jnp.float32)

        clear_outside(s, store)


def first_kernel(flags, g, cond, source, ev, od, out, state, cnd, heat, kx, ky, kz, bb):
    s = flags[1]
    core = s % 2
    for l in range(4):
        for f in range(2):
            state[0, f, PAD + l] = g[f, l]
        cnd[PAD + l] = cond[l]
        heat[PAD + l] = source[l]

    def sides(left, right):
        for l in range(4):
            for f in range(2):
                state[0, f, 1 + l] = left[f, l]
                state[0, f, PAD + 4 + l] = right[f, l]
            cnd[1 + l] = left[2, l]
            cnd[PAD + 4 + l] = right[2, l]
            heat[1 + l] = left[3, l]
            heat[PAD + 4 + l] = right[3, l]

    @pl.when(core == 0)
    def _():
        sides(od, ev)

    @pl.when(core == 1)
    def _():
        sides(ev, od)

    def store(l):
        zero = jnp.zeros((128, 128), jnp.float32)
        for f in range(2):
            state[0, f, l] = zero
        cnd[l] = zero

    clear_outside(s, store)
    set_coefficients(cnd, kx, ky, kz, bb, 1, EXT - 2)
    fine_steps(state, 4, (4, 4), (kx, ky, kz, bb), heat, s)
    for f in range(2):
        for l in range(4):
            out[f, l] = state[0, f, PAD + l]


def second_kernel(flags, a, cond, source, ev, od, evc, odc, ev5, od5, e_out, w_out, state, cnd, heat, kx, ky, kz, bb, wide):
    t, s = flags[0], flags[1]
    core = s % 2
    for l in range(4):
        for f in range(2):
            state[0, f, PAD + l] = a[f, l]
        cnd[PAD + l] = cond[l]
        heat[PAD + l] = source[l]

    def sides(left, right, leftc, rightc, left5, right5):
        for l in range(4):
            for f in range(2):
                state[0, f, 1 + l] = left[f, l]
                state[0, f, PAD + 4 + l] = right[f, l]
            cnd[1 + l] = leftc[2, l]
            cnd[PAD + 4 + l] = rightc[2, l]
            heat[1 + l] = leftc[3, l]
            heat[PAD + 4 + l] = rightc[3, l]
        state[0, 0, 0] = left5[0]
        state[0, 0, EXT - 1] = right5[0]
        cnd[0] = left5[1]
        cnd[EXT - 1] = right5[1]

    @pl.when(core == 0)
    def _():
        sides(od, ev, odc, evc, od5, ev5)

    @pl.when(core == 1)
    def _():
        sides(ev, od, evc, odc, ev5, od5)

    def store(l):
        zero = jnp.zeros((128, 128), jnp.float32)
        for f in range(2):
            state[0, f, l] = zero
        cnd[l] = zero

    clear_outside(s, store)
    set_coefficients(cnd, kx, ky, kz, bb, 0, EXT - 1)
    for f, h in ((0, 1), (1, 0)):

        def keep(l, v, change):
            wide[f, l] = v + (COARSE / FINE) * change

        sweep(lambda l: state[0, f, l], keep, kx, ky, kz, bb, PAD - h, PAD + 4 + h)
    fine_steps(state, 4, (5, 4), (kx, ky, kz, bb), heat, s)
    for l in range(PAD - 1, PAD + 5):
        wide[0, l] = state[0, 0, l] - wide[0, l]
    for l in range(PAD, PAD + 4):
        wide[1, l] = state[0, 1, l] - wide[1, l]

    def clear(l):
        wide[0, l] = jnp.zeros((128, 128), jnp.float32)

    clear_outside(s, clear)
    for l in range(4):
        w_out[l] = wide[0, PAD + l]

    def put(l, value):
        for to in range(NT):
            e_out[to, l] = value[8 * place_of(to) : 8 * place_of(to) + 8]

    def finish(l, v, change):
        wide[1, l] = v + (COARSE / FINE) * change + wide[1, l]

    sweep(lambda l: wide[0, l], finish, kx, ky, kz, bb, PAD, PAD + 4)

    @pl.when(t != NT - 1)
    def _():
        for l in range(4):
            put(l, wide[1, PAD + l])

    @pl.when(t == NT - 1)
    def _():
        for l in range(4):
            put(l, state[0, 0, PAD + l])
            w_out[l] = a[0, l]


def region(flags, cond, halo):
    chip, place = flags[1] // 2, flags[2]
    count = 8 + 2 * halo
    shape = (count, 24, 128)
    layer = lax.broadcasted_iota(jnp.int32, shape, 0) + (chip * 8 - halo)
    row = lax.broadcasted_iota(jnp.int32, shape, 1) + (place * 8 - 8)
    col = lax.broadcasted_iota(jnp.int32, shape, 2)
    inside = (layer >= 0) & (layer < 64) & (row >= 0) & (row < 128)
    mask = inside.astype(jnp.float32)
    c = cond[8 - halo : 16 + halo] * mask
    half = 0.5 * COARSE
    kx = half * (c[:-1] + c[1:])
    ky = half * (c + pltpu.roll(c, 23, 1))
    kz = jnp.where(col < 127, half * (c + pltpu.roll(c, 127, 2)), 0.0)
    bb = jnp.where((col == 0) | (col == 127), half * c, 0.0)
    return mask, kx, ky, kz, bb


def coarse_step(v, coefficients, halo, now):
    mask, kx, ky, kz, bb = coefficients
    skip = halo - now
    count = 8 + 2 * now
    inner = slice(skip + 1, skip + count - 1)
    fx = kx[skip : skip + count - 1] * (v[1:] - v[:-1])
    mid = v[1:-1]
    fy = ky[inner] * (pltpu.roll(mid, 23, 1) - mid)
    fz = kz[inner] * (pltpu.roll(mid, 127, 2) - mid)
    change = (fx[1:] - fx[:-1]) + (fy - pltpu.roll(fy, 1, 1)) + (fz - pltpu.roll(fz, 1, 2)) - bb[inner] * mid
    return mask[inner] * (mid + change)


def store_coefficients(coefficients, refs):
    for value, ref in zip(coefficients, refs):
        ref[...] = value


def gathered(core, own, x_got, x_swap, y_got, y_swap, buf, halo):
    rows = pl.ds(8, 8)
    buf[halo : halo + 8, 8:16] = own

    def put(left, right, below, above):
        buf[:halo, 8:16] = left
        buf[halo + 8 :, 8:16] = right
        buf[:, 0:8] = below
        buf[:, 16:24] = above

    @pl.when(core == 0)
    def _():
        put(x_got(), x_swap(), y_got(), y_swap())

    @pl.when(core == 1)
    def _():
        put(x_swap(), x_got(), y_swap(), y_got())


def pairs_kernel(flags, cond, own, other, xg, xs, yg, ys, p_out, ap_out, send, buf, *coef):
    core = flags[1] % 2
    store_coefficients(region(flags, cond, 2), coef)

    def tile(j):
        k = (j - 1) % NT
        mine, yours = own[k], other[k]
        first = jnp.where(core == 0, mine, yours)
        last = jnp.where(core == 0, yours, mine)
        return jnp.concatenate([first, last], 0)

    for i in range(8):
        gathered(core, tile(2 * i), lambda: xg[i], lambda: xs[i], lambda: yg[i], lambda: ys[i], buf, 2)
        c = tuple(r[...] for r in coef)
        one = coarse_step(buf[...] * c[0], c, 2, 2)
        two = coarse_step(one, c, 2, 1)
        ap_out[i] = one[1:9, 8:16]
        p_out[2 * i] = tile(2 * i)
        p_out[2 * i + 1] = tile(2 * i + 1) + two[:, 8:16]
    for q in range(4):

        @pl.when(core == 0)
        def _():
            send[q] = p_out[4 * q + 1, 0:4]

        @pl.when(core == 1)
        def _():
            send[q] = p_out[4 * q + 1, 4:8]


def half(core, value):
    return jnp.where(core == 0, value[0:4], value[4:8])


def quads_kernel(flags, cond, p, ap, xg, xs, yg, ys, p_out, zp_out, last, done, buf, *coef):
    core = flags[1] % 2
    store_coefficients(region(flags, cond, 4), coef)
    zero = jnp.zeros((4, 8, 128), jnp.float32)
    for q in range(4):
        j = 4 * q
        gathered(core, p[j + 1], lambda: xg[q], lambda: xs[q], lambda: yg[q], lambda: ys[q], buf, 4)
        c = tuple(r[...] for r in coef)
        v = buf[...] * c[0]
        powers = []
        for turn in range(4):
            v = coarse_step(v, c, 4, 4 - turn)
            powers.append(v[3 - turn : 11 - turn, 8:16])
        second = p[j + 2] + powers[1]
        third = p[j + 3] + powers[3]
        partial = [zero, half(core, ap[2 * q]), half(core, powers[0]), half(core, ap[2 * q + 1] + powers[2])]
        ends = [p[j], p[j + 1], second, third]
        if q == 0:
            last[...] = third
            for i in range(4):
                done[i, 0] = partial[i]
                done[i, 1] = half(core, ends[i])
        else:
            for i in range(4):
                p_out[4 * q - 4 + i] = ends[i]
                zp_out[4 * q - 4 + i] = partial[i]


def chain_kernel(q, flags, cond, c_in, p, zp, xg, xs, yg, ys, last, done, buf, *coef):
    core = flags[1] % 2
    store_coefficients(region(flags, cond, 8), coef)
    gathered(core, c_in[...], lambda: xg[...], lambda: xs[...], lambda: yg[...], lambda: ys[...], buf, 8)
    c = tuple(r[...] for r in coef)
    v = buf[...] * c[0]
    for turn in range(8):
        v = coarse_step(v, c, 8, 8 - turn)
        tile = v[7 - turn : 15 - turn, 8:16]
        i = turn // 2
        if turn % 2 == 0:
            done[i, 0] = zp[4 * q - 4 + i] + half(core, tile)
        else:
            full = p[4 * q - 4 + i] + tile
            done[i, 1] = half(core, full)
            if i == 3:
                last[...] = full


def final_kernel(got, w, out):
    for src in range(NT):
        rows = slice(8 * place_of(src), 8 * place_of(src) + 8)
        for l in range(4):
            out[0, l, rows] = got[src, 0, l] + w[l, rows]
            out[1, l, rows] = got[src, 1, l]


def scratch(halo):
    count = 8 + 2 * halo
    return [pltpu.VMEM((count, 24, 128), jnp.float32)] * 2 + [
        pltpu.VMEM((count - 1, 24, 128), jnp.float32),
    ] + [pltpu.VMEM((count, 24, 128), jnp.float32)] * 3


def call(kernel, outs, scratches, *args, smem=True):
    specs = [SMEM] + [VMEM] * (len(args) - 1) if smem else [VMEM] * len(args)
    return pl.pallas_call(
        kernel,
        out_shape=outs,
        in_specs=specs,
        out_specs=[VMEM] * len(outs),
        scratch_shapes=scratches,
        compiler_params=params(),
    )(*args)


def across(own_tile, send, core):
    got = odd(send)
    swap = even(got)
    left = jnp.where(core == 0, got, swap)
    right = jnp.where(core == 0, swap, got)
    wide = jnp.concatenate([left, own_tile, right], 1)
    y_got = yodd(wide)
    y_swap = even(y_got)
    return got, swap, y_got, y_swap


def body(initial, guess, cond, source):
    t = lax.axis_index("tm")
    s = lax.axis_index("space")
    core = s % 2
    place = t ^ ((t >> 1) & 1)
    flags = jnp.stack([t, s, place, core]).astype(jnp.int32)
    g = jnp.stack([jnp.where(t == NT - 1, initial, guess[0]), guess[1]])
    pack = jnp.concatenate([g, cond[None], source[None]])
    ev = even(pack)
    od = odd(pack)
    fine_scratch = [
        pltpu.VMEM((2, 2, EXT, 128, 128), jnp.float32),
    ] + [pltpu.VMEM((EXT, 128, 128), jnp.float32)] * 6
    (a,) = call(first_kernel, [struct(2, 4, 128, 128)], fine_scratch, flags, g, cond, source, ev, od)

    start = 8 * place
    rows_of = lambda x: lax.dynamic_slice_in_dim(jnp.pad(x, ((0, 0), (8, 8), (0, 0))), start, 24, 1)
    mine, yours = rows_of(cond), rows_of(ev[2])
    chip = jnp.where(core == 0, jnp.concatenate([mine, yours]), jnp.concatenate([yours, mine]))
    c_got = odd(chip)
    c_swap = even(c_got)
    tiles = jnp.where(
        core == 0, jnp.concatenate([c_got, chip, c_swap]), jnp.concatenate([c_swap, chip, c_got])
    )

    ev2 = even(a)
    near = lambda x: jnp.where(core == 0, x[0], x[3])
    tail = lambda x: jnp.where(core == 0, x[0], x[3])
    beyond = jnp.stack([tail(ev2[0]), tail(ev[2])])
    od2 = odd(jnp.concatenate([a.reshape(8, 128, 128), beyond]))
    nearest = lambda x: jnp.where(core == 0, x[3], x[0])
    ev5 = even(jnp.stack([nearest(od2[0:4]), nearest(od[2])]))
    e, w = call(
        second_kernel,
        [struct(NT, 4, 8, 128), struct(4, 128, 128)],
        fine_scratch + [pltpu.VMEM((2, EXT, 128, 128), jnp.float32)],
        flags, a, cond, source, ev2, od2[:8].reshape(2, 4, 128, 128), ev, od, ev5, od2[8:],
    )
    w_before = lax.ppermute(w, "tm", [(i, (i + 1) % NT) for i in range(NT)])
    own = lax.all_to_all(e, "tm", 0, 0)
    other = even(own)

    picks = [(2 * i - 1) % NT for i in range(8)]
    mine = jnp.stack([own[k] for k in picks])
    yours = jnp.stack([other[k] for k in picks])
    send = jnp.where(core == 0, mine[:, 0:2], mine[:, 2:4])
    both = jnp.where(core == 0, jnp.concatenate([mine, yours], 1), jnp.concatenate([yours, mine], 1))
    xg, xs, yg, ys = across(both, send, core)
    p, ap, send = call(
        pairs_kernel,
        [struct(NT, 8, 8, 128), struct(8, 8, 8, 128), struct(4, 4, 8, 128)],
        scratch(2),
        flags, tiles, own, other, xg, xs, yg, ys,
    )
    xg, xs, yg, ys = across(jnp.stack([p[1], p[5], p[9], p[13]]), send, core)
    p, zp, last, done = call(
        quads_kernel,
        [struct(12, 8, 8, 128), struct(12, 4, 8, 128), struct(8, 8, 128), struct(4, 2, 4, 8, 128)],
        scratch(4),
        flags, tiles, p, ap, xg, xs, yg, ys,
    )
    parts = [done]
    for q in (1, 2, 3):
        got = across(last[None], last[None], core)
        xg, xs, yg, ys = (x[0] for x in got)
        last, done = call(
            lambda *refs, q=q: chain_kernel(q, *refs),
            [struct(8, 8, 128), struct(4, 2, 4, 8, 128)],
            scratch(8),
            flags, tiles, last, p, zp, xg, xs, yg, ys,
        )
        parts.append(done)
    back = lax.all_to_all(jnp.concatenate(parts), "tm", 0, 0)
    (out,) = call(final_kernel, [struct(2, 4, 128, 128)], [], back, w_before, smem=False)
    return out


def solution(mesh):
    placed = (
        P("space", None, None),
        P("tm", "space", None, None),
        P("space", None, None),
        P("space", None, None),
    )
    return jax.shard_map(
        body, mesh=mesh, in_specs=placed, out_specs=P("tm", "space", None, None), check_vma=False
    )
```

time: 696 us -> 217 us (0.31)
  the two profiles are of different devices: /device:TPU:144 before, /device:TPU:16 now
where the time goes in v1:
time: 217 us; the launch traced here: 216 us
  waiting for transfers between devices  125 us (58%)
  Pallas kernels  39.7 us (18%)
  starting transfers between devices  24.6 us (11%)
  blocking collectives  21.4 us (10%)
  other arithmetic  3.2 us (1%)
  local copies, waits for them, and re-layouts  2.25 us (1%)
    ppermute x8, waiting for transfers between devices, odd(): return lax.ppermute(x, 'space', ODD)  58.2 us
    pallas_call x8, Pallas kernels, call(): pl.pallas_call(kernel, out_shape=outs, in_specs=specs, out_specs=[VMEM] *...  39.7 us
    ppermute x5, waiting for transfers between devices, yodd(): return lax.ppermute(x, ('tm', 'space'), YODD)  30.3 us
    all_to_all x1, blocking collectives, body(): own = lax.all_to_all(e, 'tm', 0, 0)  21.4 us
    ppermute x1, waiting for transfers between devices, body(): w_before = lax.ppermute(w, 'tm', [(i, (i + 1) % NT) for i in range(NT)])  20 us
    ppermute x8, starting transfers between devices, odd(): return lax.ppermute(x, 'space', ODD)  17.2 us
    ppermute x15, waiting for transfers between devices, even(): return lax.ppermute(x, 'space', EVEN)  16.1 us
  transfers between devices with their start and end apart: 30, of which 28 were waited for; matrix products, arithmetic and copies ran while one was open for 0% of the time, Pallas kernels for 0%

profile of v1, /device:TPU:16, one launch (start us, length us, event | category | flops | bytes accessed | tf_op | source)
XLA Modules:
  0.0 216.0 jit_solution(17091045928487969332)
XLA Ops:
  0.0 1.0 slice.124
  1.1 0.1 copy-done.2
  1.2 0.9 copy-done
  2.1 0.1 copy-done.1
  2.2 1.1 pad_maximum_fusion
  3.2 2.6 %collective-permute-start.3 = (f32[4,4,128,128]{3,2,1,0:T(8,128)}, f32[4,4,128,128]{3,2,1,0:T(8,128)S(1)}, u32[]{:S(2)}, u32[]{:S(2)}) collective-permute-start(f32[4,4,128,128]{3,2,1,0:T(8,128)} %pad_maximum_fusion), channel_id=1, source_target_pairs={{0,15},{1,2},{2,1},{3,4},{4,3},{5,6},{6,5},{7,8},{8,7},{9,10},{10,... | collective-permute-start | bytes 3145736 | tf_op jit(solution)/shard_map/ppermute | solution.py:42
  5.9 0.1 pad_add_fusion.flags.refs_0_
  6.0 0.1 collective-permute-done.ev.evc
  6.1 15.2 %collective-permute-done.3.od.odc = f32[4,4,128,128]{3,2,1,0:T(8,128)S(1)} collective-permute-done((f32[4,4,128,128]{3,2,1,0:T(8,128)}, f32[4,4,128,128]{3,2,1,0:T(8,128)S(1)}, u32[]{:S(2)}, u32[]{:S(2)}) %collective-permute-start.3) | collective-permute-done | bytes 1048608 | tf_op jit(solution)/shard_map/ppermute | solution.py:42
  21.3 10.8 %shard_map.46.a = f32[2,4,128,128]{3,2,1,0:T(8,128)S(1)} custom-call(s32[4]{0:T(128)S(1)} %pad_add_fusion.flags.refs_0_, f32[2,4,128,128]{3,2,1,0:T(8,128)S(1)} %pad_maximum_fusion.2.g, f32[4,128,128]{2,1,0:T(8,128)S(1)} %copy-done, f32[4,128,128]{2,1,0:T(8,128)S(1)} %copy-done.1, f32[4,4,128,128]{3,2,1,0:T(8,128)S(1)} %collective-permute-done.ev.evc, ...), custom_call_target="tpu_custom_call" | custom-call | tf_op jit(solution)/shard_map/pallas_call | solution.py:397
  32.1 0.1 collective-permute-start.4
  32.2 2.0 collective-permute-done.4.ev
  34.2 0.9 fusion.6
  35.2 2.7 %collective-permute-start.5 = (f32[10,128,128]{2,1,0:T(8,128)S(1)}, f32[10,128,128]{2,1,0:T(8,128)S(1)}, u32[]{:S(2)}, u32[]{:S(2)}) collective-permute-start(f32[10,128,128]{2,1,0:T(8,128)S(1)} %pad_maximum_fusion.1), channel_id=1, source_target_pairs={{0,15},{1,2},{2,1},{3,4},{4,3},{5,6},{6,5},{7,8},{8,7},{9,10},{10,... | collective-permute-start | bytes 1966088 | tf_op jit(solution)/shard_map/ppermute | solution.py:42
  37.9 11.0 %collective-permute-done.5 = f32[10,128,128]{2,1,0:T(8,128)S(1)} collective-permute-done((f32[10,128,128]{2,1,0:T(8,128)S(1)}, f32[10,128,128]{2,1,0:T(8,128)S(1)}, u32[]{:S(2)}, u32[]{:S(2)}) %collective-permute-start.5) | collective-permute-done | bytes 655392 | tf_op jit(solution)/shard_map/ppermute | solution.py:42
  48.9 0.1 collective-permute-start.6
  49.1 1.3 collective-permute-done.6.ev5
  50.4 15.1 %shard_map.47 = (f32[16,4,8,128]{3,2,1,0:T(8,128)S(1)}, f32[4,128,128]{2,1,0:T(8,128)S(1)}) custom-call(s32[4]{0:T(128)S(1)} %pad_add_fusion.flags.refs_0_, f32[2,4,128,128]{3,2,1,0:T(8,128)S(1)} %shard_map.46.a, f32[4,128,128]{2,1,0:T(8,128)S(1)} %copy-done, f32[4,128,128]{2,1,0:T(8,128)S(1)} %copy-done.1, f32[2,4,128,128]{3,2,1,0:T(8,128)} %collective-permute-done.4.ev, ...), custom_call_target="tpu_custom_call" | custom-call | tf_op jit(solution)/shard_map/pallas_call | solution.py:397
  65.5 21.4 %all_to_all.10.own = f32[16,4,8,128]{3,2,1,0:T(8,128)S(1)} all-to-all(f32[16,4,8,128]{3,2,1,0:T(8,128)S(1)} %get-tuple-element.19), channel_id=1, replica_groups=mesh['tm'=16,'space'=16] {'tm'}, dimensions={0} | all-to-all | bytes 524288 | tf_op jit(solution)/shard_map/all_to_all | solution.py:457
  87.0 1.8 collective-permute-start.8
  88.7 5.6 %collective-permute-done.8.xg = f32[8,2,8,128]{3,2,1,0:T(8,128)S(1)} collective-permute-done((f32[8,2,8,128]{3,2,1,0:T(8,128)S(1)}, f32[8,2,8,128]{3,2,1,0:T(8,128)S(1)}, u32[]{:S(2)}, u32[]{:S(2)}) %collective-permute-start.8) | collective-permute-done | bytes 65568 | tf_op jit(solution)/shard_map/ppermute | solution.py:42
  94.4 0.0 collective-permute-start.9
  94.4 0.5 collective-permute-start.7
  94.9 0.7 collective-permute-done.9.xs
  95.6 0.4 collective-permute-done.7.other
  96.2 0.3 collective-permute-start.10
  96.6 8.1 %collective-permute-done.10.yg = f32[8,12,8,128]{3,2,1,0:T(8,128)S(1)} collective-permute-done((f32[8,12,8,128]{3,2,1,0:T(8,128)S(1)}, f32[8,12,8,128]{3,2,1,0:T(8,128)S(1)}, u32[]{:S(2)}, u32[]{:S(2)}) %collective-permute-start.10) | collective-permute-done | bytes 393248 | tf_op jit(solution)/shard_map/ppermute | solution.py:46
  104.7 2.1 collective-permute-start.1
  106.8 5.6 %collective-permute-done.1 = f32[8,24,128]{2,1,0:T(8,128)S(1)} collective-permute-done((f32[8,24,128]{2,1,0:T(8,128)S(1)}, f32[8,24,128]{2,1,0:T(8,128)S(1)}, u32[]{:S(2)}, u32[]{:S(2)}) %collective-permute-start.1) | collective-permute-done | bytes 98336 | tf_op jit(solution)/shard_map/ppermute | solution.py:42
  112.4 1.3 collective-permute-done.2
  113.8 3.3 %shard_map.48 = (f32[16,8,8,128]{3,2,1,0:T(8,128)S(1)}, f32[8,8,8,128]{3,2,1,0:T(8,128)S(1)}, f32[4,4,8,128]{3,2,1,0:T(8,128)S(1)}) custom-call(s32[4]{0:T(128)S(1)} %pad_add_fusion.flags.refs_0_, f32[24,24,128]{2,1,0:T(8,128)S(1)} %fusion.1.cond.refs_1_, f32[16,4,8,128]{3,2,1,0:T(8,128)S(1)} %all_to_all.10.own, ...), custom_call_target="tpu_custom_call" | custom-call | tf_op jit(solution)/shard_map/pallas_call | solution.py:397
  117.0 2.2 %collective-permute-start.12 = (f32[4,4,8,128]{3,2,1,0:T(8,128)S(1)}, f32[4,4,8,128]{3,2,1,0:T(8,128)S(1)}, u32[]{:S(2)}, u32[]{:S(2)}) collective-permute-start(f32[4,4,8,128]{3,2,1,0:T(8,128)S(1)} %get-tuple-element.22), channel_id=1, source_target_pairs={{0,15},{1,2},{2,1},{3,4},{4,3},{5,6},{6,5},{7,8},{8,7},{9,10},{10,... | collective-permute-start | bytes 196616 | tf_op jit(solution)/shard_map/ppermute | solution.py:42
  119.2 5.2 %collective-permute-done.12.xg = f32[4,4,8,128]{3,2,1,0:T(8,128)S(1)} collective-permute-done((f32[4,4,8,128]{3,2,1,0:T(8,128)S(1)}, f32[4,4,8,128]{3,2,1,0:T(8,128)S(1)}, u32[]{:S(2)}, u32[]{:S(2)}) %collective-permute-start.12) | collective-permute-done | bytes 65568 | tf_op jit(solution)/shard_map/ppermute | solution.py:42
  124.4 1.2 collective-permute-done.13.xs
  125.7 0.5 collective-permute-start.14
  126.2 6.6 %collective-permute-done.14.yg = f32[4,16,8,128]{3,2,1,0:T(8,128)S(1)} collective-permute-done((f32[4,16,8,128]{3,2,1,0:T(8,128)S(1)}, f32[4,16,8,128]{3,2,1,0:T(8,128)S(1)}, u32[]{:S(2)}, u32[]{:S(2)}) %collective-permute-start.14) | collective-permute-done | bytes 262176 | tf_op jit(solution)/shard_map/ppermute | solution.py:46
  132.8 1.5 collective-permute-done.15.ys
  134.4 3.1 %shard_map.49 = (f32[12,8,8,128]{3,2,1,0:T(8,128)S(1)}, f32[12,4,8,128]{3,2,1,0:T(8,128)S(1)}, f32[8,8,128]{2,1,0:T(8,128)S(1)}, f32[4,2,4,8,128]{4,3,2,1,0:T(8,128)S(1)}) custom-call(s32[4]{0:T(128)S(1)} %pad_add_fusion.flags.refs_0_, f32[24,24,128]{2,1,0:T(8,128)S(1)} %fusion.1.cond.refs_1_, f32[16,8,8,128]{3,2,1,0:T(8,128)S(1)} %get-tuple-element.20.p, ...), custom_call_target="tpu_custom_call" | custom-call | tf_op jit(solution)/shard_map/pallas_call | solution.py:397
  137.4 2.0 collective-permute-start.16
  139.4 5.0 %collective-permute-done.16 = f32[1,8,8,128]{3,2,1,0:T(8,128)S(1)} collective-permute-done((f32[1,8,8,128]{3,2,1,0:T(8,128)S(1)}, f32[1,8,8,128]{3,2,1,0:T(8,128)S(1)}, u32[]{:S(2)}, u32[]{:S(2)}) %collective-permute-start.16) | collective-permute-done | bytes 32800 | tf_op jit(solution)/shard_map/ppermute | solution.py:42
  144.5 1.2 collective-permute-done.17
  145.7 0.3 collective-permute-start.18
  146.0 5.1 %collective-permute-done.18 = f32[1,24,8,128]{3,2,1,0:T(8,128)S(1)} collective-permute-done((f32[1,24,8,128]{3,2,1,0:T(8,128)S(1)}, f32[1,24,8,128]{3,2,1,0:T(8,128)S(1)}, u32[]{:S(2)}, u32[]{:S(2)}) %collective-permute-start.18) | collective-permute-done | bytes 98336 | tf_op jit(solution)/shard_map/ppermute | solution.py:46
  151.0 1.3 collective-permute-done.19
  152.3 2.0 shard_map.50
  154.3 1.8 collective-permute-start.20
  156.1 5.2 %collective-permute-done.20 = f32[1,8,8,128]{3,2,1,0:T(8,128)S(1)} collective-permute-done((f32[1,8,8,128]{3,2,1,0:T(8,128)S(1)}, f32[1,8,8,128]{3,2,1,0:T(8,128)S(1)}, u32[]{:S(2)}, u32[]{:S(2)}) %collective-permute-start.20) | collective-permute-done | bytes 32800 | tf_op jit(solution)/shard_map/ppermute | solution.py:42
  161.4 1.2 collective-permute-done.21
  162.6 0.1 collective-permute-start.22
  162.7 5.2 %collective-permute-done.22 = f32[1,24,8,128]{3,2,1,0:T(8,128)S(1)} collective-permute-done((f32[1,24,8,128]{3,2,1,0:T(8,128)S(1)}, f32[1,24,8,128]{3,2,1,0:T(8,128)S(1)}, u32[]{:S(2)}, u32[]{:S(2)}) %collective-permute-start.22) | collective-permute-done | bytes 98336 | tf_op jit(solution)/shard_map/ppermute | solution.py:46
  167.9 1.3 collective-permute-done.23
  169.2 2.0 shard_map.51
  171.2 1.9 collective-permute-start.24
  173.1 5.4 %collective-permute-done.24 = f32[1,8,8,128]{3,2,1,0:T(8,128)S(1)} collective-permute-done((f32[1,8,8,128]{3,2,1,0:T(8,128)S(1)}, f32[1,8,8,128]{3,2,1,0:T(8,128)S(1)}, u32[]{:S(2)}, u32[]{:S(2)}) %collective-permute-start.24) | collective-permute-done | bytes 32800 | tf_op jit(solution)/shard_map/ppermute | solution.py:42
  178.5 1.2 collective-permute-done.25
  179.7 0.1 collective-permute-start.26
  179.8 5.2 %collective-permute-done.26 = f32[1,24,8,128]{3,2,1,0:T(8,128)S(1)} collective-permute-done((f32[1,24,8,128]{3,2,1,0:T(8,128)S(1)}, f32[1,24,8,128]{3,2,1,0:T(8,128)S(1)}, u32[]{:S(2)}, u32[]{:S(2)}) %collective-permute-start.26) | collective-permute-done | bytes 98336 | tf_op jit(solution)/shard_map/ppermute | solution.py:46
  185.1 1.3 collective-permute-done.27
  186.4 2.6 %shard_map.52 = (f32[8,8,128]{2,1,0:T(8,128)}, f32[4,2,4,8,128]{4,3,2,1,0:T(8,128)S(1)}) custom-call(s32[4]{0:T(128)S(1)} %pad_add_fusion.flags.refs_0_, f32[24,24,128]{2,1,0:T(8,128)S(1)} %fusion.1.cond.refs_1_, f32[8,8,128]{2,1,0:T(8,128)S(1)} %get-tuple-element.30.refs_2_, f32[12,8,8,128]{3,2,1,0:T(8,128)S(1)} %get-tuple-element.25.refs_3_, ...), custom_call_target="tpu_custom_call" | custom-call | tf_op jit(solution)/shard_map/pallas_call | solution.py:397
  188.9 0.8 pad_maximum_fusion.3
  189.8 3.6 %all-to-all-start.1 = ((f32[16,2,4,8,128]{4,3,2,1,0:T(8,128)}), f32[16,2,4,8,128]{4,3,2,1,0:T(8,128)S(1)}, u32[]{:S(2)}, u32[]{:S(2)}) async-start(f32[16,2,4,8,128]{4,3,2,1,0:T(8,128)} %pad_maximum_fusion.3), calls=%async_computation.1 | async-start | bytes 1048576 | tf_op jit(solution)/shard_map/all_to_all | solution.py:490
  193.4 1.8 collective-permute-start.28
  195.2 20.0 %collective-permute-done.28.w = f32[4,128,128]{2,1,0:T(8,128)S(1)} collective-permute-done((f32[4,128,128]{2,1,0:T(8,128)S(1)}, f32[4,128,128]{2,1,0:T(8,128)S(1)}, u32[]{:S(2)}, u32[]{:S(2)}) %collective-permute-start.28) | collective-permute-done | bytes 262176 | tf_op jit(solution)/shard_map/ppermute | solution.py:456
  215.2 0.8 shard_map.53
  (59 shorter events, 0.5 us)
Async XLA Ops:
  0.0 1.1 copy-start.2
  1.1 0.9 copy-start
  1.1 1.0 copy-start.1
  3.2 2.9 %collective-permute-start = (f32[4,4,128,128]{3,2,1,0:T(8,128)}, f32[4,4,128,128]{3,2,1,0:T(8,128)S(1)}, u32[]{:S(2)}, u32[]{:S(2)}) collective-permute-start(f32[4,4,128,128]{3,2,1,0:T(8,128)} %pad_maximum_fusion), channel_id=1, source_target_pairs={{0,1},{1,0},{2,3},{3,2},{4,5},{5,4},{6,7},{7,6},{8,9},{9,8},{10,11... | collective-permute-start | bytes 3145736 | tf_op jit(solution)/shard_map/ppermute | solution.py:38
  3.2 18.0 %collective-permute-start.3 = (f32[4,4,128,128]{3,2,1,0:T(8,128)}, f32[4,4,128,128]{3,2,1,0:T(8,128)S(1)}, u32[]{:S(2)}, u32[]{:S(2)}) collective-permute-start(f32[4,4,128,128]{3,2,1,0:T(8,128)} %pad_maximum_fusion), channel_id=1, source_target_pairs={{0,15},{1,2},{2,1},{3,4},{4,3},{5,6},{6,5},{7,8},{8,7},{9,10},{10,... | collective-permute-start | bytes 3145736 | tf_op jit(solution)/shard_map/ppermute | solution.py:42
  32.1 2.1 collective-permute-start.4
  35.2 13.7 %collective-permute-start.5 = (f32[10,128,128]{2,1,0:T(8,128)S(1)}, f32[10,128,128]{2,1,0:T(8,128)S(1)}, u32[]{:S(2)}, u32[]{:S(2)}) collective-permute-start(f32[10,128,128]{2,1,0:T(8,128)S(1)} %pad_maximum_fusion.1), channel_id=1, source_target_pairs={{0,15},{1,2},{2,1},{3,4},{4,3},{5,6},{6,5},{7,8},{8,7},{9,10},{10,... | collective-permute-start | bytes 1966088 | tf_op jit(solution)/shard_map/ppermute | solution.py:42
  48.9 1.4 collective-permute-start.6
  87.0 7.4 %collective-permute-start.8 = (f32[8,2,8,128]{3,2,1,0:T(8,128)S(1)}, f32[8,2,8,128]{3,2,1,0:T(8,128)S(1)}, u32[]{:S(2)}, u32[]{:S(2)}) collective-permute-start(f32[8,2,8,128]{3,2,1,0:T(8,128)S(1)} %slice_select_fusion), channel_id=1, source_target_pairs={{0,15},{1,2},{2,1},{3,4},{4,3},{5,6},{6,5},{7,8},{8,7},{9,10},{10,... | collective-permute-start | bytes 196616 | tf_op jit(solution)/shard_map/ppermute | solution.py:42
  94.4 1.3 collective-permute-start.9
  94.4 1.7 collective-permute-start.7
  96.2 8.5 %collective-permute-start.10 = (f32[8,12,8,128]{3,2,1,0:T(8,128)S(1)}, f32[8,12,8,128]{3,2,1,0:T(8,128)S(1)}, u32[]{:S(2)}, u32[]{:S(2)}) collective-permute-start(f32[8,12,8,128]{3,2,1,0:T(8,128)S(1)} %pad_maximum_fusion.4), channel_id=1, source_target_pairs={{0,225},{1,16},{2,227},{3,18},{4,229},{5,20},{6,231},{7,22},{8,233... | collective-permute-start | bytes 1179656 | tf_op jit(solution)/shard_map/ppermute | solution.py:46
  104.7 9.1 %collective-permute-start.11 = (f32[8,12,8,128]{3,2,1,0:T(8,128)S(1)}, f32[8,12,8,128]{3,2,1,0:T(8,128)S(1)}, u32[]{:S(2)}, u32[]{:S(2)}) collective-permute-start(f32[8,12,8,128]{3,2,1,0:T(8,128)S(1)} %collective-permute-done.10.yg), channel_id=1, source_target_pairs={{0,1},{1,0},{2,3},{3,2},{4,5},{5,4},{6,7},{7,6},{8,9},{9,8},{10,11... | collective-permute-start | bytes 1179656 | tf_op jit(solution)/shard_map/ppermute | solution.py:38
  104.7 7.7 %collective-permute-start.1 = (f32[8,24,128]{2,1,0:T(8,128)S(1)}, f32[8,24,128]{2,1,0:T(8,128)S(1)}, u32[]{:S(2)}, u32[]{:S(2)}) collective-permute-start(f32[8,24,128]{2,1,0:T(8,128)S(1)} %maximum_select_fusion.1), channel_id=1, source_target_pairs={{0,15},{1,2},{2,1},{3,4},{4,3},{5,6},{6,5},{7,8},{8,7},{9,10},{10,... | collective-permute-start | bytes 294920 | tf_op jit(solution)/shard_map/ppermute | solution.py:42
  112.4 1.3 collective-permute-start.2
  117.0 7.4 %collective-permute-start.12 = (f32[4,4,8,128]{3,2,1,0:T(8,128)S(1)}, f32[4,4,8,128]{3,2,1,0:T(8,128)S(1)}, u32[]{:S(2)}, u32[]{:S(2)}) collective-permute-start(f32[4,4,8,128]{3,2,1,0:T(8,128)S(1)} %get-tuple-element.22), channel_id=1, source_target_pairs={{0,15},{1,2},{2,1},{3,4},{4,3},{5,6},{6,5},{7,8},{8,7},{9,10},{10,... | collective-permute-start | bytes 196616 | tf_op jit(solution)/shard_map/ppermute | solution.py:42
  124.4 1.3 collective-permute-start.13
  125.7 7.1 %collective-permute-start.14 = (f32[4,16,8,128]{3,2,1,0:T(8,128)S(1)}, f32[4,16,8,128]{3,2,1,0:T(8,128)S(1)}, u32[]{:S(2)}, u32[]{:S(2)}) collective-permute-start(f32[4,16,8,128]{3,2,1,0:T(8,128)S(1)} %pad_maximum_fusion.7), channel_id=1, source_target_pairs={{0,225},{1,16},{2,227},{3,18},{4,229},{5,20},{6,231},{7,22},{8,233... | collective-permute-start | bytes 786440 | tf_op jit(solution)/shard_map/ppermute | solution.py:46
  132.8 1.5 collective-permute-start.15
  137.4 7.0 %collective-permute-start.16 = (f32[1,8,8,128]{3,2,1,0:T(8,128)S(1)}, f32[1,8,8,128]{3,2,1,0:T(8,128)S(1)}, u32[]{:S(2)}, u32[]{:S(2)}) collective-permute-start(f32[1,8,8,128]{3,2,1,0:T(8,128)S(1)} %bitcast.43), channel_id=1, source_target_pairs={{0,15},{1,2},{2,1},{3,4},{4,3},{5,6},{6,5},{7,8},{8,7},{9,10},{10,... | collective-permute-start | bytes 98312 | tf_op jit(solution)/shard_map/ppermute | solution.py:42
  144.5 1.2 collective-permute-start.17
  145.7 5.3 %collective-permute-start.18 = (f32[1,24,8,128]{3,2,1,0:T(8,128)S(1)}, f32[1,24,8,128]{3,2,1,0:T(8,128)S(1)}, u32[]{:S(2)}, u32[]{:S(2)}) collective-permute-start(f32[1,24,8,128]{3,2,1,0:T(8,128)S(1)} %pad_maximum_fusion.9), channel_id=1, source_target_pairs={{0,225},{1,16},{2,227},{3,18},{4,229},{5,20},{6,231},{7,22},{8,233... | collective-permute-start | bytes 294920 | tf_op jit(solution)/shard_map/ppermute | solution.py:46
  151.0 1.3 collective-permute-start.19
  154.3 7.0 %collective-permute-start.20 = (f32[1,8,8,128]{3,2,1,0:T(8,128)S(1)}, f32[1,8,8,128]{3,2,1,0:T(8,128)S(1)}, u32[]{:S(2)}, u32[]{:S(2)}) collective-permute-start(f32[1,8,8,128]{3,2,1,0:T(8,128)S(1)} %bitcast.45), channel_id=1, source_target_pairs={{0,15},{1,2},{2,1},{3,4},{4,3},{5,6},{6,5},{7,8},{8,7},{9,10},{10,... | collective-permute-start | bytes 98312 | tf_op jit(solution)/shard_map/ppermute | solution.py:42
  161.4 1.2 collective-permute-start.21
  162.6 5.3 %collective-permute-start.22 = (f32[1,24,8,128]{3,2,1,0:T(8,128)S(1)}, f32[1,24,8,128]{3,2,1,0:T(8,128)S(1)}, u32[]{:S(2)}, u32[]{:S(2)}) collective-permute-start(f32[1,24,8,128]{3,2,1,0:T(8,128)S(1)} %pad_maximum_fusion.10), channel_id=1, source_target_pairs={{0,225},{1,16},{2,227},{3,18},{4,229},{5,20},{6,231},{7,22},{8,233... | collective-permute-start | bytes 294920 | tf_op jit(solution)/shard_map/ppermute | solution.py:46
  167.9 1.3 collective-permute-start.23
  171.2 7.3 %collective-permute-start.24 = (f32[1,8,8,128]{3,2,1,0:T(8,128)S(1)}, f32[1,8,8,128]{3,2,1,0:T(8,128)S(1)}, u32[]{:S(2)}, u32[]{:S(2)}) collective-permute-start(f32[1,8,8,128]{3,2,1,0:T(8,128)S(1)} %bitcast.41), channel_id=1, source_target_pairs={{0,15},{1,2},{2,1},{3,4},{4,3},{5,6},{6,5},{7,8},{8,7},{9,10},{10,... | collective-permute-start | bytes 98312 | tf_op jit(solution)/shard_map/ppermute | solution.py:42
  178.5 1.2 collective-permute-start.25
  179.7 5.3 %collective-permute-start.26 = (f32[1,24,8,128]{3,2,1,0:T(8,128)S(1)}, f32[1,24,8,128]{3,2,1,0:T(8,128)S(1)}, u32[]{:S(2)}, u32[]{:S(2)}) collective-permute-start(f32[1,24,8,128]{3,2,1,0:T(8,128)S(1)} %pad_maximum_fusion.11), channel_id=1, source_target_pairs={{0,225},{1,16},{2,227},{3,18},{4,229},{5,20},{6,231},{7,22},{8,233... | collective-permute-start | bytes 294920 | tf_op jit(solution)/shard_map/ppermute | solution.py:46
  185.1 1.3 collective-permute-start.27
  189.8 25.4 %all-to-all-start.1 = ((f32[16,2,4,8,128]{4,3,2,1,0:T(8,128)}), f32[16,2,4,8,128]{4,3,2,1,0:T(8,128)S(1)}, u32[]{:S(2)}, u32[]{:S(2)}) async-start(f32[16,2,4,8,128]{4,3,2,1,0:T(8,128)} %pad_maximum_fusion.3), calls=%async_computation.1 | async-start | bytes 1048576 | tf_op jit(solution)/shard_map/all_to_all | solution.py:490
  193.4 21.8 %collective-permute-start.28 = (f32[4,128,128]{2,1,0:T(8,128)S(1)}, f32[4,128,128]{2,1,0:T(8,128)S(1)}, u32[]{:S(2)}, u32[]{:S(2)}) collective-permute-start(f32[4,128,128]{2,1,0:T(8,128)S(1)} %get-tuple-element.32), channel_id=1, source_target_pairs={{0,16},{16,32},{32,48},{48,64},{64,80},{80,96},{96,112},{112,128},... | collective-permute-start | bytes 786440 | tf_op jit(solution)/shard_map/ppermute | solution.py:456

commit v2 on v1

--- a/solution.py
+++ b/solution.py
@@ -12,13 +12,27 @@
 PAD = 5
 EXT = 4 + 2 * PAD
 EVEN = [(i, i ^ 1) for i in range(NS)]
-ODD = [(i, (i + 1) % NS if i % 2 else (i - 1) % NS) for i in range(NS)]
+
+
+def odd_pairs():
+    pairs = []
+    for t in range(NT):
+        for s in range(NS):
+            to = s + 1 if s % 2 else s - 1
+            pairs.append((t * NS + s, t * NS + to if 0 <= to < NS else (t ^ 1) * NS + s))
+    return pairs
+
+
+ODD = odd_pairs()
 VMEM = pl.BlockSpec(memory_space=pltpu.VMEM)
 SMEM = pl.BlockSpec(memory_space=pltpu.SMEM)
 
 
 def place_of(t):
     return t ^ ((t >> 1) & 1)
+
+
+PLACE = [place_of(t) for t in range(NT)]
 
 
 def y_pairs():
@@ -39,7 +53,7 @@
 
 
 def odd(x):
-    return lax.ppermute(x, "space", ODD)
+    return lax.ppermute(x, ("tm", "space"), ODD)
 
 
 def yodd(x):
@@ -54,87 +68,99 @@
     return pltpu.CompilerParams(vmem_limit_bytes=mib * 1024 * 1024)
 
 
-def set_coefficients(cond, kx, ky, kz, bb, lo, hi):
+def set_coefficients(cond, kx, ky, kz, aa, lo, hi):
     row = lax.broadcasted_iota(jnp.int32, (128, 128), 0)
     col = lax.broadcasted_iota(jnp.int32, (128, 128), 1)
-    inner_row = row < 127
-    inner_col = col < 127
     ghosts = (
         (row == 0).astype(jnp.float32)
         + (row == 127).astype(jnp.float32)
         + (col == 0).astype(jnp.float32)
         + (col == 127).astype(jnp.float32)
     ) * (0.5 * FINE)
-
-    @pl.loop(lo, hi)
-    def _(l):
+    rows = (row < 127).astype(jnp.float32) * (0.5 * FINE)
+    cols = (col < 127).astype(jnp.float32) * (0.5 * FINE)
+    for l in range(lo, hi):
         here = cond[l]
         kx[l] = (0.5 * FINE) * (here + cond[l + 1])
-        ky[l] = jnp.where(inner_row, (0.5 * FINE) * (here + pltpu.roll(here, 127, 0)), 0.0)
-        kz[l] = jnp.where(inner_col, (0.5 * FINE) * (here + pltpu.roll(here, 127, 1)), 0.0)
-        bb[l] = ghosts * here
-
-
-def sweep(read, write, kx, ky, kz, bb, lo, hi):
-    start = kx[lo - 1] * (read(lo) - read(lo - 1))
-
-    def layer(l, behind):
-        v = read(l)
-        ahead = kx[l] * (read(l + 1) - v)
-        fy = ky[l] * (pltpu.roll(v, 127, 0) - v)
-        fz = kz[l] * (pltpu.roll(v, 127, 1) - v)
-        change = (ahead - behind) + (fy - pltpu.roll(fy, 1, 0)) + (fz - pltpu.roll(fz, 1, 1)) - bb[l] * v
-        write(l, v, change)
-        return ahead
-
-    lax.fori_loop(lo, hi, layer, start)
-
-
-def clear_outside(s, store):
+        ky[l] = rows * (here + pltpu.roll(here, 127, 0))
+        kz[l] = cols * (here + pltpu.roll(here, 127, 1))
+        aa[l] = 1.0 - ghosts * here
+
+
+def rows_at(r):
+    return slice(8 * r, 8 * r + 8)
+
+
+def sweep(read, finish, coefficients, lo, hi):
+    kx, ky, kz, aa = coefficients
+    sub = lax.broadcasted_iota(jnp.int32, (8, 128), 0)
+    bottom, top = sub == 0, sub == 7
+    behind = [kx[lo - 1, rows_at(r)] * (read(lo, rows_at(r)) - read(lo - 1, rows_at(r))) for r in range(16)]
+    for l in range(lo, hi):
+        v = [read(l, rows_at(r)) for r in range(16)]
+        rolled = [pltpu.roll(x, 7, 0) for x in v]
+        flux = [
+            ky[l, rows_at(r)] * ((jnp.where(top, rolled[r + 1], rolled[r]) if r < 15 else rolled[r]) - v[r])
+            for r in range(16)
+        ]
+        back = [pltpu.roll(x, 1, 0) for x in flux]
+        ahead = []
+        for r in range(16):
+            rows = rows_at(r)
+            fx = kx[l, rows] * (read(l + 1, rows) - v[r])
+            fz = kz[l, rows] * (pltpu.roll(v[r], 127, 1) - v[r])
+            down = jnp.where(bottom, back[r - 1] if r else 0.0, back[r])
+            total = (aa[l, rows] * v[r] + (fx - behind[r])) + ((flux[r] - down) + (fz - pltpu.roll(fz, 1, 1)))
+            finish(l, rows, v[r], total)
+            ahead.append(fx)
+        behind = ahead
+
+
+def clear_outside(s, refs, lo, hi):
+    zero = jnp.zeros((128, 128), jnp.float32)
+
     @pl.when(s == 0)
     def _():
-        for l in range(PAD):
-            store(l)
+        for ref in refs:
+            for l in range(lo, PAD):
+                ref[l] = zero
 
     @pl.when(s == NS - 1)
     def _():
-        for l in range(PAD + 4, EXT):
-            store(l)
-
-
-def fine_steps(states, count, widths, cond_refs, heat, s):
-    kx, ky, kz, bb = cond_refs
-    for turn in range(count):
-        a, b = turn % 2, (turn + 1) % 2
+        for ref in refs:
+            for l in range(PAD + 4, hi):
+                ref[l] = zero
+
+
+def fine_steps(states, widths, coefficients, heat, s):
+    for turn in range(4):
+        a, b = states[turn % 2], states[1 - turn % 2]
         for f in range(2):
             h = widths[f] - 1 - turn
 
-            def write(l, v, change):
-                states[b, f, l] = v + change + heat[l]
-
-            sweep(lambda l: states[a, f, l], write, kx, ky, kz, bb, PAD - h, PAD + 4 + h)
-
-        def store(l):
-            for f in range(2):
-                states[b, f, l] = jnp.zeros((128, 128), jnp.float32)
-
-        clear_outside(s, store)
-
-
-def first_kernel(flags, g, cond, source, ev, od, out, state, cnd, heat, kx, ky, kz, bb):
+            def finish(l, rows, v, stepped):
+                b[f, l, rows] = stepped + heat[l, rows]
+
+            sweep(lambda l, rows: a[f, l, rows], finish, coefficients, PAD - h, PAD + 4 + h)
+        if turn < 3:
+            h = max(widths) - 1 - turn
+            clear_outside(s, [b.at[0], b.at[1]], PAD - h, PAD + 4 + h)
+
+
+def first_kernel(flags, g, cond, source, ev, od, out, s0, s1, cnd, heat, *coefficients):
     s = flags[1]
     core = s % 2
     for l in range(4):
         for f in range(2):
-            state[0, f, PAD + l] = g[f, l]
+            s0[f, PAD + l] = g[f, l]
         cnd[PAD + l] = cond[l]
         heat[PAD + l] = source[l]
 
     def sides(left, right):
         for l in range(4):
             for f in range(2):
-                state[0, f, 1 + l] = left[f, l]
-                state[0, f, PAD + 4 + l] = right[f, l]
+                s0[f, 1 + l] = left[f, l]
+                s0[f, PAD + 4 + l] = right[f, l]
             cnd[1 + l] = left[2, l]
             cnd[PAD + 4 + l] = right[2, l]
             heat[1 + l] = left[3, l]
@@ -148,96 +174,87 @@
     def _():
         sides(ev, od)
 
-    def store(l):
-        zero = jnp.zeros((128, 128), jnp.float32)
-        for f in range(2):
-            state[0, f, l] = zero
-        cnd[l] = zero
-
-    clear_outside(s, store)
-    set_coefficients(cnd, kx, ky, kz, bb, 1, EXT - 2)
-    fine_steps(state, 4, (4, 4), (kx, ky, kz, bb), heat, s)
+    clear_outside(s, [s0.at[0], s0.at[1], cnd], 1, EXT - 1)
+    set_coefficients(cnd, *coefficients, 1, EXT - 2)
+    fine_steps((s0, s1), (4, 4), coefficients, heat, s)
     for f in range(2):
         for l in range(4):
-            out[f, l] = state[0, f, PAD + l]
-
-
-def second_kernel(flags, a, cond, source, ev, od, evc, odc, ev5, od5, e_out, w_out, state, cnd, heat, kx, ky, kz, bb, wide):
+            out[f, l] = s0[f, PAD + l]
+
+
+def second_kernel(
+    flags, a, cond, source, ev, od, evc, odc, ev5, chip, e_out, w_out, tiles, s0, s1, cnd, heat, *rest
+):
+    coefficients, wide = rest[:4], rest[4]
     t, s = flags[0], flags[1]
     core = s % 2
+    od_at = lambda i: od[128 * i : 128 * i + 128]
     for l in range(4):
         for f in range(2):
-            state[0, f, PAD + l] = a[f, l]
+            s0[f, PAD + l] = a[f, l]
         cnd[PAD + l] = cond[l]
         heat[PAD + l] = source[l]
-
-    def sides(left, right, leftc, rightc, left5, right5):
+    for l in range(8):
+        tiles[8 + l] = chip[l]
+
+    def sides(even, odd, even5, odd5):
         for l in range(4):
             for f in range(2):
-                state[0, f, 1 + l] = left[f, l]
-                state[0, f, PAD + 4 + l] = right[f, l]
-            cnd[1 + l] = leftc[2, l]
-            cnd[PAD + 4 + l] = rightc[2, l]
-            heat[1 + l] = leftc[3, l]
-            heat[PAD + 4 + l] = rightc[3, l]
-        state[0, 0, 0] = left5[0]
-        state[0, 0, EXT - 1] = right5[0]
-        cnd[0] = left5[1]
-        cnd[EXT - 1] = right5[1]
+                s0[f, even + l] = ev[f, l]
+                s0[f, odd + l] = od_at(4 * f + l)
+            cnd[even + l] = evc[2, l]
+            cnd[odd + l] = odc[2, l]
+            heat[even + l] = evc[3, l]
+            heat[odd + l] = odc[3, l]
+        s0[0, even5] = ev5[0:128]
+        s0[0, odd5] = od_at(8)
+        cnd[even5] = ev5[128:256]
+        cnd[odd5] = od_at(9)
+
+    def side_tiles(even, odd):
+        for l in range(8):
+            tiles[even + l] = ev5[256 + 24 * l : 280 + 24 * l]
+            tiles[odd + l] = od[1280 + 24 * l : 1304 + 24 * l]
 
     @pl.when(core == 0)
     def _():
-        sides(od, ev, odc, evc, od5, ev5)
+        sides(PAD + 4, 1, EXT - 1, 0)
+        side_tiles(16, 0)
 
     @pl.when(core == 1)
     def _():
-        sides(ev, od, evc, odc, ev5, od5)
-
-    def store(l):
-        zero = jnp.zeros((128, 128), jnp.float32)
-        for f in range(2):
-            state[0, f, l] = zero
-        cnd[l] = zero
-
-    clear_outside(s, store)
-    set_coefficients(cnd, kx, ky, kz, bb, 0, EXT - 1)
+        sides(1, PAD + 4, 0, EXT - 1)
+        side_tiles(0, 16)
+
+    clear_outside(s, [s0.at[0], s0.at[1], cnd], 0, EXT)
+    set_coefficients(cnd, *coefficients, 0, EXT - 1)
+    ratio = COARSE / FINE
     for f, h in ((0, 1), (1, 0)):
 
-        def keep(l, v, change):
-            wide[f, l] = v + (COARSE / FINE) * change
-
-        sweep(lambda l: state[0, f, l], keep, kx, ky, kz, bb, PAD - h, PAD + 4 + h)
-    fine_steps(state, 4, (5, 4), (kx, ky, kz, bb), heat, s)
+        def keep(l, rows, v, stepped):
+            wide[f, l, rows] = v + ratio * (stepped - v)
+
+        sweep(lambda l, rows: s0[f, l, rows], keep, coefficients, PAD - h, PAD + 4 + h)
+    fine_steps((s0, s1), (5, 4), coefficients, heat, s)
     for l in range(PAD - 1, PAD + 5):
-        wide[0, l] = state[0, 0, l] - wide[0, l]
-    for l in range(PAD, PAD + 4):
-        wide[1, l] = state[0, 1, l] - wide[1, l]
-
-    def clear(l):
-        wide[0, l] = jnp.zeros((128, 128), jnp.float32)
-
-    clear_outside(s, clear)
-    for l in range(4):
-        w_out[l] = wide[0, PAD + l]
-
-    def put(l, value):
-        for to in range(NT):
-            e_out[to, l] = value[8 * place_of(to) : 8 * place_of(to) + 8]
-
-    def finish(l, v, change):
-        wide[1, l] = v + (COARSE / FINE) * change + wide[1, l]
-
-    sweep(lambda l: wide[0, l], finish, kx, ky, kz, bb, PAD, PAD + 4)
+        wide[0, l] = s0[0, l] - wide[0, l]
+    clear_outside(s, [wide.at[0]], PAD - 1, PAD + 5)
 
     @pl.when(t != NT - 1)
     def _():
+        def finish(l, rows, v, stepped):
+            to = PLACE[rows.start // 8]
+            e_out[to, l - PAD] = v + ratio * (stepped - v) + (s0[1, l, rows] - wide[1, l, rows])
+
+        sweep(lambda l, rows: wide[0, l, rows], finish, coefficients, PAD, PAD + 4)
         for l in range(4):
-            put(l, wide[1, PAD + l])
+            w_out[l] = wide[0, PAD + l]
 
     @pl.when(t == NT - 1)
     def _():
         for l in range(4):
-            put(l, state[0, 0, PAD + l])
+            for r in range(16):
+                e_out[PLACE[r], l] = s0[0, PAD + l, rows_at(r)]
             w_out[l] = a[0, l]
 
 
@@ -425,36 +442,30 @@
     pack = jnp.concatenate([g, cond[None], source[None]])
     ev = even(pack)
     od = odd(pack)
-    fine_scratch = [
-        pltpu.VMEM((2, 2, EXT, 128, 128), jnp.float32),
-    ] + [pltpu.VMEM((EXT, 128, 128), jnp.float32)] * 6
+    layers = pltpu.VMEM((EXT, 128, 128), jnp.float32)
+    fine_scratch = [pltpu.VMEM((2, EXT, 128, 128), jnp.float32)] * 2 + [layers] * 6
     (a,) = call(first_kernel, [struct(2, 4, 128, 128)], fine_scratch, flags, g, cond, source, ev, od)
 
     start = 8 * place
     rows_of = lambda x: lax.dynamic_slice_in_dim(jnp.pad(x, ((0, 0), (8, 8), (0, 0))), start, 24, 1)
     mine, yours = rows_of(cond), rows_of(ev[2])
     chip = jnp.where(core == 0, jnp.concatenate([mine, yours]), jnp.concatenate([yours, mine]))
-    c_got = odd(chip)
-    c_swap = even(c_got)
-    tiles = jnp.where(
-        core == 0, jnp.concatenate([c_got, chip, c_swap]), jnp.concatenate([c_swap, chip, c_got])
-    )
 
     ev2 = even(a)
-    near = lambda x: jnp.where(core == 0, x[0], x[3])
     tail = lambda x: jnp.where(core == 0, x[0], x[3])
-    beyond = jnp.stack([tail(ev2[0]), tail(ev[2])])
-    od2 = odd(jnp.concatenate([a.reshape(8, 128, 128), beyond]))
     nearest = lambda x: jnp.where(core == 0, x[3], x[0])
-    ev5 = even(jnp.stack([nearest(od2[0:4]), nearest(od[2])]))
-    e, w = call(
+    chip_rows = chip.reshape(192, 128)
+    od2 = odd(jnp.concatenate([a.reshape(1024, 128), tail(ev2[0]), tail(ev[2]), chip_rows]))
+    ev5 = even(jnp.concatenate([nearest(od2[:512].reshape(4, 128, 128)), nearest(od[2]), od2[1280:]]))
+    e, w, tiles = call(
         second_kernel,
-        [struct(NT, 4, 8, 128), struct(4, 128, 128)],
+        [struct(NT, 4, 8, 128), struct(4, 128, 128), struct(24, 24, 128)],
         fine_scratch + [pltpu.VMEM((2, EXT, 128, 128), jnp.float32)],
-        flags, a, cond, source, ev2, od2[:8].reshape(2, 4, 128, 128), ev, od, ev5, od2[8:],
+        flags, a, cond, source, ev2, od2, ev, od, ev5, chip,
     )
     w_before = lax.ppermute(w, "tm", [(i, (i + 1) % NT) for i in range(NT)])
     own = lax.all_to_all(e, "tm", 0, 0)
+    own, w_before = lax.optimization_barrier((own, w_before))
     other = even(own)
 
     picks = [(2 * i - 1) % NT for i in range(8)]

time: 217 us -> 193 us (0.89)
  Pallas kernels: 39.7 us -> 23.4 us
  waiting for transfers between devices: 125 us -> 115 us
  starting transfers between devices: 24.6 us -> 27.7 us
    pallas_call x8, Pallas kernels: 39.7 us -> 23.4 us  [call(): pl.pallas_call(kernel, out_shape=outs, in_specs=specs, out_specs=[VMEM] *...]
    ppermute x8 -> x7, starting transfers between devices: 17.2 us -> 10.3 us  [odd(): return lax.ppermute(x, ('tm', 'space'), ODD)]
    ppermute x1, waiting for transfers between devices: 20 us -> 14 us  [body(): w_before = lax.ppermute(w, 'tm', [(i, (i + 1) % NT) for i in range(NT)])]
    all_to_all x1, starting transfers between devices: 3.57 us -> 9.47 us  [body(): own = lax.all_to_all(e, 'tm', 0, 0)]
    ppermute x5, starting transfers between devices: 1.29 us -> 5.3 us  [yodd(): return lax.ppermute(x, ('tm', 'space'), YODD)]
    ppermute x5, waiting for transfers between devices: 30.3 us -> 26.3 us  [yodd(): return lax.ppermute(x, ('tm', 'space'), YODD)]
    ppermute x8 -> x7, waiting for transfers between devices: 58.2 us -> 58.6 us  [odd(): return lax.ppermute(x, ('tm', 'space'), ODD)]
    ppermute x15 -> x14, waiting for transfers between devices: 16.1 us -> 16.4 us  [even(): return lax.ppermute(x, 'space', EVEN)]
  transfers between devices with their start and end apart: 30 -> 28, of which waited for: 28 -> 26; matrix products, arithmetic and copies ran while one was open for 0% -> 0% of each run, Pallas kernels for 0% -> 0%
where the time goes in v2:
time: 193 us
  waiting for transfers between devices  115 us (60%)
  starting transfers between devices  27.7 us (14%)
  Pallas kernels  23.4 us (12%)
  blocking collectives  22.4 us (12%)
  local copies, waits for them, and re-layouts  2.21 us (1%)
    ppermute x7, waiting for transfers between devices, odd(): return lax.ppermute(x, ('tm', 'space'), ODD)  58.6 us
    ppermute x5, waiting for transfers between devices, yodd(): return lax.ppermute(x, ('tm', 'space'), YODD)  26.3 us
    pallas_call x8, Pallas kernels, call(): pl.pallas_call(kernel, out_shape=outs, in_specs=specs, out_specs=[VMEM] *...  23.4 us
    all_to_all x1, blocking collectives, body(): back = lax.all_to_all(jnp.concatenate(parts), 'tm', 0, 0)  22.4 us
    ppermute x14, waiting for transfers between devices, even(): return lax.ppermute(x, 'space', EVEN)  16.4 us
    ppermute x1, waiting for transfers between devices, body(): w_before = lax.ppermute(w, 'tm', [(i, (i + 1) % NT) for i in range(NT)])  14 us
    ppermute x7, starting transfers between devices, odd(): return lax.ppermute(x, ('tm', 'space'), ODD)  10.3 us
    all_to_all x1, starting transfers between devices, body(): own = lax.all_to_all(e, 'tm', 0, 0)  9.47 us
  transfers between devices with their start and end apart: 28, of which 26 were waited for; matrix products, arithmetic and copies ran while one was open for 0% of the time, Pallas kernels for 0%

profile of v2, /device:TPU:16, one launch (start us, length us, event | category | flops | bytes accessed | tf_op | source)
XLA Modules:
  0.0 192.9 jit_solution(6606822638002775217)
XLA Ops:
  0.0 1.0 slice.123
  1.1 0.1 copy-done.2
  1.2 0.9 copy-done
  2.1 0.1 copy-done.1
  2.2 1.1 pad_maximum_fusion
  3.2 2.0 %collective-permute-start.1 = (f32[4,4,128,128]{3,2,1,0:T(8,128)}, f32[4,4,128,128]{3,2,1,0:T(8,128)S(1)}, u32[]{:S(2)}, u32[]{:S(2)}) collective-permute-start(f32[4,4,128,128]{3,2,1,0:T(8,128)} %pad_maximum_fusion), channel_id=1, source_target_pairs={{0,16},{1,2},{2,1},{3,4},{4,3},{5,6},{6,5},{7,8},{8,7},{9,10},{10,... | collective-permute-start | bytes 3145736 | tf_op jit(solution)/shard_map/ppermute | solution.py:56
  5.2 0.1 pad_add_fusion.flags.refs_0_
  5.3 16.0 %collective-permute-done.1.od.odc = f32[4,4,128,128]{3,2,1,0:T(8,128)S(1)} collective-permute-done((f32[4,4,128,128]{3,2,1,0:T(8,128)}, f32[4,4,128,128]{3,2,1,0:T(8,128)S(1)}, u32[]{:S(2)}, u32[]{:S(2)}) %collective-permute-start.1) | collective-permute-done | bytes 1048608 | tf_op jit(solution)/shard_map/ppermute | solution.py:56
  21.4 0.0 collective-permute-done.ev.evc
  21.4 3.9 %shard_map.46.a = f32[2,4,128,128]{3,2,1,0:T(8,128)S(1)} custom-call(s32[4]{0:T(128)S(1)} %pad_add_fusion.flags.refs_0_, f32[2,4,128,128]{3,2,1,0:T(8,128)S(1)} %pad_maximum_fusion.2.g, f32[4,128,128]{2,1,0:T(8,128)S(1)} %copy-done, f32[4,128,128]{2,1,0:T(8,128)S(1)} %copy-done.1, f32[4,4,128,128]{3,2,1,0:T(8,128)S(1)} %collective-permute-done.ev.evc, ...), custom_call_target="tpu_custom_call" | custom-call | tf_op jit(solution)/shard_map/pallas_call | solution.py:414
  25.3 0.1 collective-permute-start.2
  25.5 1.8 collective-permute-done.2.ev
  27.3 0.1 pad_maximum_fusion.1
  27.4 2.0 %collective-permute-start.3 = (f32[1472,128]{1,0:T(8,128)S(1)}, f32[1472,128]{1,0:T(8,128)S(1)}, u32[]{:S(2)}, u32[]{:S(2)}) collective-permute-start(f32[1472,128]{1,0:T(8,128)S(1)} %pad_maximum_fusion.1), channel_id=1, source_target_pairs={{0,16},{1,2},{2,1},{3,4},{4,3},{5,6},{6,5},{7,8},{8,7},{9,10},{10,... | collective-permute-start | bytes 2261000 | tf_op jit(solution)/shard_map/ppermute | solution.py:56
  29.4 12.8 %collective-permute-done.3.od = f32[1472,128]{1,0:T(8,128)S(1)} collective-permute-done((f32[1472,128]{1,0:T(8,128)S(1)}, f32[1472,128]{1,0:T(8,128)S(1)}, u32[]{:S(2)}, u32[]{:S(2)}) %collective-permute-start.3) | collective-permute-done | bytes 753696 | tf_op jit(solution)/shard_map/ppermute | solution.py:56
  42.3 0.1 collective-permute-start.4
  42.4 1.5 collective-permute-done.4.ev5
  43.9 5.8 %shard_map.47 = (f32[16,4,8,128]{3,2,1,0:T(8,128)}, f32[4,128,128]{2,1,0:T(8,128)S(1)}, f32[24,24,128]{2,1,0:T(8,128)S(1)}) custom-call(s32[4]{0:T(128)S(1)} %pad_add_fusion.flags.refs_0_, f32[2,4,128,128]{3,2,1,0:T(8,128)S(1)} %shard_map.46.a, f32[4,128,128]{2,1,0:T(8,128)S(1)} %copy-done, f32[4,128,128]{2,1,0:T(8,128)S(1)} %copy-done.1, ...), custom_call_target="tpu_custom_call" | custom-call | tf_op jit(solution)/shard_map/pallas_call | solution.py:414
  49.6 9.5 %all-to-all-start = ((f32[16,4,8,128]{3,2,1,0:T(8,128)}), f32[16,4,8,128]{3,2,1,0:T(8,128)S(1)}, u32[]{:S(2)}, u32[]{:S(2)}) async-start(f32[16,4,8,128]{3,2,1,0:T(8,128)} %get-tuple-element.23), calls=%async_computation | async-start | bytes 524288 | tf_op jit(solution)/shard_map/all_to_all | solution.py:467
  59.1 1.9 collective-permute-start.5
  61.0 14.0 %collective-permute-done.5.w = f32[4,128,128]{2,1,0:T(8,128)S(1)} collective-permute-done((f32[4,128,128]{2,1,0:T(8,128)S(1)}, f32[4,128,128]{2,1,0:T(8,128)S(1)}, u32[]{:S(2)}, u32[]{:S(2)}) %collective-permute-start.5) | collective-permute-done | bytes 262176 | tf_op jit(solution)/shard_map/ppermute | solution.py:466
  75.1 1.4 collective-permute-start.7
  76.5 5.9 %collective-permute-done.7.xg = f32[8,2,8,128]{3,2,1,0:T(8,128)S(1)} collective-permute-done((f32[8,2,8,128]{3,2,1,0:T(8,128)S(1)}, f32[8,2,8,128]{3,2,1,0:T(8,128)S(1)}, u32[]{:S(2)}, u32[]{:S(2)}) %collective-permute-start.7) | collective-permute-done | bytes 65568 | tf_op jit(solution)/shard_map/ppermute | solution.py:56
  82.5 0.5 collective-permute-start.6
  83.0 0.7 collective-permute-done.8.xs
  83.8 0.4 collective-permute-done.6.other
  84.3 1.5 collective-permute-start.9
  85.8 7.0 %collective-permute-done.9.yg = f32[8,12,8,128]{3,2,1,0:T(8,128)S(1)} collective-permute-done((f32[8,12,8,128]{3,2,1,0:T(8,128)S(1)}, f32[8,12,8,128]{3,2,1,0:T(8,128)S(1)}, u32[]{:S(2)}, u32[]{:S(2)}) %collective-permute-start.9) | collective-permute-done | bytes 393248 | tf_op jit(solution)/shard_map/ppermute | solution.py:60
  92.8 1.7 collective-permute-done.10.ys
  94.5 3.1 %shard_map.48 = (f32[16,8,8,128]{3,2,1,0:T(8,128)S(1)}, f32[8,8,8,128]{3,2,1,0:T(8,128)S(1)}, f32[4,4,8,128]{3,2,1,0:T(8,128)S(1)}) custom-call(s32[4]{0:T(128)S(1)} %pad_add_fusion.flags.refs_0_, f32[24,24,128]{2,1,0:T(8,128)S(1)} %get-tuple-element.22.cond.refs_1_, f32[16,4,8,128]{3,2,1,0:T(8,128)S(1)} %all-to-all-done.own, ...), custom_call_target="tpu_custom_call" | custom-call | tf_op jit(solution)/shard_map/pallas_call | solution.py:414
  97.6 1.5 collective-permute-start.11
  99.1 5.9 %collective-permute-done.11.xg = f32[4,4,8,128]{3,2,1,0:T(8,128)S(1)} collective-permute-done((f32[4,4,8,128]{3,2,1,0:T(8,128)S(1)}, f32[4,4,8,128]{3,2,1,0:T(8,128)S(1)}, u32[]{:S(2)}, u32[]{:S(2)}) %collective-permute-start.11) | collective-permute-done | bytes 65568 | tf_op jit(solution)/shard_map/ppermute | solution.py:56
  105.0 1.2 collective-permute-done.12.xs
  106.3 1.3 collective-permute-start.13
  107.6 5.8 %collective-permute-done.13.yg = f32[4,16,8,128]{3,2,1,0:T(8,128)S(1)} collective-permute-done((f32[4,16,8,128]{3,2,1,0:T(8,128)S(1)}, f32[4,16,8,128]{3,2,1,0:T(8,128)S(1)}, u32[]{:S(2)}, u32[]{:S(2)}) %collective-permute-start.13) | collective-permute-done | bytes 262176 | tf_op jit(solution)/shard_map/ppermute | solution.py:60
  113.4 0.0 collective-permute-start.14
  113.4 1.5 collective-permute-done.14.ys
  114.9 3.1 %shard_map.49 = (f32[12,8,8,128]{3,2,1,0:T(8,128)S(1)}, f32[12,4,8,128]{3,2,1,0:T(8,128)S(1)}, f32[8,8,128]{2,1,0:T(8,128)S(1)}, f32[4,2,4,8,128]{4,3,2,1,0:T(8,128)S(1)}) custom-call(s32[4]{0:T(128)S(1)} %pad_add_fusion.flags.refs_0_, f32[24,24,128]{2,1,0:T(8,128)S(1)} %get-tuple-element.22.cond.refs_1_, f32[16,8,8,128]{3,2,1,0:T(8,128)S(1)} %get-tuple-element.26.p, ...), custom_call_target="tpu_custom_call" | custom-call | tf_op jit(solution)/shard_map/pallas_call | solution.py:414
  118.0 1.3 collective-permute-start.15
  119.3 5.7 %collective-permute-done.15 = f32[1,8,8,128]{3,2,1,0:T(8,128)S(1)} collective-permute-done((f32[1,8,8,128]{3,2,1,0:T(8,128)S(1)}, f32[1,8,8,128]{3,2,1,0:T(8,128)S(1)}, u32[]{:S(2)}, u32[]{:S(2)}) %collective-permute-start.15) | collective-permute-done | bytes 32800 | tf_op jit(solution)/shard_map/ppermute | solution.py:56
  125.1 1.2 collective-permute-done.16
  126.3 1.1 collective-permute-start.17
  127.4 4.2 %collective-permute-done.17 = f32[1,24,8,128]{3,2,1,0:T(8,128)S(1)} collective-permute-done((f32[1,24,8,128]{3,2,1,0:T(8,128)S(1)}, f32[1,24,8,128]{3,2,1,0:T(8,128)S(1)}, u32[]{:S(2)}, u32[]{:S(2)}) %collective-permute-start.17) | collective-permute-done | bytes 98336 | tf_op jit(solution)/shard_map/ppermute | solution.py:60
  131.6 0.0 collective-permute-start.18
  131.6 1.3 collective-permute-done.18
  132.9 2.2 %shard_map.50 = (f32[8,8,128]{2,1,0:T(8,128)S(1)}, f32[4,2,4,8,128]{4,3,2,1,0:T(8,128)S(1)}) custom-call(s32[4]{0:T(128)S(1)} %pad_add_fusion.flags.refs_0_, f32[24,24,128]{2,1,0:T(8,128)S(1)} %get-tuple-element.22.cond.refs_1_, f32[8,8,128]{2,1,0:T(8,128)S(1)} %get-tuple-element.30.refs_2_, f32[12,8,8,128]{3,2,1,0:T(8,128)S(1)} %get-tuple-element.31.refs_3_, ...), custom_call_target="tpu_custom_call" | custom-call | tf_op jit(solution)/shard_map/pallas_call | solution.py:414
  135.1 1.1 collective-permute-start.19
  136.2 6.0 %collective-permute-done.19 = f32[1,8,8,128]{3,2,1,0:T(8,128)S(1)} collective-permute-done((f32[1,8,8,128]{3,2,1,0:T(8,128)S(1)}, f32[1,8,8,128]{3,2,1,0:T(8,128)S(1)}, u32[]{:S(2)}, u32[]{:S(2)}) %collective-permute-start.19) | collective-permute-done | bytes 32800 | tf_op jit(solution)/shard_map/ppermute | solution.py:56
  142.3 1.2 collective-permute-done.20
  143.5 0.8 collective-permute-start.21
  144.3 4.6 %collective-permute-done.21 = f32[1,24,8,128]{3,2,1,0:T(8,128)S(1)} collective-permute-done((f32[1,24,8,128]{3,2,1,0:T(8,128)S(1)}, f32[1,24,8,128]{3,2,1,0:T(8,128)S(1)}, u32[]{:S(2)}, u32[]{:S(2)}) %collective-permute-start.21) | collective-permute-done | bytes 98336 | tf_op jit(solution)/shard_map/ppermute | solution.py:60
  148.9 0.0 collective-permute-start.22
  148.9 1.3 collective-permute-done.22
  150.2 2.0 %shard_map.51 = (f32[8,8,128]{2,1,0:T(8,128)S(1)}, f32[4,2,4,8,128]{4,3,2,1,0:T(8,128)S(1)}) custom-call(s32[4]{0:T(128)S(1)} %pad_add_fusion.flags.refs_0_, f32[24,24,128]{2,1,0:T(8,128)S(1)} %get-tuple-element.22.cond.refs_1_, f32[8,8,128]{2,1,0:T(8,128)S(1)} %get-tuple-element.34.refs_2_, f32[12,8,8,128]{3,2,1,0:T(8,128)S(1)} %get-tuple-element.31.refs_3_, ...), custom_call_target="tpu_custom_call" | custom-call | tf_op jit(solution)/shard_map/pallas_call | solution.py:414
  152.1 0.9 collective-permute-start.23
  153.1 6.1 %collective-permute-done.23 = f32[1,8,8,128]{3,2,1,0:T(8,128)S(1)} collective-permute-done((f32[1,8,8,128]{3,2,1,0:T(8,128)S(1)}, f32[1,8,8,128]{3,2,1,0:T(8,128)S(1)}, u32[]{:S(2)}, u32[]{:S(2)}) %collective-permute-start.23) | collective-permute-done | bytes 32800 | tf_op jit(solution)/shard_map/ppermute | solution.py:56
  159.2 1.2 collective-permute-done.24
  160.4 0.6 collective-permute-start.25
  161.0 4.8 %collective-permute-done.25 = f32[1,24,8,128]{3,2,1,0:T(8,128)S(1)} collective-permute-done((f32[1,24,8,128]{3,2,1,0:T(8,128)S(1)}, f32[1,24,8,128]{3,2,1,0:T(8,128)S(1)}, u32[]{:S(2)}, u32[]{:S(2)}) %collective-permute-start.25) | collective-permute-done | bytes 98336 | tf_op jit(solution)/shard_map/ppermute | solution.py:60
  165.8 0.0 collective-permute-start.26
  165.8 1.3 collective-permute-done.26
  167.1 2.6 %shard_map.52 = (f32[8,8,128]{2,1,0:T(8,128)}, f32[4,2,4,8,128]{4,3,2,1,0:T(8,128)S(1)}) custom-call(s32[4]{0:T(128)S(1)} %pad_add_fusion.flags.refs_0_, f32[24,24,128]{2,1,0:T(8,128)S(1)} %get-tuple-element.22.cond.refs_1_, f32[8,8,128]{2,1,0:T(8,128)S(1)} %get-tuple-element.36.refs_2_, f32[12,8,8,128]{3,2,1,0:T(8,128)S(1)} %get-tuple-element.31.refs_3_, ...), custom_call_target="tpu_custom_call" | custom-call | tf_op jit(solution)/shard_map/pallas_call | solution.py:414
  169.7 22.4 %all_to_all.10.got = f32[16,2,4,8,128]{4,3,2,1,0:T(8,128)S(1)} all-to-all(f32[16,2,4,8,128]{4,3,2,1,0:T(8,128)S(1)} %pad_maximum_fusion.3), channel_id=1, replica_groups=mesh['tm'=16,'space'=16] {'tm'}, dimensions={0} | all-to-all | bytes 1048576 | tf_op jit(solution)/shard_map/all_to_all | solution.py:501
  192.1 0.8 shard_map.53
  (53 shorter events, 0.5 us)
Async XLA Ops:
  0.0 1.1 copy-start.2
  1.1 0.9 copy-start
  1.1 1.0 copy-start.1
  3.2 18.2 %collective-permute-start.1 = (f32[4,4,128,128]{3,2,1,0:T(8,128)}, f32[4,4,128,128]{3,2,1,0:T(8,128)S(1)}, u32[]{:S(2)}, u32[]{:S(2)}) collective-permute-start(f32[4,4,128,128]{3,2,1,0:T(8,128)} %pad_maximum_fusion), channel_id=1, source_target_pairs={{0,16},{1,2},{2,1},{3,4},{4,3},{5,6},{6,5},{7,8},{8,7},{9,10},{10,... | collective-permute-start | bytes 3145736 | tf_op jit(solution)/shard_map/ppermute | solution.py:56
  5.2 16.2 %collective-permute-start = (f32[4,4,128,128]{3,2,1,0:T(8,128)}, f32[4,4,128,128]{3,2,1,0:T(8,128)S(1)}, u32[]{:S(2)}, u32[]{:S(2)}) collective-permute-start(f32[4,4,128,128]{3,2,1,0:T(8,128)} %pad_maximum_fusion), channel_id=1, source_target_pairs={{0,1},{1,0},{2,3},{3,2},{4,5},{5,4},{6,7},{7,6},{8,9},{9,8},{10,11... | collective-permute-start | bytes 3145736 | tf_op jit(solution)/shard_map/ppermute | solution.py:52
  25.3 2.0 %collective-permute-start.2 = (f32[2,4,128,128]{3,2,1,0:T(8,128)S(1)}, f32[2,4,128,128]{3,2,1,0:T(8,128)S(1)}, u32[]{:S(2)}, u32[]{:S(2)}) collective-permute-start(f32[2,4,128,128]{3,2,1,0:T(8,128)S(1)} %shard_map.46.a), channel_id=1, source_target_pairs={{0,1},{1,0},{2,3},{3,2},{4,5},{5,4},{6,7},{7,6},{8,9},{9,8},{10,11... | collective-permute-start | bytes 1572872 | tf_op jit(solution)/shard_map/ppermute | solution.py:52
  27.4 14.9 %collective-permute-start.3 = (f32[1472,128]{1,0:T(8,128)S(1)}, f32[1472,128]{1,0:T(8,128)S(1)}, u32[]{:S(2)}, u32[]{:S(2)}) collective-permute-start(f32[1472,128]{1,0:T(8,128)S(1)} %pad_maximum_fusion.1), channel_id=1, source_target_pairs={{0,16},{1,2},{2,1},{3,4},{4,3},{5,6},{6,5},{7,8},{8,7},{9,10},{10,... | collective-permute-start | bytes 2261000 | tf_op jit(solution)/shard_map/ppermute | solution.py:56
  42.3 1.6 collective-permute-start.4
  49.6 25.4 %all-to-all-start = ((f32[16,4,8,128]{3,2,1,0:T(8,128)}), f32[16,4,8,128]{3,2,1,0:T(8,128)S(1)}, u32[]{:S(2)}, u32[]{:S(2)}) async-start(f32[16,4,8,128]{3,2,1,0:T(8,128)} %get-tuple-element.23), calls=%async_computation | async-start | bytes 524288 | tf_op jit(solution)/shard_map/all_to_all | solution.py:467
  59.1 15.9 %collective-permute-start.5 = (f32[4,128,128]{2,1,0:T(8,128)S(1)}, f32[4,128,128]{2,1,0:T(8,128)S(1)}, u32[]{:S(2)}, u32[]{:S(2)}) collective-permute-start(f32[4,128,128]{2,1,0:T(8,128)S(1)} %get-tuple-element.24), channel_id=1, source_target_pairs={{0,16},{16,32},{32,48},{48,64},{64,80},{80,96},{96,112},{112,128},... | collective-permute-start | bytes 786440 | tf_op jit(solution)/shard_map/ppermute | solution.py:466
  75.1 7.4 %collective-permute-start.7 = (f32[8,2,8,128]{3,2,1,0:T(8,128)S(1)}, f32[8,2,8,128]{3,2,1,0:T(8,128)S(1)}, u32[]{:S(2)}, u32[]{:S(2)}) collective-permute-start(f32[8,2,8,128]{3,2,1,0:T(8,128)S(1)} %slice_select_fusion), channel_id=1, source_target_pairs={{0,16},{1,2},{2,1},{3,4},{4,3},{5,6},{6,5},{7,8},{8,7},{9,10},{10,... | collective-permute-start | bytes 196616 | tf_op jit(solution)/shard_map/ppermute | solution.py:56
  82.5 1.3 collective-permute-start.8
  82.5 1.7 collective-permute-start.6
  84.3 8.5 %collective-permute-start.9 = (f32[8,12,8,128]{3,2,1,0:T(8,128)S(1)}, f32[8,12,8,128]{3,2,1,0:T(8,128)S(1)}, u32[]{:S(2)}, u32[]{:S(2)}) collective-permute-start(f32[8,12,8,128]{3,2,1,0:T(8,128)S(1)} %pad_maximum_fusion.4), channel_id=1, source_target_pairs={{0,225},{1,16},{2,227},{3,18},{4,229},{5,20},{6,231},{7,22},{8,233... | collective-permute-start | bytes 1179656 | tf_op jit(solution)/shard_map/ppermute | solution.py:60
  92.8 1.7 collective-permute-start.10
  97.6 7.4 %collective-permute-start.11 = (f32[4,4,8,128]{3,2,1,0:T(8,128)S(1)}, f32[4,4,8,128]{3,2,1,0:T(8,128)S(1)}, u32[]{:S(2)}, u32[]{:S(2)}) collective-permute-start(f32[4,4,8,128]{3,2,1,0:T(8,128)S(1)} %get-tuple-element.28), channel_id=1, source_target_pairs={{0,16},{1,2},{2,1},{3,4},{4,3},{5,6},{6,5},{7,8},{8,7},{9,10},{10,... | collective-permute-start | bytes 196616 | tf_op jit(solution)/shard_map/ppermute | solution.py:56
  105.0 1.3 collective-permute-start.12
  106.3 7.1 %collective-permute-start.13 = (f32[4,16,8,128]{3,2,1,0:T(8,128)S(1)}, f32[4,16,8,128]{3,2,1,0:T(8,128)S(1)}, u32[]{:S(2)}, u32[]{:S(2)}) collective-permute-start(f32[4,16,8,128]{3,2,1,0:T(8,128)S(1)} %pad_maximum_fusion.5), channel_id=1, source_target_pairs={{0,225},{1,16},{2,227},{3,18},{4,229},{5,20},{6,231},{7,22},{8,233... | collective-permute-start | bytes 786440 | tf_op jit(solution)/shard_map/ppermute | solution.py:60
  113.4 1.5 collective-permute-start.14
  118.0 7.0 %collective-permute-start.15 = (f32[1,8,8,128]{3,2,1,0:T(8,128)S(1)}, f32[1,8,8,128]{3,2,1,0:T(8,128)S(1)}, u32[]{:S(2)}, u32[]{:S(2)}) collective-permute-start(f32[1,8,8,128]{3,2,1,0:T(8,128)S(1)} %bitcast.43), channel_id=1, source_target_pairs={{0,16},{1,2},{2,1},{3,4},{4,3},{5,6},{6,5},{7,8},{8,7},{9,10},{10,... | collective-permute-start | bytes 98312 | tf_op jit(solution)/shard_map/ppermute | solution.py:56
  125.1 1.2 collective-permute-start.16
  126.3 5.3 %collective-permute-start.17 = (f32[1,24,8,128]{3,2,1,0:T(8,128)S(1)}, f32[1,24,8,128]{3,2,1,0:T(8,128)S(1)}, u32[]{:S(2)}, u32[]{:S(2)}) collective-permute-start(f32[1,24,8,128]{3,2,1,0:T(8,128)S(1)} %pad_maximum_fusion.7), channel_id=1, source_target_pairs={{0,225},{1,16},{2,227},{3,18},{4,229},{5,20},{6,231},{7,22},{8,233... | collective-permute-start | bytes 294920 | tf_op jit(solution)/shard_map/ppermute | solution.py:60
  131.6 1.3 collective-permute-start.18
  135.1 7.1 %collective-permute-start.19 = (f32[1,8,8,128]{3,2,1,0:T(8,128)S(1)}, f32[1,8,8,128]{3,2,1,0:T(8,128)S(1)}, u32[]{:S(2)}, u32[]{:S(2)}) collective-permute-start(f32[1,8,8,128]{3,2,1,0:T(8,128)S(1)} %bitcast.45), channel_id=1, source_target_pairs={{0,16},{1,2},{2,1},{3,4},{4,3},{5,6},{6,5},{7,8},{8,7},{9,10},{10,... | collective-permute-start | bytes 98312 | tf_op jit(solution)/shard_map/ppermute | solution.py:56
  142.3 1.2 collective-permute-start.20
  143.5 5.3 %collective-permute-start.21 = (f32[1,24,8,128]{3,2,1,0:T(8,128)S(1)}, f32[1,24,8,128]{3,2,1,0:T(8,128)S(1)}, u32[]{:S(2)}, u32[]{:S(2)}) collective-permute-start(f32[1,24,8,128]{3,2,1,0:T(8,128)S(1)} %pad_maximum_fusion.8), channel_id=1, source_target_pairs={{0,225},{1,16},{2,227},{3,18},{4,229},{5,20},{6,231},{7,22},{8,233... | collective-permute-start | bytes 294920 | tf_op jit(solution)/shard_map/ppermute | solution.py:60
  148.9 1.3 collective-permute-start.22
  152.1 7.0 %collective-permute-start.23 = (f32[1,8,8,128]{3,2,1,0:T(8,128)S(1)}, f32[1,8,8,128]{3,2,1,0:T(8,128)S(1)}, u32[]{:S(2)}, u32[]{:S(2)}) collective-permute-start(f32[1,8,8,128]{3,2,1,0:T(8,128)S(1)} %bitcast.41), channel_id=1, source_target_pairs={{0,16},{1,2},{2,1},{3,4},{4,3},{5,6},{6,5},{7,8},{8,7},{9,10},{10,... | collective-permute-start | bytes 98312 | tf_op jit(solution)/shard_map/ppermute | solution.py:56
  159.2 1.2 collective-permute-start.24
  160.4 5.3 %collective-permute-start.25 = (f32[1,24,8,128]{3,2,1,0:T(8,128)S(1)}, f32[1,24,8,128]{3,2,1,0:T(8,128)S(1)}, u32[]{:S(2)}, u32[]{:S(2)}) collective-permute-start(f32[1,24,8,128]{3,2,1,0:T(8,128)S(1)} %pad_maximum_fusion.9), channel_id=1, source_target_pairs={{0,225},{1,16},{2,227},{3,18},{4,229},{5,20},{6,231},{7,22},{8,233... | collective-permute-start | bytes 294920 | tf_op jit(solution)/shard_map/ppermute | solution.py:60
  165.8 1.3 collective-permute-start.26

commit v3 on v2

--- a/solution.py
+++ b/solution.py
@@ -1,3 +1,5 @@
+import functools
+
 import jax
 import jax.numpy as jnp
 from jax import lax
@@ -147,14 +149,28 @@
             clear_outside(s, [b.at[0], b.at[1]], PAD - h, PAD + 4 + h)
 
 
-def first_kernel(flags, g, cond, source, ev, od, out, s0, s1, cnd, heat, *coefficients):
+def pack_kernel(flags, initial, guess, cond, source, out):
+    @pl.when(flags[0] == NT - 1)
+    def _():
+        out[0] = initial[...]
+
+    @pl.when(flags[0] != NT - 1)
+    def _():
+        out[0] = guess[0]
+
+    out[1] = guess[1]
+    out[2] = cond[...]
+    out[3] = source[...]
+
+
+def first_kernel(flags, pack, ev, od, out, s0, s1, cnd, heat, *coefficients):
     s = flags[1]
     core = s % 2
     for l in range(4):
         for f in range(2):
-            s0[f, PAD + l] = g[f, l]
-        cnd[PAD + l] = cond[l]
-        heat[PAD + l] = source[l]
+            s0[f, PAD + l] = pack[f, l]
+        cnd[PAD + l] = pack[2, l]
+        heat[PAD + l] = pack[3, l]
 
     def sides(left, right):
         for l in range(4):
@@ -289,96 +305,143 @@
     return mask[inner] * (mid + change)
 
 
-def store_coefficients(coefficients, refs):
-    for value, ref in zip(coefficients, refs):
+HALOS = (6, 4, 2)
+STARTS = (0, 6, 10, 12)
+Y_STARTS = (0, 20, 28, 31)
+
+
+def half(core, value):
+    return jnp.where(core == 0, value[0:4], value[4:8])
+
+
+def slot(j):
+    return (j - 1) % NT
+
+
+def chips_kernel(flags, own, other, chip, send):
+    def run(first, last, side):
+        for j in range(NT):
+            chip[j, 0:4] = first[slot(j)]
+            chip[j, 4:8] = last[slot(j)]
+        for q in range(4):
+            for i, h in enumerate(HALOS):
+                a, b = STARTS[i], STARTS[i] + h
+                send[q, a:b] = chip[4 * q + i, side(h)]
+
+    @pl.when(flags[1] % 2 == 0)
+    def _():
+        run(own, other, lambda h: slice(0, h))
+
+    @pl.when(flags[1] % 2 == 1)
+    def _():
+        run(other, own, lambda h: slice(8 - h, 8))
+
+
+def rows_kernel(flags, chip, got, swap, send):
+    def run(left, right, upward):
+        for q in range(4):
+            for i, h in enumerate(HALOS):
+                rows = 8 >> i
+                pick = slice(8 - rows, 8) if upward else slice(0, rows)
+                a = STARTS[i]
+
+                def layer(l):
+                    if l < h:
+                        return left[q, a + l, pick]
+                    if l < h + 8:
+                        return chip[4 * q + i, l - h, pick]
+                    return right[q, a + l - h - 8, pick]
+
+                per = 8 // rows
+                for l in range(8 + 2 * h):
+                    k = l % per
+                    send[q, Y_STARTS[i] + l // per, rows * k : rows * k + rows] = layer(l)
+
+    @pl.when(flags[1] % 2 == 0)
+    def _():
+        run(got, swap, False)
+
+    @pl.when(flags[1] % 2 == 1)
+    def _():
+        run(swap, got, True)
+
+
+def quads_kernel(flags, cond, chip, xg, xs, yg, ys, p_out, zp_out, ends, last, done, b0, b1, b2, *coef):
+    core = flags[1] % 2
+    for value, ref in zip(region(flags, cond, 6), coef):
         ref[...] = value
-
-
-def gathered(core, own, x_got, x_swap, y_got, y_swap, buf, halo):
-    rows = pl.ds(8, 8)
-    buf[halo : halo + 8, 8:16] = own
-
-    def put(left, right, below, above):
-        buf[:halo, 8:16] = left
-        buf[halo + 8 :, 8:16] = right
-        buf[:, 0:8] = below
-        buf[:, 16:24] = above
-
-    @pl.when(core == 0)
-    def _():
-        put(x_got(), x_swap(), y_got(), y_swap())
-
-    @pl.when(core == 1)
-    def _():
-        put(x_swap(), x_got(), y_swap(), y_got())
-
-
-def pairs_kernel(flags, cond, own, other, xg, xs, yg, ys, p_out, ap_out, send, buf, *coef):
-    core = flags[1] % 2
-    store_coefficients(region(flags, cond, 2), coef)
-
-    def tile(j):
-        k = (j - 1) % NT
-        mine, yours = own[k], other[k]
-        first = jnp.where(core == 0, mine, yours)
-        last = jnp.where(core == 0, yours, mine)
-        return jnp.concatenate([first, last], 0)
-
-    for i in range(8):
-        gathered(core, tile(2 * i), lambda: xg[i], lambda: xs[i], lambda: yg[i], lambda: ys[i], buf, 2)
-        c = tuple(r[...] for r in coef)
-        one = coarse_step(buf[...] * c[0], c, 2, 2)
-        two = coarse_step(one, c, 2, 1)
-        ap_out[i] = one[1:9, 8:16]
-        p_out[2 * i] = tile(2 * i)
-        p_out[2 * i + 1] = tile(2 * i + 1) + two[:, 8:16]
+    b1[...] = jnp.zeros((16, 24, 128), jnp.float32)
+    b2[...] = jnp.zeros((12, 24, 128), jnp.float32)
+    c = tuple(r[...] for r in coef)
+    zero = jnp.zeros((4, 8, 128), jnp.float32)
     for q in range(4):
+
+        def fill(left, right, below, above):
+            for i, (h, buf) in enumerate(zip(HALOS, (b0, b1, b2))):
+                a, rows = STARTS[i], 8 >> i
+                buf[h : h + 8, 8:16] = chip[4 * q + i]
+                buf[0:h, 8:16] = left[q, a : a + h]
+                buf[h + 8 :, 8:16] = right[q, a : a + h]
+                per = 8 // rows
+                for l in range(8 + 2 * h):
+                    k = rows * (l % per)
+                    at = Y_STARTS[i] + l // per
+                    buf[l, 8 - rows : 8] = below[q, at, k : k + rows]
+                    buf[l, 16 : 16 + rows] = above[q, at, k : k + rows]
 
         @pl.when(core == 0)
         def _():
-            send[q] = p_out[4 * q + 1, 0:4]
+            fill(xg, xs, yg, ys)
 
         @pl.when(core == 1)
         def _():
-            send[q] = p_out[4 * q + 1, 4:8]
-
-
-def half(core, value):
-    return jnp.where(core == 0, value[0:4], value[4:8])
-
-
-def quads_kernel(flags, cond, p, ap, xg, xs, yg, ys, p_out, zp_out, last, done, buf, *coef):
+            fill(xs, xg, ys, yg)
+
+        p = b0[...] * c[0]
+        values, partial = [chip[4 * q]], [zero]
+        for i in range(3):
+            h = HALOS[i]
+            one = coarse_step(p, c, 6, h)
+            two = coarse_step(one, c, 6, h - 1)
+            partial.append(half(core, one[h - 1 : h + 7, 8:16]))
+            if i < 2:
+                p = two + (b1, b2)[i][...] * c[0][2 * i + 2 : 18 - 2 * i]
+                values.append(p[h - 2 : h + 6, 8:16])
+            else:
+                values.append(two[:, 8:16] + chip[4 * q + 3])
+        for i in range(4):
+            if q == 0:
+                done[i, 0] = partial[i]
+                done[i, 1] = half(core, values[i])
+            else:
+                p_out[4 * q - 4 + i] = half(core, values[i])
+                zp_out[4 * q - 4 + i] = partial[i]
+        if q == 0:
+            last[...] = values[3]
+        else:
+            ends[q - 1] = values[3]
+
+
+def chain_kernel(q, flags, cond, c_in, p, zp, ends, xg, xs, yg, ys, last, done, buf, *coef):
     core = flags[1] % 2
-    store_coefficients(region(flags, cond, 4), coef)
-    zero = jnp.zeros((4, 8, 128), jnp.float32)
-    for q in range(4):
-        j = 4 * q
-        gathered(core, p[j + 1], lambda: xg[q], lambda: xs[q], lambda: yg[q], lambda: ys[q], buf, 4)
-        c = tuple(r[...] for r in coef)
-        v = buf[...] * c[0]
-        powers = []
-        for turn in range(4):
-            v = coarse_step(v, c, 4, 4 - turn)
-            powers.append(v[3 - turn : 11 - turn, 8:16])
-        second = p[j + 2] + powers[1]
-        third = p[j + 3] + powers[3]
-        partial = [zero, half(core, ap[2 * q]), half(core, powers[0]), half(core, ap[2 * q + 1] + powers[2])]
-        ends = [p[j], p[j + 1], second, third]
-        if q == 0:
-            last[...] = third
-            for i in range(4):
-                done[i, 0] = partial[i]
-                done[i, 1] = half(core, ends[i])
-        else:
-            for i in range(4):
-                p_out[4 * q - 4 + i] = ends[i]
-                zp_out[4 * q - 4 + i] = partial[i]
-
-
-def chain_kernel(q, flags, cond, c_in, p, zp, xg, xs, yg, ys, last, done, buf, *coef):
-    core = flags[1] % 2
-    store_coefficients(region(flags, cond, 8), coef)
-    gathered(core, c_in[...], lambda: xg[...], lambda: xs[...], lambda: yg[...], lambda: ys[...], buf, 8)
+    for value, ref in zip(region(flags, cond, 8), coef):
+        ref[...] = value
+    buf[8:16, 8:16] = c_in[...]
+
+    def put(left, right, below, above):
+        buf[0:8, 8:16] = left[...]
+        buf[16:24, 8:16] = right[...]
+        buf[:, 0:8] = below[...]
+        buf[:, 16:24] = above[...]
+
+    @pl.when(core == 0)
+    def _():
+        put(xg, xs, yg, ys)
+
+    @pl.when(core == 1)
+    def _():
+        put(xs, xg, ys, yg)
+
     c = tuple(r[...] for r in coef)
     v = buf[...] * c[0]
     for turn in range(8):
@@ -388,10 +451,8 @@
         if turn % 2 == 0:
             done[i, 0] = zp[4 * q - 4 + i] + half(core, tile)
         else:
-            full = p[4 * q - 4 + i] + tile
-            done[i, 1] = half(core, full)
-            if i == 3:
-                last[...] = full
+            done[i, 1] = p[4 * q - 4 + i] + half(core, tile)
+    last[...] = ends[q - 1] + tile
 
 
 def final_kernel(got, w, out):
@@ -402,11 +463,10 @@
             out[1, l, rows] = got[src, 1, l]
 
 
-def scratch(halo):
-    count = 8 + 2 * halo
-    return [pltpu.VMEM((count, 24, 128), jnp.float32)] * 2 + [
-        pltpu.VMEM((count - 1, 24, 128), jnp.float32),
-    ] + [pltpu.VMEM((count, 24, 128), jnp.float32)] * 3
+def coefficient_scratch(halo):
+    counts = [8 + 2 * halo] * 5
+    counts[1] -= 1
+    return [pltpu.VMEM((count, 24, 128), jnp.float32) for count in counts]
 
 
 def call(kernel, outs, scratches, *args, smem=True):
@@ -421,30 +481,18 @@
     )(*args)
 
 
-def across(own_tile, send, core):
-    got = odd(send)
-    swap = even(got)
-    left = jnp.where(core == 0, got, swap)
-    right = jnp.where(core == 0, swap, got)
-    wide = jnp.concatenate([left, own_tile, right], 1)
-    y_got = yodd(wide)
-    y_swap = even(y_got)
-    return got, swap, y_got, y_swap
-
-
 def body(initial, guess, cond, source):
     t = lax.axis_index("tm")
     s = lax.axis_index("space")
     core = s % 2
     place = t ^ ((t >> 1) & 1)
     flags = jnp.stack([t, s, place, core]).astype(jnp.int32)
-    g = jnp.stack([jnp.where(t == NT - 1, initial, guess[0]), guess[1]])
-    pack = jnp.concatenate([g, cond[None], source[None]])
+    (pack,) = call(pack_kernel, [struct(4, 4, 128, 128)], [], flags, initial, guess, cond, source)
     ev = even(pack)
     od = odd(pack)
     layers = pltpu.VMEM((EXT, 128, 128), jnp.float32)
     fine_scratch = [pltpu.VMEM((2, EXT, 128, 128), jnp.float32)] * 2 + [layers] * 6
-    (a,) = call(first_kernel, [struct(2, 4, 128, 128)], fine_scratch, flags, g, cond, source, ev, od)
+    (a,) = call(first_kernel, [struct(2, 4, 128, 128)], fine_scratch, flags, pack, ev, od)
 
     start = 8 * place
     rows_of = lambda x: lax.dynamic_slice_in_dim(jnp.pad(x, ((0, 0), (8, 8), (0, 0))), start, 24, 1)
@@ -465,38 +513,42 @@
     )
     w_before = lax.ppermute(w, "tm", [(i, (i + 1) % NT) for i in range(NT)])
     own = lax.all_to_all(e, "tm", 0, 0)
-    own, w_before = lax.optimization_barrier((own, w_before))
     other = even(own)
-
-    picks = [(2 * i - 1) % NT for i in range(8)]
-    mine = jnp.stack([own[k] for k in picks])
-    yours = jnp.stack([other[k] for k in picks])
-    send = jnp.where(core == 0, mine[:, 0:2], mine[:, 2:4])
-    both = jnp.where(core == 0, jnp.concatenate([mine, yours], 1), jnp.concatenate([yours, mine], 1))
-    xg, xs, yg, ys = across(both, send, core)
-    p, ap, send = call(
-        pairs_kernel,
-        [struct(NT, 8, 8, 128), struct(8, 8, 8, 128), struct(4, 4, 8, 128)],
-        scratch(2),
-        flags, tiles, own, other, xg, xs, yg, ys,
-    )
-    xg, xs, yg, ys = across(jnp.stack([p[1], p[5], p[9], p[13]]), send, core)
-    p, zp, last, done = call(
+    chips, send = call(chips_kernel, [struct(NT, 8, 8, 128), struct(4, 12, 8, 128)], [], flags, own, other)
+    xg = odd(send)
+    xs = even(xg)
+    (send,) = call(rows_kernel, [struct(4, 31, 8, 128)], [], flags, chips, xg, xs)
+    yg = yodd(send)
+    ys = even(yg)
+    regions = [pltpu.VMEM((8 + 2 * h, 24, 128), jnp.float32) for h in HALOS]
+    p, zp, ends, last, done = call(
         quads_kernel,
-        [struct(12, 8, 8, 128), struct(12, 4, 8, 128), struct(8, 8, 128), struct(4, 2, 4, 8, 128)],
-        scratch(4),
-        flags, tiles, p, ap, xg, xs, yg, ys,
+        [
+            struct(12, 4, 8, 128),
+            struct(12, 4, 8, 128),
+            struct(3, 8, 8, 128),
+            struct(8, 8, 128),
+            struct(4, 2, 4, 8, 128),
+        ],
+        regions + coefficient_scratch(6),
+        flags, tiles, chips, xg, xs, yg, ys,
     )
     parts = [done]
     for q in (1, 2, 3):
-        got = across(last[None], last[None], core)
-        xg, xs, yg, ys = (x[0] for x in got)
+        xg = odd(last)
+        xs = even(xg)
+        left = jnp.where(core == 0, xg, xs)
+        right = jnp.where(core == 0, xs, xg)
+        yg = yodd(jnp.concatenate([left, last, right]))
+        ys = even(yg)
         last, done = call(
-            lambda *refs, q=q: chain_kernel(q, *refs),
+            functools.partial(chain_kernel, q),
             [struct(8, 8, 128), struct(4, 2, 4, 8, 128)],
-            scratch(8),
-            flags, tiles, last, p, zp, xg, xs, yg, ys,
+            [pltpu.VMEM((24, 24, 128), jnp.float32)] + coefficient_scratch(8),
+            flags, tiles, last, p, zp, ends, xg, xs, yg, ys,
         )
+        if q == 2:
+            last, w_before = lax.optimization_barrier((last, w_before))
         parts.append(done)
     back = lax.all_to_all(jnp.concatenate(parts), "tm", 0, 0)
     (out,) = call(final_kernel, [struct(2, 4, 128, 128)], [], back, w_before, smem=False)

time: 193 us -> 179 us (0.927)
  waiting for transfers between devices: 115 us -> 90.9 us
  blocking collectives: 22.4 us -> 42.5 us
  starting transfers between devices: 27.7 us -> 17.8 us
    all_to_all x0 -> x1, blocking collectives: none -> 21.4 us  [body(): own = lax.all_to_all(e, 'tm', 0, 0)]
    ppermute x1, waiting for transfers between devices: 14 us -> 0.01 us  [body(): w_before = lax.ppermute(w, 'tm', [(i, (i + 1) % NT) for i in range(NT)])]
    all_to_all x1 -> x0, starting transfers between devices: 9.47 us -> none  [body(): own = lax.all_to_all(e, 'tm', 0, 0)]
    ppermute x7 -> x6, waiting for transfers between devices: 58.6 us -> 50.2 us  [odd(): return lax.ppermute(x, ('tm', 'space'), ODD)]
    ppermute x5 -> x4, starting transfers between devices: 5.3 us -> 0.37 us  [yodd(): return lax.ppermute(x, ('tm', 'space'), YODD)]
    ppermute x14 -> x12, starting transfers between devices: 0.72 us -> 4.77 us  [even(): return lax.ppermute(x, 'space', EVEN)]
    unnamed x20 -> x12, local copies, waits for them, and re-layouts: 1.1 us -> 3.9 us
    ppermute x7 -> x6, starting transfers between devices: 10.3 us -> 12.6 us  [odd(): return lax.ppermute(x, ('tm', 'space'), ODD)]
  transfers between devices with their start and end apart: 28 -> 23, of which waited for: 26 -> 21; matrix products, arithmetic and copies ran while one was open for 0% -> 0% of each run, Pallas kernels for 0% -> 1%
where the time goes in v3:
time: 179 us; the launch traced here: 178 us
  waiting for transfers between devices  90.9 us (51%)
  blocking collectives  42.5 us (24%)
  Pallas kernels  22.7 us (13%)
  starting transfers between devices  17.8 us (10%)
  local copies, waits for them, and re-layouts  3.95 us (2%)
    ppermute x6, waiting for transfers between devices, odd(): return lax.ppermute(x, ('tm', 'space'), ODD)  50.2 us
    ppermute x4, waiting for transfers between devices, yodd(): return lax.ppermute(x, ('tm', 'space'), YODD)  25.3 us
    pallas_call x10, Pallas kernels, call(): pl.pallas_call(kernel, out_shape=outs, in_specs=specs, out_specs=[VMEM] *...  22.7 us
    all_to_all x1, blocking collectives, body(): own = lax.all_to_all(e, 'tm', 0, 0)  21.4 us
    all_to_all x1, blocking collectives, body(): back = lax.all_to_all(jnp.concatenate(parts), 'tm', 0, 0)  21.1 us
    ppermute x12, waiting for transfers between devices, even(): return lax.ppermute(x, 'space', EVEN)  15.3 us
    ppermute x6, starting transfers between devices, odd(): return lax.ppermute(x, ('tm', 'space'), ODD)  12.6 us
    ppermute x12, starting transfers between devices, even(): return lax.ppermute(x, 'space', EVEN)  4.77 us
  transfers between devices with their start and end apart: 23, of which 21 were waited for; matrix products, arithmetic and copies ran while one was open for 0% of the time, Pallas kernels for 1%

profile of v3, /device:TPU:16, one launch (start us, length us, event | category | flops | bytes accessed | tf_op | source)
XLA Modules:
  0.0 178.4 jit_solution(14830487931634525733)
XLA Ops:
  0.0 0.1 pad_add_fusion.flags
  0.1 0.9 copy-done
  1.0 0.9 copy-done.2
  2.0 1.0 copy-done.4
  3.0 0.9 copy-done.5
  4.0 0.6 shard_map.46.pack
  4.6 2.1 %collective-permute-start.1 = (f32[4,4,128,128]{3,2,1,0:T(8,128)S(1)}, f32[4,4,128,128]{3,2,1,0:T(8,128)S(1)}, u32[]{:S(2)}, u32[]{:S(2)}) collective-permute-start(f32[4,4,128,128]{3,2,1,0:T(8,128)S(1)} %shard_map.46.pack), channel_id=1, source_target_pairs={{0,16},{1,2},{2,1},{3,4},{4,3},{5,6},{6,5},{7,8},{8,7},{9,10},{10,... | collective-permute-start | bytes 3145736 | tf_op jit(solution)/shard_map/ppermute | solution.py:58
  6.7 0.0 collective-permute-start
  6.7 16.0 %collective-permute-done.1.od.odc = f32[4,4,128,128]{3,2,1,0:T(8,128)S(1)} collective-permute-done((f32[4,4,128,128]{3,2,1,0:T(8,128)S(1)}, f32[4,4,128,128]{3,2,1,0:T(8,128)S(1)}, u32[]{:S(2)}, u32[]{:S(2)}) %collective-permute-start.1) | collective-permute-done | bytes 1048608 | tf_op jit(solution)/shard_map/ppermute | solution.py:58
  22.6 0.0 collective-permute-done.ev.evc
  22.6 3.9 %shard_map.47.a = f32[2,4,128,128]{3,2,1,0:T(8,128)S(1)} custom-call(s32[4]{0:T(128)S(1)} %pad_add_fusion.flags, f32[4,4,128,128]{3,2,1,0:T(8,128)S(1)} %shard_map.46.pack, f32[4,4,128,128]{3,2,1,0:T(8,128)S(1)} %collective-permute-done.ev.evc, f32[4,4,128,128]{3,2,1,0:T(8,128)S(1)} %collective-permute-done.1.od.odc), custom_call_target="tpu_custom_call" | custom-call | tf_op jit(solution)/shard_map/pallas_call | solution.py:474
  26.5 0.1 collective-permute-start.2
  26.7 1.8 %collective-permute-done.2.ev = f32[2,4,128,128]{3,2,1,0:T(8,128)S(1)} collective-permute-done((f32[2,4,128,128]{3,2,1,0:T(8,128)S(1)}, f32[2,4,128,128]{3,2,1,0:T(8,128)S(1)}, u32[]{:S(2)}, u32[]{:S(2)}) %collective-permute-start.2) | collective-permute-done | bytes 524320 | tf_op jit(solution)/shard_map/ppermute | solution.py:54
  28.5 0.1 pad_maximum_fusion
  28.6 2.1 %collective-permute-start.3 = (f32[1472,128]{1,0:T(8,128)S(1)}, f32[1472,128]{1,0:T(8,128)S(1)}, u32[]{:S(2)}, u32[]{:S(2)}) collective-permute-start(f32[1472,128]{1,0:T(8,128)S(1)} %pad_maximum_fusion), channel_id=1, source_target_pairs={{0,16},{1,2},{2,1},{3,4},{4,3},{5,6},{6,5},{7,8},{8,7},{9,10},{10,... | collective-permute-start | bytes 2261000 | tf_op jit(solution)/shard_map/ppermute | solution.py:58
  30.7 12.8 %collective-permute-done.3.od = f32[1472,128]{1,0:T(8,128)S(1)} collective-permute-done((f32[1472,128]{1,0:T(8,128)S(1)}, f32[1472,128]{1,0:T(8,128)S(1)}, u32[]{:S(2)}, u32[]{:S(2)}) %collective-permute-start.3) | collective-permute-done | bytes 753696 | tf_op jit(solution)/shard_map/ppermute | solution.py:58
  43.5 0.0 copy-start.3
  43.5 0.1 collective-permute-start.4
  43.6 1.5 collective-permute-done.4.ev5
  45.1 5.1 %shard_map.48 = (f32[16,4,8,128]{3,2,1,0:T(8,128)S(1)}, f32[4,128,128]{2,1,0:T(8,128)S(1)}, f32[24,24,128]{2,1,0:T(8,128)S(1)}) custom-call(s32[4]{0:T(128)S(1)} %pad_add_fusion.flags, f32[2,4,128,128]{3,2,1,0:T(8,128)S(1)} %shard_map.47.a, f32[4,128,128]{2,1,0:T(8,128)S(1)} %copy-done.1, f32[4,128,128]{2,1,0:T(8,128)S(1)} %copy-done.3, ...), custom_call_target="tpu_custom_call" | custom-call | tf_op jit(solution)/shard_map/pallas_call | solution.py:474
  50.2 21.4 %all_to_all.10.own = f32[16,4,8,128]{3,2,1,0:T(8,128)S(1)} all-to-all(f32[16,4,8,128]{3,2,1,0:T(8,128)S(1)} %get-tuple-element.23), channel_id=1, replica_groups=mesh['tm'=16,'space'=16] {'tm'}, dimensions={0} | all-to-all | bytes 524288 | tf_op jit(solution)/shard_map/all_to_all | solution.py:515
  71.6 0.0 collective-permute-start.5
  71.6 1.5 collective-permute-done.5.other
  73.1 0.6 shard_map.49
  73.7 2.3 %collective-permute-start.6 = (f32[4,12,8,128]{3,2,1,0:T(8,128)S(1)}, f32[4,12,8,128]{3,2,1,0:T(8,128)S(1)}, u32[]{:S(2)}, u32[]{:S(2)}) collective-permute-start(f32[4,12,8,128]{3,2,1,0:T(8,128)S(1)} %get-tuple-element.25), channel_id=1, source_target_pairs={{0,16},{1,2},{2,1},{3,4},{4,3},{5,6},{6,5},{7,8},{8,7},{9,10},{10,... | collective-permute-start | bytes 589832 | tf_op jit(solution)/shard_map/ppermute | solution.py:58
  76.0 6.5 %collective-permute-done.6.got.xg = f32[4,12,8,128]{3,2,1,0:T(8,128)S(1)} collective-permute-done((f32[4,12,8,128]{3,2,1,0:T(8,128)S(1)}, f32[4,12,8,128]{3,2,1,0:T(8,128)S(1)}, u32[]{:S(2)}, u32[]{:S(2)}) %collective-permute-start.6) | collective-permute-done | bytes 196640 | tf_op jit(solution)/shard_map/ppermute | solution.py:58
  82.5 0.0 collective-permute-start.7
  82.5 1.4 collective-permute-done.7.swap.xs
  84.0 0.6 shard_map.50
  84.6 0.1 collective-permute-start.8
  84.7 9.6 %collective-permute-done.8.yg = f32[4,31,8,128]{3,2,1,0:T(8,128)S(1)} collective-permute-done((f32[4,31,8,128]{3,2,1,0:T(8,128)S(1)}, f32[4,31,8,128]{3,2,1,0:T(8,128)S(1)}, u32[]{:S(2)}, u32[]{:S(2)}) %collective-permute-start.8) | collective-permute-done | bytes 507936 | tf_op jit(solution)/shard_map/ppermute | solution.py:62
  94.3 0.0 collective-permute-start.9
  94.3 1.9 %collective-permute-done.9.ys = f32[4,31,8,128]{3,2,1,0:T(8,128)S(1)} collective-permute-done((f32[4,31,8,128]{3,2,1,0:T(8,128)S(1)}, f32[4,31,8,128]{3,2,1,0:T(8,128)S(1)}, u32[]{:S(2)}, u32[]{:S(2)}) %collective-permute-start.9) | collective-permute-done | bytes 507936 | tf_op jit(solution)/shard_map/ppermute | solution.py:54
  96.2 4.5 %shard_map.51 = (f32[12,4,8,128]{3,2,1,0:T(8,128)S(1)}, f32[12,4,8,128]{3,2,1,0:T(8,128)S(1)}, f32[3,8,8,128]{3,2,1,0:T(8,128)S(1)}, f32[8,8,128]{2,1,0:T(8,128)S(1)}, f32[4,2,4,8,128]{4,3,2,1,0:T(8,128)S(1)}) custom-call(s32[4]{0:T(128)S(1)} %pad_add_fusion.flags, f32[24,24,128]{2,1,0:T(8,128)S(1)} %get-tuple-element.22.cond, ...), custom_call_target="tpu_custom_call" | custom-call | tf_op jit(solution)/shard_map/pallas_call | solution.py:474
  100.7 2.1 %collective-permute-start.10 = (f32[8,8,128]{2,1,0:T(8,128)S(1)}, f32[8,8,128]{2,1,0:T(8,128)S(1)}, u32[]{:S(2)}, u32[]{:S(2)}) collective-permute-start(f32[8,8,128]{2,1,0:T(8,128)S(1)} %get-tuple-element.27.c_in), channel_id=1, source_target_pairs={{0,16},{1,2},{2,1},{3,4},{4,3},{5,6},{6,5},{7,8},{8,7},{9,10},{10,... | collective-permute-start | bytes 98312 | tf_op jit(solution)/shard_map/ppermute | solution.py:58
  102.8 4.9 %collective-permute-done.10.xg = f32[8,8,128]{2,1,0:T(8,128)S(1)} collective-permute-done((f32[8,8,128]{2,1,0:T(8,128)S(1)}, f32[8,8,128]{2,1,0:T(8,128)S(1)}, u32[]{:S(2)}, u32[]{:S(2)}) %collective-permute-start.10) | collective-permute-done | bytes 32800 | tf_op jit(solution)/shard_map/ppermute | solution.py:58
  107.7 0.0 collective-permute-start.11
  107.7 1.2 collective-permute-done.11.xs
  109.0 0.1 collective-permute-start.12
  109.1 5.2 %collective-permute-done.12.yg = f32[24,8,128]{2,1,0:T(8,128)S(1)} collective-permute-done((f32[24,8,128]{2,1,0:T(8,128)S(1)}, f32[24,8,128]{2,1,0:T(8,128)S(1)}, u32[]{:S(2)}, u32[]{:S(2)}) %collective-permute-start.12) | collective-permute-done | bytes 98336 | tf_op jit(solution)/shard_map/ppermute | solution.py:62
  114.3 0.0 collective-permute-start.13
  114.3 1.3 collective-permute-done.13.ys
  115.6 2.0 %shard_map.52 = (f32[8,8,128]{2,1,0:T(8,128)S(1)}, f32[4,2,4,8,128]{4,3,2,1,0:T(8,128)S(1)}) custom-call(s32[4]{0:T(128)S(1)} %pad_add_fusion.flags, f32[24,24,128]{2,1,0:T(8,128)S(1)} %get-tuple-element.22.cond, f32[8,8,128]{2,1,0:T(8,128)S(1)} %get-tuple-element.27.c_in, f32[12,4,8,128]{3,2,1,0:T(8,128)S(1)} %get-tuple-element.28.p, ...), custom_call_target="tpu_custom_call" | custom-call | tf_op jit(solution)/shard_map/pallas_call | solution.py:474
  117.6 1.9 %collective-permute-start.14 = (f32[8,8,128]{2,1,0:T(8,128)S(1)}, f32[8,8,128]{2,1,0:T(8,128)S(1)}, u32[]{:S(2)}, u32[]{:S(2)}) collective-permute-start(f32[8,8,128]{2,1,0:T(8,128)S(1)} %get-tuple-element.32.c_in), channel_id=1, source_target_pairs={{0,16},{1,2},{2,1},{3,4},{4,3},{5,6},{6,5},{7,8},{8,7},{9,10},{10,... | collective-permute-start | bytes 98312 | tf_op jit(solution)/shard_map/ppermute | solution.py:58
  119.5 5.1 %collective-permute-done.14.xg = f32[8,8,128]{2,1,0:T(8,128)S(1)} collective-permute-done((f32[8,8,128]{2,1,0:T(8,128)S(1)}, f32[8,8,128]{2,1,0:T(8,128)S(1)}, u32[]{:S(2)}, u32[]{:S(2)}) %collective-permute-start.14) | collective-permute-done | bytes 32800 | tf_op jit(solution)/shard_map/ppermute | solution.py:58
  124.6 0.0 collective-permute-start.15
  124.6 0.0 collective-permute-start.18
  124.6 1.2 collective-permute-done.15.xs
  125.9 0.1 collective-permute-start.16
  126.0 5.2 %collective-permute-done.16.yg = f32[24,8,128]{2,1,0:T(8,128)S(1)} collective-permute-done((f32[24,8,128]{2,1,0:T(8,128)S(1)}, f32[24,8,128]{2,1,0:T(8,128)S(1)}, u32[]{:S(2)}, u32[]{:S(2)}) %collective-permute-start.16) | collective-permute-done | bytes 98336 | tf_op jit(solution)/shard_map/ppermute | solution.py:62
  131.2 4.6 %collective-permute-start.17 = (f32[24,8,128]{2,1,0:T(8,128)S(1)}, f32[24,8,128]{2,1,0:T(8,128)S(1)}, u32[]{:S(2)}, u32[]{:S(2)}) collective-permute-start(f32[24,8,128]{2,1,0:T(8,128)S(1)} %collective-permute-done.16.yg), channel_id=1, source_target_pairs={{0,1},{1,0},{2,3},{3,2},{4,5},{5,4},{6,7},{7,6},{8,9},{9,8},{10,11... | collective-permute-start | bytes 294920 | tf_op jit(solution)/shard_map/ppermute | solution.py:54
  135.8 0.9 collective-permute-done.17.ys
  136.7 2.0 %shard_map.53 = (f32[8,8,128]{2,1,0:T(8,128)S(1)}, f32[4,2,4,8,128]{4,3,2,1,0:T(8,128)S(1)}) custom-call(s32[4]{0:T(128)S(1)} %pad_add_fusion.flags, f32[24,24,128]{2,1,0:T(8,128)S(1)} %get-tuple-element.22.cond, f32[8,8,128]{2,1,0:T(8,128)S(1)} %get-tuple-element.32.c_in, f32[12,4,8,128]{3,2,1,0:T(8,128)S(1)} %get-tuple-element.28.p, ...), custom_call_target="tpu_custom_call" | custom-call | tf_op jit(solution)/shard_map/pallas_call | solution.py:474
  138.7 0.0 collective-permute-done.18.w
  138.7 2.2 %collective-permute-start.19 = (f32[8,8,128]{2,1,0:T(8,128)S(1)}, f32[8,8,128]{2,1,0:T(8,128)S(1)}, u32[]{:S(2)}, u32[]{:S(2)}) collective-permute-start(f32[8,8,128]{2,1,0:T(8,128)S(1)} %get-tuple-element.36.c_in), channel_id=1, source_target_pairs={{0,16},{1,2},{2,1},{3,4},{4,3},{5,6},{6,5},{7,8},{8,7},{9,10},{10,... | collective-permute-start | bytes 98312 | tf_op jit(solution)/shard_map/ppermute | solution.py:58
  140.9 5.0 %collective-permute-done.19.xg = f32[8,8,128]{2,1,0:T(8,128)S(1)} collective-permute-done((f32[8,8,128]{2,1,0:T(8,128)S(1)}, f32[8,8,128]{2,1,0:T(8,128)S(1)}, u32[]{:S(2)}, u32[]{:S(2)}) %collective-permute-start.19) | collective-permute-done | bytes 32800 | tf_op jit(solution)/shard_map/ppermute | solution.py:58
  145.8 1.2 collective-permute-done.20.xs
  147.1 0.1 collective-permute-start.21
  147.2 5.2 %collective-permute-done.21.yg = f32[24,8,128]{2,1,0:T(8,128)S(1)} collective-permute-done((f32[24,8,128]{2,1,0:T(8,128)S(1)}, f32[24,8,128]{2,1,0:T(8,128)S(1)}, u32[]{:S(2)}, u32[]{:S(2)}) %collective-permute-start.21) | collective-permute-done | bytes 98336 | tf_op jit(solution)/shard_map/ppermute | solution.py:62
  152.4 0.0 collective-permute-start.22
  152.4 1.3 collective-permute-done.22.ys
  153.7 2.6 %shard_map.54 = (f32[8,8,128]{2,1,0:T(8,128)}, f32[4,2,4,8,128]{4,3,2,1,0:T(8,128)S(1)}) custom-call(s32[4]{0:T(128)S(1)} %pad_add_fusion.flags, f32[24,24,128]{2,1,0:T(8,128)S(1)} %get-tuple-element.22.cond, f32[8,8,128]{2,1,0:T(8,128)S(1)} %get-tuple-element.36.c_in, f32[12,4,8,128]{3,2,1,0:T(8,128)S(1)} %get-tuple-element.28.p, ...), custom_call_target="tpu_custom_call" | custom-call | tf_op jit(solution)/shard_map/pallas_call | solution.py:474
  156.4 21.1 %all_to_all.11.got = f32[16,2,4,8,128]{4,3,2,1,0:T(8,128)S(1)} all-to-all(f32[16,2,4,8,128]{4,3,2,1,0:T(8,128)S(1)} %pad_maximum_fusion.1), channel_id=1, replica_groups=mesh['tm'=16,'space'=16] {'tm'}, dimensions={0} | all-to-all | bytes 1048576 | tf_op jit(solution)/shard_map/all_to_all | solution.py:553
  177.5 0.9 shard_map.55
  (25 shorter events, 0.2 us)
Async XLA Ops:
  0.1 1.0 copy-start
  1.0 0.9 copy-start.2
  2.0 1.0 copy-start.4
  3.0 0.9 copy-start.5
  4.0 2.7 %copy-start.1 = (f32[4,128,128]{2,1,0:T(8,128)S(1)}, f32[4,128,128]{2,1,0:T(8,128)}, u32[]{:S(2)}) copy-start(f32[4,128,128]{2,1,0:T(8,128)} %cond.3) | copy-start | bytes 786436
  4.6 18.0 %collective-permute-start.1 = (f32[4,4,128,128]{3,2,1,0:T(8,128)S(1)}, f32[4,4,128,128]{3,2,1,0:T(8,128)S(1)}, u32[]{:S(2)}, u32[]{:S(2)}) collective-permute-start(f32[4,4,128,128]{3,2,1,0:T(8,128)S(1)} %shard_map.46.pack), channel_id=1, source_target_pairs={{0,16},{1,2},{2,1},{3,4},{4,3},{5,6},{6,5},{7,8},{8,7},{9,10},{10,... | collective-permute-start | bytes 3145736 | tf_op jit(solution)/shard_map/ppermute | solution.py:58
  6.7 16.0 %collective-permute-start = (f32[4,4,128,128]{3,2,1,0:T(8,128)S(1)}, f32[4,4,128,128]{3,2,1,0:T(8,128)S(1)}, u32[]{:S(2)}, u32[]{:S(2)}) collective-permute-start(f32[4,4,128,128]{3,2,1,0:T(8,128)S(1)} %shard_map.46.pack), channel_id=1, source_target_pairs={{0,1},{1,0},{2,3},{3,2},{4,5},{5,4},{6,7},{7,6},{8,9},{9,8},{10,11... | collective-permute-start | bytes 3145736 | tf_op jit(solution)/shard_map/ppermute | solution.py:54
  26.5 2.0 %collective-permute-start.2 = (f32[2,4,128,128]{3,2,1,0:T(8,128)S(1)}, f32[2,4,128,128]{3,2,1,0:T(8,128)S(1)}, u32[]{:S(2)}, u32[]{:S(2)}) collective-permute-start(f32[2,4,128,128]{3,2,1,0:T(8,128)S(1)} %shard_map.47.a), channel_id=1, source_target_pairs={{0,1},{1,0},{2,3},{3,2},{4,5},{5,4},{6,7},{7,6},{8,9},{9,8},{10,11... | collective-permute-start | bytes 1572872 | tf_op jit(solution)/shard_map/ppermute | solution.py:54
  28.6 14.9 %collective-permute-start.3 = (f32[1472,128]{1,0:T(8,128)S(1)}, f32[1472,128]{1,0:T(8,128)S(1)}, u32[]{:S(2)}, u32[]{:S(2)}) collective-permute-start(f32[1472,128]{1,0:T(8,128)S(1)} %pad_maximum_fusion), channel_id=1, source_target_pairs={{0,16},{1,2},{2,1},{3,4},{4,3},{5,6},{6,5},{7,8},{8,7},{9,10},{10,... | collective-permute-start | bytes 2261000 | tf_op jit(solution)/shard_map/ppermute | solution.py:58
  43.5 1.6 copy-start.3
  43.5 1.6 collective-permute-start.4
  71.6 1.5 collective-permute-start.5
  73.7 8.8 %collective-permute-start.6 = (f32[4,12,8,128]{3,2,1,0:T(8,128)S(1)}, f32[4,12,8,128]{3,2,1,0:T(8,128)S(1)}, u32[]{:S(2)}, u32[]{:S(2)}) collective-permute-start(f32[4,12,8,128]{3,2,1,0:T(8,128)S(1)} %get-tuple-element.25), channel_id=1, source_target_pairs={{0,16},{1,2},{2,1},{3,4},{4,3},{5,6},{6,5},{7,8},{8,7},{9,10},{10,... | collective-permute-start | bytes 589832 | tf_op jit(solution)/shard_map/ppermute | solution.py:58
  82.5 1.4 collective-permute-start.7
  84.6 9.7 %collective-permute-start.8 = (f32[4,31,8,128]{3,2,1,0:T(8,128)S(1)}, f32[4,31,8,128]{3,2,1,0:T(8,128)S(1)}, u32[]{:S(2)}, u32[]{:S(2)}) collective-permute-start(f32[4,31,8,128]{3,2,1,0:T(8,128)S(1)} %shard_map.50), channel_id=1, source_target_pairs={{0,225},{1,16},{2,227},{3,18},{4,229},{5,20},{6,231},{7,22},{8,233... | collective-permute-start | bytes 1523720 | tf_op jit(solution)/shard_map/ppermute | solution.py:62
  94.3 1.9 %collective-permute-start.9 = (f32[4,31,8,128]{3,2,1,0:T(8,128)S(1)}, f32[4,31,8,128]{3,2,1,0:T(8,128)S(1)}, u32[]{:S(2)}, u32[]{:S(2)}) collective-permute-start(f32[4,31,8,128]{3,2,1,0:T(8,128)S(1)} %collective-permute-done.8.yg), channel_id=1, source_target_pairs={{0,1},{1,0},{2,3},{3,2},{4,5},{5,4},{6,7},{7,6},{8,9},{9,8},{10,11... | collective-permute-start | bytes 1523720 | tf_op jit(solution)/shard_map/ppermute | solution.py:54
  100.7 7.0 %collective-permute-start.10 = (f32[8,8,128]{2,1,0:T(8,128)S(1)}, f32[8,8,128]{2,1,0:T(8,128)S(1)}, u32[]{:S(2)}, u32[]{:S(2)}) collective-permute-start(f32[8,8,128]{2,1,0:T(8,128)S(1)} %get-tuple-element.27.c_in), channel_id=1, source_target_pairs={{0,16},{1,2},{2,1},{3,4},{4,3},{5,6},{6,5},{7,8},{8,7},{9,10},{10,... | collective-permute-start | bytes 98312 | tf_op jit(solution)/shard_map/ppermute | solution.py:58
  107.7 1.2 collective-permute-start.11
  109.0 5.3 %collective-permute-start.12 = (f32[24,8,128]{2,1,0:T(8,128)S(1)}, f32[24,8,128]{2,1,0:T(8,128)S(1)}, u32[]{:S(2)}, u32[]{:S(2)}) collective-permute-start(f32[24,8,128]{2,1,0:T(8,128)S(1)} %pad_maximum_fusion.3), channel_id=1, source_target_pairs={{0,225},{1,16},{2,227},{3,18},{4,229},{5,20},{6,231},{7,22},{8,233... | collective-permute-start | bytes 294920 | tf_op jit(solution)/shard_map/ppermute | solution.py:62
  114.3 1.3 collective-permute-start.13
  117.6 7.0 %collective-permute-start.14 = (f32[8,8,128]{2,1,0:T(8,128)S(1)}, f32[8,8,128]{2,1,0:T(8,128)S(1)}, u32[]{:S(2)}, u32[]{:S(2)}) collective-permute-start(f32[8,8,128]{2,1,0:T(8,128)S(1)} %get-tuple-element.32.c_in), channel_id=1, source_target_pairs={{0,16},{1,2},{2,1},{3,4},{4,3},{5,6},{6,5},{7,8},{8,7},{9,10},{10,... | collective-permute-start | bytes 98312 | tf_op jit(solution)/shard_map/ppermute | solution.py:58
  124.6 1.2 collective-permute-start.15
  124.6 14.1 %collective-permute-start.18 = (f32[4,128,128]{2,1,0:T(8,128)S(1)}, f32[4,128,128]{2,1,0:T(8,128)S(1)}, u32[]{:S(2)}, u32[]{:S(2)}) collective-permute-start(f32[4,128,128]{2,1,0:T(8,128)S(1)} %get-tuple-element.35), channel_id=1, source_target_pairs={{0,16},{16,32},{32,48},{48,64},{64,80},{80,96},{96,112},{112,128},... | collective-permute-start | bytes 786440 | tf_op jit(solution)/shard_map/ppermute | solution.py:514
  125.9 5.3 %collective-permute-start.16 = (f32[24,8,128]{2,1,0:T(8,128)S(1)}, f32[24,8,128]{2,1,0:T(8,128)S(1)}, u32[]{:S(2)}, u32[]{:S(2)}) collective-permute-start(f32[24,8,128]{2,1,0:T(8,128)S(1)} %pad_maximum_fusion.4), channel_id=1, source_target_pairs={{0,225},{1,16},{2,227},{3,18},{4,229},{5,20},{6,231},{7,22},{8,233... | collective-permute-start | bytes 294920 | tf_op jit(solution)/shard_map/ppermute | solution.py:62
  131.2 5.5 %collective-permute-start.17 = (f32[24,8,128]{2,1,0:T(8,128)S(1)}, f32[24,8,128]{2,1,0:T(8,128)S(1)}, u32[]{:S(2)}, u32[]{:S(2)}) collective-permute-start(f32[24,8,128]{2,1,0:T(8,128)S(1)} %collective-permute-done.16.yg), channel_id=1, source_target_pairs={{0,1},{1,0},{2,3},{3,2},{4,5},{5,4},{6,7},{7,6},{8,9},{9,8},{10,11... | collective-permute-start | bytes 294920 | tf_op jit(solution)/shard_map/ppermute | solution.py:54
  138.7 7.1 %collective-permute-start.19 = (f32[8,8,128]{2,1,0:T(8,128)S(1)}, f32[8,8,128]{2,1,0:T(8,128)S(1)}, u32[]{:S(2)}, u32[]{:S(2)}) collective-permute-start(f32[8,8,128]{2,1,0:T(8,128)S(1)} %get-tuple-element.36.c_in), channel_id=1, source_target_pairs={{0,16},{1,2},{2,1},{3,4},{4,3},{5,6},{6,5},{7,8},{8,7},{9,10},{10,... | collective-permute-start | bytes 98312 | tf_op jit(solution)/shard_map/ppermute | solution.py:58
  145.8 1.2 collective-permute-start.20
  147.1 5.3 %collective-permute-start.21 = (f32[24,8,128]{2,1,0:T(8,128)S(1)}, f32[24,8,128]{2,1,0:T(8,128)S(1)}, u32[]{:S(2)}, u32[]{:S(2)}) collective-permute-start(f32[24,8,128]{2,1,0:T(8,128)S(1)} %pad_maximum_fusion.5), channel_id=1, source_target_pairs={{0,225},{1,16},{2,227},{3,18},{4,229},{5,20},{6,231},{7,22},{8,233... | collective-permute-start | bytes 294920 | tf_op jit(solution)/shard_map/ppermute | solution.py:62
  152.4 1.3 collective-permute-start.22

commit v4 on v3

--- a/solution.py
+++ b/solution.py
@@ -21,7 +21,7 @@
     for t in range(NT):
         for s in range(NS):
             to = s + 1 if s % 2 else s - 1
-            pairs.append((t * NS + s, t * NS + to if 0 <= to < NS else (t ^ 1) * NS + s))
+            pairs.append((t * NS + s, t * NS + to if 0 <= to < NS else (t ^ 2) * NS + s))
     return pairs
 
 
@@ -149,20 +149,6 @@
             clear_outside(s, [b.at[0], b.at[1]], PAD - h, PAD + 4 + h)
 
 
-def pack_kernel(flags, initial, guess, cond, source, out):
-    @pl.when(flags[0] == NT - 1)
-    def _():
-        out[0] = initial[...]
-
-    @pl.when(flags[0] != NT - 1)
-    def _():
-        out[0] = guess[0]
-
-    out[1] = guess[1]
-    out[2] = cond[...]
-    out[3] = source[...]
-
-
 def first_kernel(flags, pack, ev, od, out, s0, s1, cnd, heat, *coefficients):
     s = flags[1]
     core = s % 2
@@ -199,7 +185,7 @@
 
 
 def second_kernel(
-    flags, a, cond, source, ev, od, evc, odc, ev5, chip, e_out, w_out, tiles, s0, s1, cnd, heat, *rest
+    flags, a, pack, ev, od, evc, odc, ev5, chip, e_out, w_out, tiles, s0, s1, cnd, heat, *rest
 ):
     coefficients, wide = rest[:4], rest[4]
     t, s = flags[0], flags[1]
@@ -208,8 +194,8 @@
     for l in range(4):
         for f in range(2):
             s0[f, PAD + l] = a[f, l]
-        cnd[PAD + l] = cond[l]
-        heat[PAD + l] = source[l]
+        cnd[PAD + l] = pack[2, l]
+        heat[PAD + l] = pack[3, l]
     for l in range(8):
         tiles[8 + l] = chip[l]
 
@@ -487,7 +473,8 @@
     core = s % 2
     place = t ^ ((t >> 1) & 1)
     flags = jnp.stack([t, s, place, core]).astype(jnp.int32)
-    (pack,) = call(pack_kernel, [struct(4, 4, 128, 128)], [], flags, initial, guess, cond, source)
+    swap = (jnp.arange(4) == 0)[:, None, None, None] & (t == NT - 1)
+    pack = jnp.where(swap, initial[None], jnp.concatenate([guess, cond[None], source[None]]))
     ev = even(pack)
     od = odd(pack)
     layers = pltpu.VMEM((EXT, 128, 128), jnp.float32)
@@ -496,7 +483,7 @@
 
     start = 8 * place
     rows_of = lambda x: lax.dynamic_slice_in_dim(jnp.pad(x, ((0, 0), (8, 8), (0, 0))), start, 24, 1)
-    mine, yours = rows_of(cond), rows_of(ev[2])
+    mine, yours = rows_of(pack[2]), rows_of(ev[2])
     chip = jnp.where(core == 0, jnp.concatenate([mine, yours]), jnp.concatenate([yours, mine]))
 
     ev2 = even(a)
@@ -509,15 +496,17 @@
         second_kernel,
         [struct(NT, 4, 8, 128), struct(4, 128, 128), struct(24, 24, 128)],
         fine_scratch + [pltpu.VMEM((2, EXT, 128, 128), jnp.float32)],
-        flags, a, cond, source, ev2, od2, ev, od, ev5, chip,
+        flags, a, pack, ev2, od2, ev, od, ev5, chip,
     )
+    own = lax.all_to_all(e, "tm", 0, 0)
+    own, w = lax.optimization_barrier((own, w))
     w_before = lax.ppermute(w, "tm", [(i, (i + 1) % NT) for i in range(NT)])
-    own = lax.all_to_all(e, "tm", 0, 0)
     other = even(own)
     chips, send = call(chips_kernel, [struct(NT, 8, 8, 128), struct(4, 12, 8, 128)], [], flags, own, other)
     xg = odd(send)
     xs = even(xg)
     (send,) = call(rows_kernel, [struct(4, 31, 8, 128)], [], flags, chips, xg, xs)
+    send, w_before = lax.optimization_barrier((send, w_before))
     yg = yodd(send)
     ys = even(yg)
     regions = [pltpu.VMEM((8 + 2 * h, 24, 128), jnp.float32) for h in HALOS]
@@ -547,8 +536,6 @@
             [pltpu.VMEM((24, 24, 128), jnp.float32)] + coefficient_scratch(8),
             flags, tiles, last, p, zp, ends, xg, xs, yg, ys,
         )
-        if q == 2:
-            last, w_before = lax.optimization_barrier((last, w_before))
         parts.append(done)
     back = lax.all_to_all(jnp.concatenate(parts), "tm", 0, 0)
     (out,) = call(final_kernel, [struct(2, 4, 128, 128)], [], back, w_before, smem=False)

time: 179 us -> 171 us (0.955)
  local copies, waits for them, and re-layouts: 3.95 us -> 0.08 us
  starting transfers between devices: 17.8 us -> 14.1 us
    ppermute x12, starting transfers between devices: 4.77 us -> 0.21 us  [even(): return lax.ppermute(x, 'space', EVEN)]
    unnamed x12 -> x0, local copies, waits for them, and re-layouts: 3.9 us -> none
    pallas_call x10 -> x9, Pallas kernels: 22.7 us -> 22 us  [call(): pl.pallas_call(kernel, out_shape=outs, in_specs=specs, out_specs=[VMEM] *...]
  transfers between devices with their start and end apart: 23 -> 23, of which waited for: 21 -> 21; matrix products, arithmetic and copies ran while one was open for 0% -> 0% of each run, Pallas kernels for 1% -> 0%
where the time goes in v4:
time: 171 us
  waiting for transfers between devices  90.1 us (53%)
  blocking collectives  42.5 us (25%)
  Pallas kernels  22 us (13%)
  starting transfers between devices  14.1 us (8%)
  other arithmetic  1.72 us (1%)
    ppermute x6, waiting for transfers between devices, odd(): return lax.ppermute(x, ('tm', 'space'), ODD)  49.1 us
    ppermute x4, waiting for transfers between devices, yodd(): return lax.ppermute(x, ('tm', 'space'), YODD)  25.3 us
    pallas_call x9, Pallas kernels, call(): pl.pallas_call(kernel, out_shape=outs, in_specs=specs, out_specs=[VMEM] *...  22 us
    all_to_all x1, blocking collectives, body(): own = lax.all_to_all(e, 'tm', 0, 0)  21.4 us
    all_to_all x1, blocking collectives, body(): back = lax.all_to_all(jnp.concatenate(parts), 'tm', 0, 0)  21.1 us
    ppermute x12, waiting for transfers between devices, even(): return lax.ppermute(x, 'space', EVEN)  15.7 us
    ppermute x6, starting transfers between devices, odd(): return lax.ppermute(x, ('tm', 'space'), ODD)  12.2 us
  transfers between devices with their start and end apart: 23, of which 21 were waited for; matrix products, arithmetic and copies ran while one was open for 0% of the time, Pallas kernels for 0%

profile of v4, /device:TPU:16, one launch (start us, length us, event | category | flops | bytes accessed | tf_op | source)
XLA Modules:
  0.0 170.8 jit_solution(1424035916476197668)
XLA Ops:
  0.0 1.4 maximum_select_fusion.pack
  1.4 2.1 %collective-permute-start.1 = (f32[4,4,128,128]{3,2,1,0:T(8,128)S(1)}, f32[4,4,128,128]{3,2,1,0:T(8,128)S(1)}, u32[]{:S(2)}, u32[]{:S(2)}) collective-permute-start(f32[4,4,128,128]{3,2,1,0:T(8,128)S(1)} %maximum_select_fusion.pack), channel_id=1, source_target_pairs={{0,32},{1,2},{2,1},{3,4},{4,3},{5,6},{6,5},{7,8},{8,7},{9,10},{10,... | collective-permute-start | bytes 3145736 | tf_op jit(solution)/shard_map/ppermute | solution.py:58
  3.5 0.0 collective-permute-start
  3.5 0.1 pad_add_fusion.flags
  3.6 15.7 %collective-permute-done.1.od.odc = f32[4,4,128,128]{3,2,1,0:T(8,128)S(1)} collective-permute-done((f32[4,4,128,128]{3,2,1,0:T(8,128)S(1)}, f32[4,4,128,128]{3,2,1,0:T(8,128)S(1)}, u32[]{:S(2)}, u32[]{:S(2)}) %collective-permute-start.1) | collective-permute-done | bytes 1048608 | tf_op jit(solution)/shard_map/ppermute | solution.py:58
  19.4 0.0 collective-permute-done.ev.evc
  19.4 3.9 %shard_map.46.a = f32[2,4,128,128]{3,2,1,0:T(8,128)S(1)} custom-call(s32[4]{0:T(128)S(1)} %pad_add_fusion.flags, f32[4,4,128,128]{3,2,1,0:T(8,128)S(1)} %maximum_select_fusion.pack, f32[4,4,128,128]{3,2,1,0:T(8,128)S(1)} %collective-permute-done.ev.evc, f32[4,4,128,128]{3,2,1,0:T(8,128)S(1)} %collective-permute-done.1.od.odc), custom_call_target="tpu_custom_call" | custom-call | tf_op jit(solution)/shard_map/pallas_call | solution.py:460
  23.3 0.1 collective-permute-start.2
  23.5 1.8 %collective-permute-done.2.ev = f32[2,4,128,128]{3,2,1,0:T(8,128)S(1)} collective-permute-done((f32[2,4,128,128]{3,2,1,0:T(8,128)S(1)}, f32[2,4,128,128]{3,2,1,0:T(8,128)S(1)}, u32[]{:S(2)}, u32[]{:S(2)}) %collective-permute-start.2) | collective-permute-done | bytes 524320 | tf_op jit(solution)/shard_map/ppermute | solution.py:54
  25.3 0.1 pad_maximum_fusion
  25.3 2.1 %collective-permute-start.3 = (f32[1472,128]{1,0:T(8,128)S(1)}, f32[1472,128]{1,0:T(8,128)S(1)}, u32[]{:S(2)}, u32[]{:S(2)}) collective-permute-start(f32[1472,128]{1,0:T(8,128)S(1)} %pad_maximum_fusion), channel_id=1, source_target_pairs={{0,32},{1,2},{2,1},{3,4},{4,3},{5,6},{6,5},{7,8},{8,7},{9,10},{10,... | collective-permute-start | bytes 2261000 | tf_op jit(solution)/shard_map/ppermute | solution.py:58
  27.4 12.7 %collective-permute-done.3.od = f32[1472,128]{1,0:T(8,128)S(1)} collective-permute-done((f32[1472,128]{1,0:T(8,128)S(1)}, f32[1472,128]{1,0:T(8,128)S(1)}, u32[]{:S(2)}, u32[]{:S(2)}) %collective-permute-start.3) | collective-permute-done | bytes 753696 | tf_op jit(solution)/shard_map/ppermute | solution.py:58
  40.2 0.1 collective-permute-start.4
  40.3 1.5 collective-permute-done.4.ev5
  41.7 5.1 %shard_map.47 = (f32[16,4,8,128]{3,2,1,0:T(8,128)S(1)}, f32[4,128,128]{2,1,0:T(8,128)S(1)}, f32[24,24,128]{2,1,0:T(8,128)S(1)}) custom-call(s32[4]{0:T(128)S(1)} %pad_add_fusion.flags, f32[2,4,128,128]{3,2,1,0:T(8,128)S(1)} %shard_map.46.a, f32[4,4,128,128]{3,2,1,0:T(8,128)S(1)} %maximum_select_fusion.pack, ...), custom_call_target="tpu_custom_call" | custom-call | tf_op jit(solution)/shard_map/pallas_call | solution.py:460
  46.8 21.4 %all_to_all.10.own = f32[16,4,8,128]{3,2,1,0:T(8,128)S(1)} all-to-all(f32[16,4,8,128]{3,2,1,0:T(8,128)S(1)} %get-tuple-element.25), channel_id=1, replica_groups=mesh['tm'=16,'space'=16] {'tm'}, dimensions={0} | all-to-all | bytes 524288 | tf_op jit(solution)/shard_map/all_to_all | solution.py:501
  68.2 0.0 collective-permute-start.5
  68.2 1.5 collective-permute-done.5.other
  69.7 0.6 shard_map.48
  70.3 2.3 %collective-permute-start.6 = (f32[4,12,8,128]{3,2,1,0:T(8,128)S(1)}, f32[4,12,8,128]{3,2,1,0:T(8,128)S(1)}, u32[]{:S(2)}, u32[]{:S(2)}) collective-permute-start(f32[4,12,8,128]{3,2,1,0:T(8,128)S(1)} %get-tuple-element.29), channel_id=1, source_target_pairs={{0,32},{1,2},{2,1},{3,4},{4,3},{5,6},{6,5},{7,8},{8,7},{9,10},{10,... | collective-permute-start | bytes 589832 | tf_op jit(solution)/shard_map/ppermute | solution.py:58
  72.7 1.3 collective-permute-start.8
  73.9 5.3 %collective-permute-done.6.got.xg = f32[4,12,8,128]{3,2,1,0:T(8,128)S(1)} collective-permute-done((f32[4,12,8,128]{3,2,1,0:T(8,128)S(1)}, f32[4,12,8,128]{3,2,1,0:T(8,128)S(1)}, u32[]{:S(2)}, u32[]{:S(2)}) %collective-permute-start.6) | collective-permute-done | bytes 196640 | tf_op jit(solution)/shard_map/ppermute | solution.py:58
  79.2 0.0 collective-permute-start.7
  79.3 1.4 collective-permute-done.7.swap.xs
  80.7 0.6 shard_map.49
  81.3 0.0 collective-permute-done.8.w
  81.3 0.1 collective-permute-start.9
  81.4 9.6 %collective-permute-done.9.yg = f32[4,31,8,128]{3,2,1,0:T(8,128)S(1)} collective-permute-done((f32[4,31,8,128]{3,2,1,0:T(8,128)S(1)}, f32[4,31,8,128]{3,2,1,0:T(8,128)S(1)}, u32[]{:S(2)}, u32[]{:S(2)}) %collective-permute-start.9) | collective-permute-done | bytes 507936 | tf_op jit(solution)/shard_map/ppermute | solution.py:62
  91.1 0.0 collective-permute-start.10
  91.1 1.9 %collective-permute-done.10.ys = f32[4,31,8,128]{3,2,1,0:T(8,128)S(1)} collective-permute-done((f32[4,31,8,128]{3,2,1,0:T(8,128)S(1)}, f32[4,31,8,128]{3,2,1,0:T(8,128)S(1)}, u32[]{:S(2)}, u32[]{:S(2)}) %collective-permute-start.10) | collective-permute-done | bytes 507936 | tf_op jit(solution)/shard_map/ppermute | solution.py:54
  92.9 4.5 %shard_map.50 = (f32[12,4,8,128]{3,2,1,0:T(8,128)S(1)}, f32[12,4,8,128]{3,2,1,0:T(8,128)S(1)}, f32[3,8,8,128]{3,2,1,0:T(8,128)S(1)}, f32[8,8,128]{2,1,0:T(8,128)S(1)}, f32[4,2,4,8,128]{4,3,2,1,0:T(8,128)S(1)}) custom-call(s32[4]{0:T(128)S(1)} %pad_add_fusion.flags, f32[24,24,128]{2,1,0:T(8,128)S(1)} %get-tuple-element.24.cond, ...), custom_call_target="tpu_custom_call" | custom-call | tf_op jit(solution)/shard_map/pallas_call | solution.py:460
  97.4 2.1 %collective-permute-start.11 = (f32[8,8,128]{2,1,0:T(8,128)S(1)}, f32[8,8,128]{2,1,0:T(8,128)S(1)}, u32[]{:S(2)}, u32[]{:S(2)}) collective-permute-start(f32[8,8,128]{2,1,0:T(8,128)S(1)} %get-tuple-element.33.c_in), channel_id=1, source_target_pairs={{0,32},{1,2},{2,1},{3,4},{4,3},{5,6},{6,5},{7,8},{8,7},{9,10},{10,... | collective-permute-start | bytes 98312 | tf_op jit(solution)/shard_map/ppermute | solution.py:58
  99.5 4.9 %collective-permute-done.11.xg = f32[8,8,128]{2,1,0:T(8,128)S(1)} collective-permute-done((f32[8,8,128]{2,1,0:T(8,128)S(1)}, f32[8,8,128]{2,1,0:T(8,128)S(1)}, u32[]{:S(2)}, u32[]{:S(2)}) %collective-permute-start.11) | collective-permute-done | bytes 32800 | tf_op jit(solution)/shard_map/ppermute | solution.py:58
  104.5 0.0 collective-permute-start.12
  104.5 1.2 collective-permute-done.12.xs
  105.7 0.1 collective-permute-start.13
  105.8 5.2 %collective-permute-done.13.yg = f32[24,8,128]{2,1,0:T(8,128)S(1)} collective-permute-done((f32[24,8,128]{2,1,0:T(8,128)S(1)}, f32[24,8,128]{2,1,0:T(8,128)S(1)}, u32[]{:S(2)}, u32[]{:S(2)}) %collective-permute-start.13) | collective-permute-done | bytes 98336 | tf_op jit(solution)/shard_map/ppermute | solution.py:62
  111.0 0.0 collective-permute-start.14
  111.0 1.3 collective-permute-done.14.ys
  112.3 2.0 %shard_map.51 = (f32[8,8,128]{2,1,0:T(8,128)S(1)}, f32[4,2,4,8,128]{4,3,2,1,0:T(8,128)S(1)}) custom-call(s32[4]{0:T(128)S(1)} %pad_add_fusion.flags, f32[24,24,128]{2,1,0:T(8,128)S(1)} %get-tuple-element.24.cond, f32[8,8,128]{2,1,0:T(8,128)S(1)} %get-tuple-element.33.c_in, f32[12,4,8,128]{3,2,1,0:T(8,128)S(1)} %get-tuple-element.34.p, ...), custom_call_target="tpu_custom_call" | custom-call | tf_op jit(solution)/shard_map/pallas_call | solution.py:460
  114.3 1.9 %collective-permute-start.15 = (f32[8,8,128]{2,1,0:T(8,128)S(1)}, f32[8,8,128]{2,1,0:T(8,128)S(1)}, u32[]{:S(2)}, u32[]{:S(2)}) collective-permute-start(f32[8,8,128]{2,1,0:T(8,128)S(1)} %get-tuple-element.38.c_in), channel_id=1, source_target_pairs={{0,32},{1,2},{2,1},{3,4},{4,3},{5,6},{6,5},{7,8},{8,7},{9,10},{10,... | collective-permute-start | bytes 98312 | tf_op jit(solution)/shard_map/ppermute | solution.py:58
  116.2 5.1 %collective-permute-done.15.xg = f32[8,8,128]{2,1,0:T(8,128)S(1)} collective-permute-done((f32[8,8,128]{2,1,0:T(8,128)S(1)}, f32[8,8,128]{2,1,0:T(8,128)S(1)}, u32[]{:S(2)}, u32[]{:S(2)}) %collective-permute-start.15) | collective-permute-done | bytes 32800 | tf_op jit(solution)/shard_map/ppermute | solution.py:58
  121.4 0.0 collective-permute-start.16
  121.4 1.2 collective-permute-done.16.xs
  122.6 0.1 collective-permute-start.17
  122.7 5.2 %collective-permute-done.17.yg = f32[24,8,128]{2,1,0:T(8,128)S(1)} collective-permute-done((f32[24,8,128]{2,1,0:T(8,128)S(1)}, f32[24,8,128]{2,1,0:T(8,128)S(1)}, u32[]{:S(2)}, u32[]{:S(2)}) %collective-permute-start.17) | collective-permute-done | bytes 98336 | tf_op jit(solution)/shard_map/ppermute | solution.py:62
  127.9 0.0 collective-permute-start.18
  127.9 1.3 collective-permute-done.18.ys
  129.2 2.0 %shard_map.52 = (f32[8,8,128]{2,1,0:T(8,128)S(1)}, f32[4,2,4,8,128]{4,3,2,1,0:T(8,128)S(1)}) custom-call(s32[4]{0:T(128)S(1)} %pad_add_fusion.flags, f32[24,24,128]{2,1,0:T(8,128)S(1)} %get-tuple-element.24.cond, f32[8,8,128]{2,1,0:T(8,128)S(1)} %get-tuple-element.38.c_in, f32[12,4,8,128]{3,2,1,0:T(8,128)S(1)} %get-tuple-element.34.p, ...), custom_call_target="tpu_custom_call" | custom-call | tf_op jit(solution)/shard_map/pallas_call | solution.py:460
  131.2 1.7 %collective-permute-start.19 = (f32[8,8,128]{2,1,0:T(8,128)S(1)}, f32[8,8,128]{2,1,0:T(8,128)S(1)}, u32[]{:S(2)}, u32[]{:S(2)}) collective-permute-start(f32[8,8,128]{2,1,0:T(8,128)S(1)} %get-tuple-element.40.c_in), channel_id=1, source_target_pairs={{0,32},{1,2},{2,1},{3,4},{4,3},{5,6},{6,5},{7,8},{8,7},{9,10},{10,... | collective-permute-start | bytes 98312 | tf_op jit(solution)/shard_map/ppermute | solution.py:58
  133.0 5.3 %collective-permute-done.19.xg = f32[8,8,128]{2,1,0:T(8,128)S(1)} collective-permute-done((f32[8,8,128]{2,1,0:T(8,128)S(1)}, f32[8,8,128]{2,1,0:T(8,128)S(1)}, u32[]{:S(2)}, u32[]{:S(2)}) %collective-permute-start.19) | collective-permute-done | bytes 32800 | tf_op jit(solution)/shard_map/ppermute | solution.py:58
  138.3 0.0 collective-permute-start.20
  138.3 1.2 collective-permute-done.20.xs
  139.5 0.1 collective-permute-start.21
  139.6 5.2 %collective-permute-done.21.yg = f32[24,8,128]{2,1,0:T(8,128)S(1)} collective-permute-done((f32[24,8,128]{2,1,0:T(8,128)S(1)}, f32[24,8,128]{2,1,0:T(8,128)S(1)}, u32[]{:S(2)}, u32[]{:S(2)}) %collective-permute-start.21) | collective-permute-done | bytes 98336 | tf_op jit(solution)/shard_map/ppermute | solution.py:62
  144.8 0.0 collective-permute-start.22
  144.8 1.3 collective-permute-done.22.ys
  146.1 2.6 %shard_map.53 = (f32[8,8,128]{2,1,0:T(8,128)}, f32[4,2,4,8,128]{4,3,2,1,0:T(8,128)S(1)}) custom-call(s32[4]{0:T(128)S(1)} %pad_add_fusion.flags, f32[24,24,128]{2,1,0:T(8,128)S(1)} %get-tuple-element.24.cond, f32[8,8,128]{2,1,0:T(8,128)S(1)} %get-tuple-element.40.c_in, f32[12,4,8,128]{3,2,1,0:T(8,128)S(1)} %get-tuple-element.34.p, ...), custom_call_target="tpu_custom_call" | custom-call | tf_op jit(solution)/shard_map/pallas_call | solution.py:460
  148.8 21.1 %all_to_all.11.got = f32[16,2,4,8,128]{4,3,2,1,0:T(8,128)S(1)} all-to-all(f32[16,2,4,8,128]{4,3,2,1,0:T(8,128)S(1)} %pad_maximum_fusion.1), channel_id=1, replica_groups=mesh['tm'=16,'space'=16] {'tm'}, dimensions={0} | all-to-all | bytes 1048576 | tf_op jit(solution)/shard_map/all_to_all | solution.py:540
  169.9 0.9 shard_map.54
  (19 shorter events, 0.2 us)
Async XLA Ops:
  1.4 17.9 %collective-permute-start.1 = (f32[4,4,128,128]{3,2,1,0:T(8,128)S(1)}, f32[4,4,128,128]{3,2,1,0:T(8,128)S(1)}, u32[]{:S(2)}, u32[]{:S(2)}) collective-permute-start(f32[4,4,128,128]{3,2,1,0:T(8,128)S(1)} %maximum_select_fusion.pack), channel_id=1, source_target_pairs={{0,32},{1,2},{2,1},{3,4},{4,3},{5,6},{6,5},{7,8},{8,7},{9,10},{10,... | collective-permute-start | bytes 3145736 | tf_op jit(solution)/shard_map/ppermute | solution.py:58
  3.5 15.9 %collective-permute-start = (f32[4,4,128,128]{3,2,1,0:T(8,128)S(1)}, f32[4,4,128,128]{3,2,1,0:T(8,128)S(1)}, u32[]{:S(2)}, u32[]{:S(2)}) collective-permute-start(f32[4,4,128,128]{3,2,1,0:T(8,128)S(1)} %maximum_select_fusion.pack), channel_id=1, source_target_pairs={{0,1},{1,0},{2,3},{3,2},{4,5},{5,4},{6,7},{7,6},{8,9},{9,8},{10,11... | collective-permute-start | bytes 3145736 | tf_op jit(solution)/shard_map/ppermute | solution.py:54
  23.3 2.0 %collective-permute-start.2 = (f32[2,4,128,128]{3,2,1,0:T(8,128)S(1)}, f32[2,4,128,128]{3,2,1,0:T(8,128)S(1)}, u32[]{:S(2)}, u32[]{:S(2)}) collective-permute-start(f32[2,4,128,128]{3,2,1,0:T(8,128)S(1)} %shard_map.46.a), channel_id=1, source_target_pairs={{0,1},{1,0},{2,3},{3,2},{4,5},{5,4},{6,7},{7,6},{8,9},{9,8},{10,11... | collective-permute-start | bytes 1572872 | tf_op jit(solution)/shard_map/ppermute | solution.py:54
  25.3 14.8 %collective-permute-start.3 = (f32[1472,128]{1,0:T(8,128)S(1)}, f32[1472,128]{1,0:T(8,128)S(1)}, u32[]{:S(2)}, u32[]{:S(2)}) collective-permute-start(f32[1472,128]{1,0:T(8,128)S(1)} %pad_maximum_fusion), channel_id=1, source_target_pairs={{0,32},{1,2},{2,1},{3,4},{4,3},{5,6},{6,5},{7,8},{8,7},{9,10},{10,... | collective-permute-start | bytes 2261000 | tf_op jit(solution)/shard_map/ppermute | solution.py:58
  40.2 1.6 collective-permute-start.4
  68.2 1.5 collective-permute-start.5
  70.3 8.9 %collective-permute-start.6 = (f32[4,12,8,128]{3,2,1,0:T(8,128)S(1)}, f32[4,12,8,128]{3,2,1,0:T(8,128)S(1)}, u32[]{:S(2)}, u32[]{:S(2)}) collective-permute-start(f32[4,12,8,128]{3,2,1,0:T(8,128)S(1)} %get-tuple-element.29), channel_id=1, source_target_pairs={{0,32},{1,2},{2,1},{3,4},{4,3},{5,6},{6,5},{7,8},{8,7},{9,10},{10,... | collective-permute-start | bytes 589832 | tf_op jit(solution)/shard_map/ppermute | solution.py:58
  72.7 8.7 %collective-permute-start.8 = (f32[4,128,128]{2,1,0:T(8,128)S(1)}, f32[4,128,128]{2,1,0:T(8,128)S(1)}, u32[]{:S(2)}, u32[]{:S(2)}) collective-permute-start(f32[4,128,128]{2,1,0:T(8,128)S(1)} %get-tuple-element.30), channel_id=1, source_target_pairs={{0,16},{16,32},{32,48},{48,64},{64,80},{80,96},{96,112},{112,128},... | collective-permute-start | bytes 786440 | tf_op jit(solution)/shard_map/ppermute | solution.py:503
  79.2 1.4 collective-permute-start.7
  81.3 9.7 %collective-permute-start.9 = (f32[4,31,8,128]{3,2,1,0:T(8,128)S(1)}, f32[4,31,8,128]{3,2,1,0:T(8,128)S(1)}, u32[]{:S(2)}, u32[]{:S(2)}) collective-permute-start(f32[4,31,8,128]{3,2,1,0:T(8,128)S(1)} %shard_map.49), channel_id=1, source_target_pairs={{0,225},{1,16},{2,227},{3,18},{4,229},{5,20},{6,231},{7,22},{8,233... | collective-permute-start | bytes 1523720 | tf_op jit(solution)/shard_map/ppermute | solution.py:62
  91.1 1.9 %collective-permute-start.10 = (f32[4,31,8,128]{3,2,1,0:T(8,128)S(1)}, f32[4,31,8,128]{3,2,1,0:T(8,128)S(1)}, u32[]{:S(2)}, u32[]{:S(2)}) collective-permute-start(f32[4,31,8,128]{3,2,1,0:T(8,128)S(1)} %collective-permute-done.9.yg), channel_id=1, source_target_pairs={{0,1},{1,0},{2,3},{3,2},{4,5},{5,4},{6,7},{7,6},{8,9},{9,8},{10,11... | collective-permute-start | bytes 1523720 | tf_op jit(solution)/shard_map/ppermute | solution.py:54
  97.4 7.0 %collective-permute-start.11 = (f32[8,8,128]{2,1,0:T(8,128)S(1)}, f32[8,8,128]{2,1,0:T(8,128)S(1)}, u32[]{:S(2)}, u32[]{:S(2)}) collective-permute-start(f32[8,8,128]{2,1,0:T(8,128)S(1)} %get-tuple-element.33.c_in), channel_id=1, source_target_pairs={{0,32},{1,2},{2,1},{3,4},{4,3},{5,6},{6,5},{7,8},{8,7},{9,10},{10,... | collective-permute-start | bytes 98312 | tf_op jit(solution)/shard_map/ppermute | solution.py:58
  104.5 1.2 collective-permute-start.12
  105.7 5.3 %collective-permute-start.13 = (f32[24,8,128]{2,1,0:T(8,128)S(1)}, f32[24,8,128]{2,1,0:T(8,128)S(1)}, u32[]{:S(2)}, u32[]{:S(2)}) collective-permute-start(f32[24,8,128]{2,1,0:T(8,128)S(1)} %pad_maximum_fusion.3), channel_id=1, source_target_pairs={{0,225},{1,16},{2,227},{3,18},{4,229},{5,20},{6,231},{7,22},{8,233... | collective-permute-start | bytes 294920 | tf_op jit(solution)/shard_map/ppermute | solution.py:62
  111.0 1.3 collective-permute-start.14
  114.3 7.0 %collective-permute-start.15 = (f32[8,8,128]{2,1,0:T(8,128)S(1)}, f32[8,8,128]{2,1,0:T(8,128)S(1)}, u32[]{:S(2)}, u32[]{:S(2)}) collective-permute-start(f32[8,8,128]{2,1,0:T(8,128)S(1)} %get-tuple-element.38.c_in), channel_id=1, source_target_pairs={{0,32},{1,2},{2,1},{3,4},{4,3},{5,6},{6,5},{7,8},{8,7},{9,10},{10,... | collective-permute-start | bytes 98312 | tf_op jit(solution)/shard_map/ppermute | solution.py:58
  121.4 1.2 collective-permute-start.16
  122.6 5.3 %collective-permute-start.17 = (f32[24,8,128]{2,1,0:T(8,128)S(1)}, f32[24,8,128]{2,1,0:T(8,128)S(1)}, u32[]{:S(2)}, u32[]{:S(2)}) collective-permute-start(f32[24,8,128]{2,1,0:T(8,128)S(1)} %pad_maximum_fusion.4), channel_id=1, source_target_pairs={{0,225},{1,16},{2,227},{3,18},{4,229},{5,20},{6,231},{7,22},{8,233... | collective-permute-start | bytes 294920 | tf_op jit(solution)/shard_map/ppermute | solution.py:62
  127.9 1.3 collective-permute-start.18
  131.2 7.0 %collective-permute-start.19 = (f32[8,8,128]{2,1,0:T(8,128)S(1)}, f32[8,8,128]{2,1,0:T(8,128)S(1)}, u32[]{:S(2)}, u32[]{:S(2)}) collective-permute-start(f32[8,8,128]{2,1,0:T(8,128)S(1)} %get-tuple-element.40.c_in), channel_id=1, source_target_pairs={{0,32},{1,2},{2,1},{3,4},{4,3},{5,6},{6,5},{7,8},{8,7},{9,10},{10,... | collective-permute-start | bytes 98312 | tf_op jit(solution)/shard_map/ppermute | solution.py:58
  138.3 1.2 collective-permute-start.20
  139.5 5.3 %collective-permute-start.21 = (f32[24,8,128]{2,1,0:T(8,128)S(1)}, f32[24,8,128]{2,1,0:T(8,128)S(1)}, u32[]{:S(2)}, u32[]{:S(2)}) collective-permute-start(f32[24,8,128]{2,1,0:T(8,128)S(1)} %pad_maximum_fusion.5), channel_id=1, source_target_pairs={{0,225},{1,16},{2,227},{3,18},{4,229},{5,20},{6,231},{7,22},{8,233... | collective-permute-start | bytes 294920 | tf_op jit(solution)/shard_map/ppermute | solution.py:62
  144.8 1.3 collective-permute-start.22

commit v5 on v4

--- a/solution.py
+++ b/solution.py
@@ -293,7 +293,26 @@
 
 HALOS = (6, 4, 2)
 STARTS = (0, 6, 10, 12)
-Y_STARTS = (0, 20, 28, 31)
+
+
+def y_pieces():
+    wanted = []
+    for i, h in enumerate(HALOS):
+        for l in range(8 + 2 * h):
+            rows = h - max(h - l, l - h - 7, 0)
+            if rows:
+                wanted.append((rows, i, l))
+    room, pieces = [], []
+    for rows, i, l in sorted(wanted, reverse=True):
+        tile = next((k for k, free in enumerate(room) if free >= rows), len(room))
+        if tile == len(room):
+            room.append(8)
+        pieces.append((i, l, rows, tile, 8 - room[tile]))
+        room[tile] -= rows
+    return pieces, len(room)
+
+
+PIECES, Y_TILES = y_pieces()
 
 
 def half(core, value):
@@ -326,22 +345,16 @@
 def rows_kernel(flags, chip, got, swap, send):
     def run(left, right, upward):
         for q in range(4):
-            for i, h in enumerate(HALOS):
-                rows = 8 >> i
+            for i, l, rows, tile, first in PIECES:
+                h, a = HALOS[i], STARTS[i]
                 pick = slice(8 - rows, 8) if upward else slice(0, rows)
-                a = STARTS[i]
-
-                def layer(l):
-                    if l < h:
-                        return left[q, a + l, pick]
-                    if l < h + 8:
-                        return chip[4 * q + i, l - h, pick]
-                    return right[q, a + l - h - 8, pick]
-
-                per = 8 // rows
-                for l in range(8 + 2 * h):
-                    k = l % per
-                    send[q, Y_STARTS[i] + l // per, rows * k : rows * k + rows] = layer(l)
+                if l < h:
+                    value = left[q, a + l, pick]
+                elif l < h + 8:
+                    value = chip[4 * q + i, l - h, pick]
+                else:
+                    value = right[q, a + l - h - 8, pick]
+                send[q, tile, first : first + rows] = value
 
     @pl.when(flags[1] % 2 == 0)
     def _():
@@ -352,28 +365,27 @@
         run(swap, got, True)
 
 
-def quads_kernel(flags, cond, chip, xg, xs, yg, ys, p_out, zp_out, ends, last, done, b0, b1, b2, *coef):
+def quads_kernel(groups, flags, cond, chip, xg, xs, yg, ys, *refs):
+    outs, (b0, b1, b2), coef = refs[:-8], refs[-8:-5], refs[-5:]
     core = flags[1] % 2
     for value, ref in zip(region(flags, cond, 6), coef):
         ref[...] = value
-    b1[...] = jnp.zeros((16, 24, 128), jnp.float32)
-    b2[...] = jnp.zeros((12, 24, 128), jnp.float32)
+    for h, buf in zip(HALOS, (b0, b1, b2)):
+        buf[...] = jnp.zeros((8 + 2 * h, 24, 128), jnp.float32)
     c = tuple(r[...] for r in coef)
     zero = jnp.zeros((4, 8, 128), jnp.float32)
-    for q in range(4):
+    for q in groups:
 
         def fill(left, right, below, above):
             for i, (h, buf) in enumerate(zip(HALOS, (b0, b1, b2))):
-                a, rows = STARTS[i], 8 >> i
+                a = STARTS[i]
                 buf[h : h + 8, 8:16] = chip[4 * q + i]
                 buf[0:h, 8:16] = left[q, a : a + h]
                 buf[h + 8 :, 8:16] = right[q, a : a + h]
-                per = 8 // rows
-                for l in range(8 + 2 * h):
-                    k = rows * (l % per)
-                    at = Y_STARTS[i] + l // per
-                    buf[l, 8 - rows : 8] = below[q, at, k : k + rows]
-                    buf[l, 16 : 16 + rows] = above[q, at, k : k + rows]
+            for i, l, rows, tile, first in PIECES:
+                buf = (b0, b1, b2)[i]
+                buf[l, 8 - rows : 8] = below[q, tile, first : first + rows]
+                buf[l, 16 : 16 + rows] = above[q, tile, first : first + rows]
 
         @pl.when(core == 0)
         def _():
@@ -395,17 +407,18 @@
                 values.append(p[h - 2 : h + 6, 8:16])
             else:
                 values.append(two[:, 8:16] + chip[4 * q + 3])
-        for i in range(4):
-            if q == 0:
+        if q == 0:
+            last, done = outs
+            last[...] = values[3]
+            for i in range(4):
                 done[i, 0] = partial[i]
                 done[i, 1] = half(core, values[i])
-            else:
+        else:
+            p_out, zp_out, ends = outs
+            ends[q - 1] = values[3]
+            for i in range(4):
                 p_out[4 * q - 4 + i] = half(core, values[i])
                 zp_out[4 * q - 4 + i] = partial[i]
-        if q == 0:
-            last[...] = values[3]
-        else:
-            ends[q - 1] = values[3]
 
 
 def chain_kernel(q, flags, cond, c_in, p, zp, ends, xg, xs, yg, ys, last, done, buf, *coef):
@@ -455,7 +468,7 @@
     return [pltpu.VMEM((count, 24, 128), jnp.float32) for count in counts]
 
 
-def call(kernel, outs, scratches, *args, smem=True):
+def call(kernel, outs, scratches, *args, smem=True, cost=None):
     specs = [SMEM] + [VMEM] * (len(args) - 1) if smem else [VMEM] * len(args)
     return pl.pallas_call(
         kernel,
@@ -464,6 +477,7 @@
         out_specs=[VMEM] * len(outs),
         scratch_shapes=scratches,
         compiler_params=params(),
+        cost_estimate=cost,
     )(*args)
 
 
@@ -505,26 +519,30 @@
     chips, send = call(chips_kernel, [struct(NT, 8, 8, 128), struct(4, 12, 8, 128)], [], flags, own, other)
     xg = odd(send)
     xs = even(xg)
-    (send,) = call(rows_kernel, [struct(4, 31, 8, 128)], [], flags, chips, xg, xs)
+    (send,) = call(rows_kernel, [struct(4, Y_TILES, 8, 128)], [], flags, chips, xg, xs)
     send, w_before = lax.optimization_barrier((send, w_before))
     yg = yodd(send)
     ys = even(yg)
     regions = [pltpu.VMEM((8 + 2 * h, 24, 128), jnp.float32) for h in HALOS]
-    p, zp, ends, last, done = call(
-        quads_kernel,
-        [
-            struct(12, 4, 8, 128),
-            struct(12, 4, 8, 128),
-            struct(3, 8, 8, 128),
-            struct(8, 8, 128),
-            struct(4, 2, 4, 8, 128),
-        ],
-        regions + coefficient_scratch(6),
+    quad_scratch = regions + coefficient_scratch(6)
+    last, done = call(
+        functools.partial(quads_kernel, (0,)),
+        [struct(8, 8, 128), struct(4, 2, 4, 8, 128)],
+        quad_scratch,
         flags, tiles, chips, xg, xs, yg, ys,
+    )
+    p, zp, ends = call(
+        functools.partial(quads_kernel, (1, 2, 3)),
+        [struct(12, 4, 8, 128), struct(12, 4, 8, 128), struct(3, 8, 8, 128)],
+        quad_scratch,
+        flags, tiles, chips, xg, xs, yg, ys,
+        cost=pl.CostEstimate(flops=30_000_000, bytes_accessed=4_000_000, transcendentals=0),
     )
     parts = [done]
     for q in (1, 2, 3):
         xg = odd(last)
+        if q == 1:
+            xg, p, zp, ends = lax.optimization_barrier((xg, p, zp, ends))
         xs = even(xg)
         left = jnp.where(core == 0, xg, xs)
         right = jnp.where(core == 0, xs, xg)

time: 171 us -> 166 us (0.971)
  waiting for transfers between devices: 90.1 us -> 83.9 us
    ppermute x6, waiting for transfers between devices: 49.1 us -> 45.5 us  [odd(): return lax.ppermute(x, ('tm', 'space'), ODD)]
    ppermute x4, waiting for transfers between devices: 25.3 us -> 23.1 us  [yodd(): return lax.ppermute(x, ('tm', 'space'), YODD)]
    pallas_call x9 -> x10, Pallas kernels: 22 us -> 22.8 us  [call(): pl.pallas_call(kernel, out_shape=outs, in_specs=specs, out_specs=[VMEM] *...]
  transfers between devices with their start and end apart: 23 -> 23, of which waited for: 21 -> 21; matrix products, arithmetic and copies ran while one was open for 0% -> 0% of each run, Pallas kernels for 0% -> 3%
where the time goes in v5:
time: 166 us; the launch traced here: 165 us
  waiting for transfers between devices  83.9 us (51%)
  blocking collectives  42.5 us (26%)
  Pallas kernels  22.8 us (14%)
  starting transfers between devices  14.1 us (8%)
  other arithmetic  1.72 us (1%)
    ppermute x6, waiting for transfers between devices, odd(): return lax.ppermute(x, ('tm', 'space'), ODD)  45.5 us
    ppermute x4, waiting for transfers between devices, yodd(): return lax.ppermute(x, ('tm', 'space'), YODD)  23.1 us
    pallas_call x10, Pallas kernels, call(): pl.pallas_call(kernel, out_shape=outs, in_specs=specs, out_specs=[VMEM] *...  22.8 us
    all_to_all x1, blocking collectives, body(): own = lax.all_to_all(e, 'tm', 0, 0)  21.4 us
    all_to_all x1, blocking collectives, body(): back = lax.all_to_all(jnp.concatenate(parts), 'tm', 0, 0)  21.1 us
    ppermute x12, waiting for transfers between devices, even(): return lax.ppermute(x, 'space', EVEN)  15.3 us
    ppermute x6, starting transfers between devices, odd(): return lax.ppermute(x, ('tm', 'space'), ODD)  12.3 us
  transfers between devices with their start and end apart: 23, of which 21 were waited for; matrix products, arithmetic and copies ran while one was open for 0% of the time, Pallas kernels for 3%

profile of v5, /device:TPU:16, one launch (start us, length us, event | category | flops | bytes accessed | tf_op | source)
XLA Modules:
  0.0 165.4 jit_solution(13729285048351643574)
XLA Ops:
  0.0 1.4 maximum_select_fusion.pack
  1.4 2.1 %collective-permute-start.1 = (f32[4,4,128,128]{3,2,1,0:T(8,128)S(1)}, f32[4,4,128,128]{3,2,1,0:T(8,128)S(1)}, u32[]{:S(2)}, u32[]{:S(2)}) collective-permute-start(f32[4,4,128,128]{3,2,1,0:T(8,128)S(1)} %maximum_select_fusion.pack), channel_id=1, source_target_pairs={{0,32},{1,2},{2,1},{3,4},{4,3},{5,6},{6,5},{7,8},{8,7},{9,10},{10,... | collective-permute-start | bytes 3145736 | tf_op jit(solution)/shard_map/ppermute | solution.py:58
  3.5 0.0 collective-permute-start
  3.5 0.1 pad_add_fusion.flags
  3.6 15.7 %collective-permute-done.1.od.odc = f32[4,4,128,128]{3,2,1,0:T(8,128)S(1)} collective-permute-done((f32[4,4,128,128]{3,2,1,0:T(8,128)S(1)}, f32[4,4,128,128]{3,2,1,0:T(8,128)S(1)}, u32[]{:S(2)}, u32[]{:S(2)}) %collective-permute-start.1) | collective-permute-done | bytes 1048608 | tf_op jit(solution)/shard_map/ppermute | solution.py:58
  19.4 0.0 collective-permute-done.ev.evc
  19.4 3.9 %shard_map.46.a = f32[2,4,128,128]{3,2,1,0:T(8,128)S(1)} custom-call(s32[4]{0:T(128)S(1)} %pad_add_fusion.flags, f32[4,4,128,128]{3,2,1,0:T(8,128)S(1)} %maximum_select_fusion.pack, f32[4,4,128,128]{3,2,1,0:T(8,128)S(1)} %collective-permute-done.ev.evc, f32[4,4,128,128]{3,2,1,0:T(8,128)S(1)} %collective-permute-done.1.od.odc), custom_call_target="tpu_custom_call" | custom-call | tf_op jit(solution)/shard_map/pallas_call | solution.py:473
  23.3 0.1 collective-permute-start.2
  23.5 1.8 %collective-permute-done.2.ev = f32[2,4,128,128]{3,2,1,0:T(8,128)S(1)} collective-permute-done((f32[2,4,128,128]{3,2,1,0:T(8,128)S(1)}, f32[2,4,128,128]{3,2,1,0:T(8,128)S(1)}, u32[]{:S(2)}, u32[]{:S(2)}) %collective-permute-start.2) | collective-permute-done | bytes 524320 | tf_op jit(solution)/shard_map/ppermute | solution.py:54
  25.3 0.1 pad_maximum_fusion
  25.3 2.1 %collective-permute-start.3 = (f32[1472,128]{1,0:T(8,128)S(1)}, f32[1472,128]{1,0:T(8,128)S(1)}, u32[]{:S(2)}, u32[]{:S(2)}) collective-permute-start(f32[1472,128]{1,0:T(8,128)S(1)} %pad_maximum_fusion), channel_id=1, source_target_pairs={{0,32},{1,2},{2,1},{3,4},{4,3},{5,6},{6,5},{7,8},{8,7},{9,10},{10,... | collective-permute-start | bytes 2261000 | tf_op jit(solution)/shard_map/ppermute | solution.py:58
  27.4 12.7 %collective-permute-done.3.od = f32[1472,128]{1,0:T(8,128)S(1)} collective-permute-done((f32[1472,128]{1,0:T(8,128)S(1)}, f32[1472,128]{1,0:T(8,128)S(1)}, u32[]{:S(2)}, u32[]{:S(2)}) %collective-permute-start.3) | collective-permute-done | bytes 753696 | tf_op jit(solution)/shard_map/ppermute | solution.py:58
  40.2 0.1 collective-permute-start.4
  40.3 1.5 collective-permute-done.4.ev5
  41.7 5.1 %shard_map.47 = (f32[16,4,8,128]{3,2,1,0:T(8,128)S(1)}, f32[4,128,128]{2,1,0:T(8,128)S(1)}, f32[24,24,128]{2,1,0:T(8,128)S(1)}) custom-call(s32[4]{0:T(128)S(1)} %pad_add_fusion.flags, f32[2,4,128,128]{3,2,1,0:T(8,128)S(1)} %shard_map.46.a, f32[4,4,128,128]{3,2,1,0:T(8,128)S(1)} %maximum_select_fusion.pack, ...), custom_call_target="tpu_custom_call" | custom-call | tf_op jit(solution)/shard_map/pallas_call | solution.py:473
  46.8 21.4 %all_to_all.10.own = f32[16,4,8,128]{3,2,1,0:T(8,128)S(1)} all-to-all(f32[16,4,8,128]{3,2,1,0:T(8,128)S(1)} %get-tuple-element.29), channel_id=1, replica_groups=mesh['tm'=16,'space'=16] {'tm'}, dimensions={0} | all-to-all | bytes 524288 | tf_op jit(solution)/shard_map/all_to_all | solution.py:515
  68.2 0.0 collective-permute-start.5
  68.2 1.5 collective-permute-done.5.other
  69.7 0.6 shard_map.48
  70.3 2.3 %collective-permute-start.6 = (f32[4,12,8,128]{3,2,1,0:T(8,128)S(1)}, f32[4,12,8,128]{3,2,1,0:T(8,128)S(1)}, u32[]{:S(2)}, u32[]{:S(2)}) collective-permute-start(f32[4,12,8,128]{3,2,1,0:T(8,128)S(1)} %get-tuple-element.33), channel_id=1, source_target_pairs={{0,32},{1,2},{2,1},{3,4},{4,3},{5,6},{6,5},{7,8},{8,7},{9,10},{10,... | collective-permute-start | bytes 589832 | tf_op jit(solution)/shard_map/ppermute | solution.py:58
  72.7 1.3 collective-permute-start.8
  73.9 5.3 %collective-permute-done.6.got.xg = f32[4,12,8,128]{3,2,1,0:T(8,128)S(1)} collective-permute-done((f32[4,12,8,128]{3,2,1,0:T(8,128)S(1)}, f32[4,12,8,128]{3,2,1,0:T(8,128)S(1)}, u32[]{:S(2)}, u32[]{:S(2)}) %collective-permute-start.6) | collective-permute-done | bytes 196640 | tf_op jit(solution)/shard_map/ppermute | solution.py:58
  79.2 0.0 collective-permute-start.7
  79.3 1.4 collective-permute-done.7.swap.xs
  80.7 0.6 shard_map.49
  81.3 0.0 collective-permute-done.8.w
  81.3 0.1 collective-permute-start.9
  81.4 7.3 %collective-permute-done.9.yg = f32[4,18,8,128]{3,2,1,0:T(8,128)S(1)} collective-permute-done((f32[4,18,8,128]{3,2,1,0:T(8,128)S(1)}, f32[4,18,8,128]{3,2,1,0:T(8,128)S(1)}, u32[]{:S(2)}, u32[]{:S(2)}) %collective-permute-start.9) | collective-permute-done | bytes 294944 | tf_op jit(solution)/shard_map/ppermute | solution.py:62
  88.8 0.0 collective-permute-start.10
  88.8 1.6 collective-permute-done.10.ys
  90.4 1.7 %shard_map.50 = (f32[8,8,128]{2,1,0:T(8,128)S(1)}, f32[4,2,4,8,128]{4,3,2,1,0:T(8,128)S(1)}) custom-call(s32[4]{0:T(128)S(1)} %pad_add_fusion.flags, f32[24,24,128]{2,1,0:T(8,128)S(1)} %get-tuple-element.28.cond, f32[16,8,8,128]{3,2,1,0:T(8,128)S(1)} %get-tuple-element.32.chip, f32[4,12,8,128]{3,2,1,0:T(8,128)S(1)} %collective-permute-done.6.got.xg, ...), custom_call_target="tpu_custom_call" | custom-call | tf_op jit(solution)/shard_map/pallas_call | solution.py:473
  92.0 2.1 %collective-permute-start.11 = (f32[8,8,128]{2,1,0:T(8,128)S(1)}, f32[8,8,128]{2,1,0:T(8,128)S(1)}, u32[]{:S(2)}, u32[]{:S(2)}) collective-permute-start(f32[8,8,128]{2,1,0:T(8,128)S(1)} %get-tuple-element.37.c_in), channel_id=1, source_target_pairs={{0,32},{1,2},{2,1},{3,4},{4,3},{5,6},{6,5},{7,8},{8,7},{9,10},{10,... | collective-permute-start | bytes 98312 | tf_op jit(solution)/shard_map/ppermute | solution.py:58
  94.1 3.5 %shard_map.51 = (f32[12,4,8,128]{3,2,1,0:T(8,128)S(1)}, f32[12,4,8,128]{3,2,1,0:T(8,128)S(1)}, f32[3,8,8,128]{3,2,1,0:T(8,128)S(1)}) custom-call(s32[4]{0:T(128)S(1)} %pad_add_fusion.flags, f32[24,24,128]{2,1,0:T(8,128)S(1)} %get-tuple-element.28.cond, f32[16,8,8,128]{3,2,1,0:T(8,128)S(1)} %get-tuple-element.32.chip, ...), custom_call_target="tpu_custom_call" | custom-call | flops 30000000 | bytes 4000000 | tf_op jit(solution)/shard_map/pallas_call | solution.py:473
  97.7 1.4 collective-permute-done.11.xg
  99.1 0.0 collective-permute-start.12
  99.1 1.2 collective-permute-done.12.xs
  100.3 0.1 collective-permute-start.13
  100.4 5.2 %collective-permute-done.13.yg = f32[24,8,128]{2,1,0:T(8,128)S(1)} collective-permute-done((f32[24,8,128]{2,1,0:T(8,128)S(1)}, f32[24,8,128]{2,1,0:T(8,128)S(1)}, u32[]{:S(2)}, u32[]{:S(2)}) %collective-permute-start.13) | collective-permute-done | bytes 98336 | tf_op jit(solution)/shard_map/ppermute | solution.py:62
  105.7 0.0 collective-permute-start.14
  105.7 1.3 collective-permute-done.14.ys
  107.0 2.0 %shard_map.52 = (f32[8,8,128]{2,1,0:T(8,128)S(1)}, f32[4,2,4,8,128]{4,3,2,1,0:T(8,128)S(1)}) custom-call(s32[4]{0:T(128)S(1)} %pad_add_fusion.flags, f32[24,24,128]{2,1,0:T(8,128)S(1)} %get-tuple-element.28.cond, f32[8,8,128]{2,1,0:T(8,128)S(1)} %get-tuple-element.37.c_in, f32[12,4,8,128]{3,2,1,0:T(8,128)S(1)} %get-tuple-element.41.p, ...), custom_call_target="tpu_custom_call" | custom-call | tf_op jit(solution)/shard_map/pallas_call | solution.py:473
  108.9 2.0 %collective-permute-start.15 = (f32[8,8,128]{2,1,0:T(8,128)S(1)}, f32[8,8,128]{2,1,0:T(8,128)S(1)}, u32[]{:S(2)}, u32[]{:S(2)}) collective-permute-start(f32[8,8,128]{2,1,0:T(8,128)S(1)} %get-tuple-element.46.c_in), channel_id=1, source_target_pairs={{0,32},{1,2},{2,1},{3,4},{4,3},{5,6},{6,5},{7,8},{8,7},{9,10},{10,... | collective-permute-start | bytes 98312 | tf_op jit(solution)/shard_map/ppermute | solution.py:58
  110.9 5.1 %collective-permute-done.15.xg = f32[8,8,128]{2,1,0:T(8,128)S(1)} collective-permute-done((f32[8,8,128]{2,1,0:T(8,128)S(1)}, f32[8,8,128]{2,1,0:T(8,128)S(1)}, u32[]{:S(2)}, u32[]{:S(2)}) %collective-permute-start.15) | collective-permute-done | bytes 32800 | tf_op jit(solution)/shard_map/ppermute | solution.py:58
  116.0 0.0 collective-permute-start.16
  116.0 1.2 collective-permute-done.16.xs
  117.2 0.1 collective-permute-start.17
  117.3 5.2 %collective-permute-done.17.yg = f32[24,8,128]{2,1,0:T(8,128)S(1)} collective-permute-done((f32[24,8,128]{2,1,0:T(8,128)S(1)}, f32[24,8,128]{2,1,0:T(8,128)S(1)}, u32[]{:S(2)}, u32[]{:S(2)}) %collective-permute-start.17) | collective-permute-done | bytes 98336 | tf_op jit(solution)/shard_map/ppermute | solution.py:62
  122.5 0.0 collective-permute-start.18
  122.6 1.3 collective-permute-done.18.ys
  123.9 2.0 %shard_map.53 = (f32[8,8,128]{2,1,0:T(8,128)S(1)}, f32[4,2,4,8,128]{4,3,2,1,0:T(8,128)S(1)}) custom-call(s32[4]{0:T(128)S(1)} %pad_add_fusion.flags, f32[24,24,128]{2,1,0:T(8,128)S(1)} %get-tuple-element.28.cond, f32[8,8,128]{2,1,0:T(8,128)S(1)} %get-tuple-element.46.c_in, f32[12,4,8,128]{3,2,1,0:T(8,128)S(1)} %get-tuple-element.41.p, ...), custom_call_target="tpu_custom_call" | custom-call | tf_op jit(solution)/shard_map/pallas_call | solution.py:473
  125.8 1.8 %collective-permute-start.19 = (f32[8,8,128]{2,1,0:T(8,128)S(1)}, f32[8,8,128]{2,1,0:T(8,128)S(1)}, u32[]{:S(2)}, u32[]{:S(2)}) collective-permute-start(f32[8,8,128]{2,1,0:T(8,128)S(1)} %get-tuple-element.48.c_in), channel_id=1, source_target_pairs={{0,32},{1,2},{2,1},{3,4},{4,3},{5,6},{6,5},{7,8},{8,7},{9,10},{10,... | collective-permute-start | bytes 98312 | tf_op jit(solution)/shard_map/ppermute | solution.py:58
  127.6 5.2 %collective-permute-done.19.xg = f32[8,8,128]{2,1,0:T(8,128)S(1)} collective-permute-done((f32[8,8,128]{2,1,0:T(8,128)S(1)}, f32[8,8,128]{2,1,0:T(8,128)S(1)}, u32[]{:S(2)}, u32[]{:S(2)}) %collective-permute-start.19) | collective-permute-done | bytes 32800 | tf_op jit(solution)/shard_map/ppermute | solution.py:58
  132.9 0.0 collective-permute-start.20
  132.9 1.2 collective-permute-done.20.xs
  134.1 0.1 collective-permute-start.21
  134.2 5.2 %collective-permute-done.21.yg = f32[24,8,128]{2,1,0:T(8,128)S(1)} collective-permute-done((f32[24,8,128]{2,1,0:T(8,128)S(1)}, f32[24,8,128]{2,1,0:T(8,128)S(1)}, u32[]{:S(2)}, u32[]{:S(2)}) %collective-permute-start.21) | collective-permute-done | bytes 98336 | tf_op jit(solution)/shard_map/ppermute | solution.py:62
  139.4 0.0 collective-permute-start.22
  139.4 1.3 collective-permute-done.22.ys
  140.7 2.6 %shard_map.54 = (f32[8,8,128]{2,1,0:T(8,128)}, f32[4,2,4,8,128]{4,3,2,1,0:T(8,128)S(1)}) custom-call(s32[4]{0:T(128)S(1)} %pad_add_fusion.flags, f32[24,24,128]{2,1,0:T(8,128)S(1)} %get-tuple-element.28.cond, f32[8,8,128]{2,1,0:T(8,128)S(1)} %get-tuple-element.48.c_in, f32[12,4,8,128]{3,2,1,0:T(8,128)S(1)} %get-tuple-element.41.p, ...), custom_call_target="tpu_custom_call" | custom-call | tf_op jit(solution)/shard_map/pallas_call | solution.py:473
  143.4 21.1 %all_to_all.11.got = f32[16,2,4,8,128]{4,3,2,1,0:T(8,128)S(1)} all-to-all(f32[16,2,4,8,128]{4,3,2,1,0:T(8,128)S(1)} %pad_maximum_fusion.1), channel_id=1, replica_groups=mesh['tm'=16,'space'=16] {'tm'}, dimensions={0} | all-to-all | bytes 1048576 | tf_op jit(solution)/shard_map/all_to_all | solution.py:558
  164.5 0.9 shard_map.55
  (19 shorter events, 0.2 us)
Async XLA Ops:
  1.4 17.9 %collective-permute-start.1 = (f32[4,4,128,128]{3,2,1,0:T(8,128)S(1)}, f32[4,4,128,128]{3,2,1,0:T(8,128)S(1)}, u32[]{:S(2)}, u32[]{:S(2)}) collective-permute-start(f32[4,4,128,128]{3,2,1,0:T(8,128)S(1)} %maximum_select_fusion.pack), channel_id=1, source_target_pairs={{0,32},{1,2},{2,1},{3,4},{4,3},{5,6},{6,5},{7,8},{8,7},{9,10},{10,... | collective-permute-start | bytes 3145736 | tf_op jit(solution)/shard_map/ppermute | solution.py:58
  3.5 15.9 %collective-permute-start = (f32[4,4,128,128]{3,2,1,0:T(8,128)S(1)}, f32[4,4,128,128]{3,2,1,0:T(8,128)S(1)}, u32[]{:S(2)}, u32[]{:S(2)}) collective-permute-start(f32[4,4,128,128]{3,2,1,0:T(8,128)S(1)} %maximum_select_fusion.pack), channel_id=1, source_target_pairs={{0,1},{1,0},{2,3},{3,2},{4,5},{5,4},{6,7},{7,6},{8,9},{9,8},{10,11... | collective-permute-start | bytes 3145736 | tf_op jit(solution)/shard_map/ppermute | solution.py:54
  23.3 2.0 %collective-permute-start.2 = (f32[2,4,128,128]{3,2,1,0:T(8,128)S(1)}, f32[2,4,128,128]{3,2,1,0:T(8,128)S(1)}, u32[]{:S(2)}, u32[]{:S(2)}) collective-permute-start(f32[2,4,128,128]{3,2,1,0:T(8,128)S(1)} %shard_map.46.a), channel_id=1, source_target_pairs={{0,1},{1,0},{2,3},{3,2},{4,5},{5,4},{6,7},{7,6},{8,9},{9,8},{10,11... | collective-permute-start | bytes 1572872 | tf_op jit(solution)/shard_map/ppermute | solution.py:54
  25.3 14.8 %collective-permute-start.3 = (f32[1472,128]{1,0:T(8,128)S(1)}, f32[1472,128]{1,0:T(8,128)S(1)}, u32[]{:S(2)}, u32[]{:S(2)}) collective-permute-start(f32[1472,128]{1,0:T(8,128)S(1)} %pad_maximum_fusion), channel_id=1, source_target_pairs={{0,32},{1,2},{2,1},{3,4},{4,3},{5,6},{6,5},{7,8},{8,7},{9,10},{10,... | collective-permute-start | bytes 2261000 | tf_op jit(solution)/shard_map/ppermute | solution.py:58
  40.2 1.6 collective-permute-start.4
  68.2 1.5 collective-permute-start.5
  70.3 8.9 %collective-permute-start.6 = (f32[4,12,8,128]{3,2,1,0:T(8,128)S(1)}, f32[4,12,8,128]{3,2,1,0:T(8,128)S(1)}, u32[]{:S(2)}, u32[]{:S(2)}) collective-permute-start(f32[4,12,8,128]{3,2,1,0:T(8,128)S(1)} %get-tuple-element.33), channel_id=1, source_target_pairs={{0,32},{1,2},{2,1},{3,4},{4,3},{5,6},{6,5},{7,8},{8,7},{9,10},{10,... | collective-permute-start | bytes 589832 | tf_op jit(solution)/shard_map/ppermute | solution.py:58
  72.7 8.7 %collective-permute-start.8 = (f32[4,128,128]{2,1,0:T(8,128)S(1)}, f32[4,128,128]{2,1,0:T(8,128)S(1)}, u32[]{:S(2)}, u32[]{:S(2)}) collective-permute-start(f32[4,128,128]{2,1,0:T(8,128)S(1)} %get-tuple-element.34), channel_id=1, source_target_pairs={{0,16},{16,32},{32,48},{48,64},{64,80},{80,96},{96,112},{112,128},... | collective-permute-start | bytes 786440 | tf_op jit(solution)/shard_map/ppermute | solution.py:517
  79.2 1.4 collective-permute-start.7
  81.3 7.4 %collective-permute-start.9 = (f32[4,18,8,128]{3,2,1,0:T(8,128)S(1)}, f32[4,18,8,128]{3,2,1,0:T(8,128)S(1)}, u32[]{:S(2)}, u32[]{:S(2)}) collective-permute-start(f32[4,18,8,128]{3,2,1,0:T(8,128)S(1)} %shard_map.49), channel_id=1, source_target_pairs={{0,225},{1,16},{2,227},{3,18},{4,229},{5,20},{6,231},{7,22},{8,233... | collective-permute-start | bytes 884744 | tf_op jit(solution)/shard_map/ppermute | solution.py:62
  88.8 1.6 collective-permute-start.10
  92.0 7.0 %collective-permute-start.11 = (f32[8,8,128]{2,1,0:T(8,128)S(1)}, f32[8,8,128]{2,1,0:T(8,128)S(1)}, u32[]{:S(2)}, u32[]{:S(2)}) collective-permute-start(f32[8,8,128]{2,1,0:T(8,128)S(1)} %get-tuple-element.37.c_in), channel_id=1, source_target_pairs={{0,32},{1,2},{2,1},{3,4},{4,3},{5,6},{6,5},{7,8},{8,7},{9,10},{10,... | collective-permute-start | bytes 98312 | tf_op jit(solution)/shard_map/ppermute | solution.py:58
  99.1 1.2 collective-permute-start.12
  100.3 5.3 %collective-permute-start.13 = (f32[24,8,128]{2,1,0:T(8,128)S(1)}, f32[24,8,128]{2,1,0:T(8,128)S(1)}, u32[]{:S(2)}, u32[]{:S(2)}) collective-permute-start(f32[24,8,128]{2,1,0:T(8,128)S(1)} %pad_maximum_fusion.3), channel_id=1, source_target_pairs={{0,225},{1,16},{2,227},{3,18},{4,229},{5,20},{6,231},{7,22},{8,233... | collective-permute-start | bytes 294920 | tf_op jit(solution)/shard_map/ppermute | solution.py:62
  105.7 1.3 collective-permute-start.14
  108.9 7.0 %collective-permute-start.15 = (f32[8,8,128]{2,1,0:T(8,128)S(1)}, f32[8,8,128]{2,1,0:T(8,128)S(1)}, u32[]{:S(2)}, u32[]{:S(2)}) collective-permute-start(f32[8,8,128]{2,1,0:T(8,128)S(1)} %get-tuple-element.46.c_in), channel_id=1, source_target_pairs={{0,32},{1,2},{2,1},{3,4},{4,3},{5,6},{6,5},{7,8},{8,7},{9,10},{10,... | collective-permute-start | bytes 98312 | tf_op jit(solution)/shard_map/ppermute | solution.py:58
  116.0 1.2 collective-permute-start.16
  117.2 5.3 %collective-permute-start.17 = (f32[24,8,128]{2,1,0:T(8,128)S(1)}, f32[24,8,128]{2,1,0:T(8,128)S(1)}, u32[]{:S(2)}, u32[]{:S(2)}) collective-permute-start(f32[24,8,128]{2,1,0:T(8,128)S(1)} %pad_maximum_fusion.4), channel_id=1, source_target_pairs={{0,225},{1,16},{2,227},{3,18},{4,229},{5,20},{6,231},{7,22},{8,233... | collective-permute-start | bytes 294920 | tf_op jit(solution)/shard_map/ppermute | solution.py:62
  122.5 1.3 collective-permute-start.18
  125.8 7.0 %collective-permute-start.19 = (f32[8,8,128]{2,1,0:T(8,128)S(1)}, f32[8,8,128]{2,1,0:T(8,128)S(1)}, u32[]{:S(2)}, u32[]{:S(2)}) collective-permute-start(f32[8,8,128]{2,1,0:T(8,128)S(1)} %get-tuple-element.48.c_in), channel_id=1, source_target_pairs={{0,32},{1,2},{2,1},{3,4},{4,3},{5,6},{6,5},{7,8},{8,7},{9,10},{10,... | collective-permute-start | bytes 98312 | tf_op jit(solution)/shard_map/ppermute | solution.py:58
  132.9 1.2 collective-permute-start.20
  134.1 5.3 %collective-permute-start.21 = (f32[24,8,128]{2,1,0:T(8,128)S(1)}, f32[24,8,128]{2,1,0:T(8,128)S(1)}, u32[]{:S(2)}, u32[]{:S(2)}) collective-permute-start(f32[24,8,128]{2,1,0:T(8,128)S(1)} %pad_maximum_fusion.5), channel_id=1, source_target_pairs={{0,225},{1,16},{2,227},{3,18},{4,229},{5,20},{6,231},{7,22},{8,233... | collective-permute-start | bytes 294920 | tf_op jit(solution)/shard_map/ppermute | solution.py:62
  139.4 1.3 collective-permute-start.22

commit v6 on v5

--- a/solution.py
+++ b/solution.py
@@ -14,6 +14,7 @@
 PAD = 5
 EXT = 4 + 2 * PAD
 EVEN = [(i, i ^ 1) for i in range(NS)]
+VMEM = pl.BlockSpec(memory_space=pltpu.VMEM)
 
 
 def odd_pairs():
@@ -26,28 +27,34 @@
 
 
 ODD = odd_pairs()
-VMEM = pl.BlockSpec(memory_space=pltpu.VMEM)
-SMEM = pl.BlockSpec(memory_space=pltpu.SMEM)
-
-
-def place_of(t):
+
+
+def place_of(t, half):
+    t = t ^ half
     return t ^ ((t >> 1) & 1)
 
 
-PLACE = [place_of(t) for t in range(NT)]
-
-
-def y_pairs():
-    at = {place_of(t): t for t in range(NT)}
+PLACE = [[place_of(t, half) for t in range(NT)] for half in range(2)]
+AT = [[PLACE[half].index(p) for p in range(NT)] for half in range(2)]
+
+
+def chain_pairs(along_x):
     pairs = []
     for t in range(NT):
         for s in range(NS):
             step = 1 if s % 2 else -1
-            pairs.append((t * NS + s, at[(place_of(t) + step) % NT] * NS + (s ^ 1)))
+            half, place = s // 8, PLACE[s // 8][t]
+            if not along_x:
+                pairs.append((t * NS + s, AT[half][(place + step) % NT] * NS + (s ^ 1)))
+            elif 0 <= s + step < NS:
+                pairs.append((t * NS + s, AT[(s + step) // 8][place] * NS + s + step))
+            else:
+                pairs.append((t * NS + s, (t ^ 2) * NS + s))
     return pairs
 
 
-YODD = y_pairs()
+XODD = chain_pairs(True)
+YODD = chain_pairs(False)
 
 
 def even(x):
@@ -56,6 +63,10 @@
 
 def odd(x):
     return lax.ppermute(x, ("tm", "space"), ODD)
+
+
+def xodd(x):
+    return lax.ppermute(x, ("tm", "space"), XODD)
 
 
 def yodd(x):
@@ -149,8 +160,8 @@
             clear_outside(s, [b.at[0], b.at[1]], PAD - h, PAD + 4 + h)
 
 
-def first_kernel(flags, pack, ev, od, out, s0, s1, cnd, heat, *coefficients):
-    s = flags[1]
+def first_kernel(pack, ev, od, out, s0, s1, cnd, heat, *coefficients):
+    s = lax.axis_index("space")
     core = s % 2
     for l in range(4):
         for f in range(2):
@@ -185,10 +196,10 @@
 
 
 def second_kernel(
-    flags, a, pack, ev, od, evc, odc, ev5, chip, e_out, w_out, tiles, s0, s1, cnd, heat, *rest
+    a, pack, ev, od, evc, odc, ev5, e_out, w_out, s0, s1, cnd, heat, *rest
 ):
     coefficients, wide = rest[:4], rest[4]
-    t, s = flags[0], flags[1]
+    t, s = lax.axis_index("tm"), lax.axis_index("space")
     core = s % 2
     od_at = lambda i: od[128 * i : 128 * i + 128]
     for l in range(4):
@@ -196,8 +207,6 @@
             s0[f, PAD + l] = a[f, l]
         cnd[PAD + l] = pack[2, l]
         heat[PAD + l] = pack[3, l]
-    for l in range(8):
-        tiles[8 + l] = chip[l]
 
     def sides(even, odd, even5, odd5):
         for l in range(4):
@@ -213,20 +222,13 @@
         cnd[even5] = ev5[128:256]
         cnd[odd5] = od_at(9)
 
-    def side_tiles(even, odd):
-        for l in range(8):
-            tiles[even + l] = ev5[256 + 24 * l : 280 + 24 * l]
-            tiles[odd + l] = od[1280 + 24 * l : 1304 + 24 * l]
-
     @pl.when(core == 0)
     def _():
         sides(PAD + 4, 1, EXT - 1, 0)
-        side_tiles(16, 0)
 
     @pl.when(core == 1)
     def _():
         sides(1, PAD + 4, 0, EXT - 1)
-        side_tiles(0, 16)
 
     clear_outside(s, [s0.at[0], s0.at[1], cnd], 0, EXT)
     set_coefficients(cnd, *coefficients, 0, EXT - 1)
@@ -242,26 +244,31 @@
         wide[0, l] = s0[0, l] - wide[0, l]
     clear_outside(s, [wide.at[0]], PAD - 1, PAD + 5)
 
-    @pl.when(t != NT - 1)
-    def _():
-        def finish(l, rows, v, stepped):
-            to = PLACE[rows.start // 8]
-            e_out[to, l - PAD] = v + ratio * (stepped - v) + (s0[1, l, rows] - wide[1, l, rows])
-
-        sweep(lambda l, rows: wide[0, l, rows], finish, coefficients, PAD, PAD + 4)
-        for l in range(4):
-            w_out[l] = wide[0, PAD + l]
-
-    @pl.when(t == NT - 1)
-    def _():
-        for l in range(4):
-            for r in range(16):
-                e_out[PLACE[r], l] = s0[0, PAD + l, rows_at(r)]
-            w_out[l] = a[0, l]
-
-
-def region(flags, cond, halo):
-    chip, place = flags[1] // 2, flags[2]
+    def leave(h):
+        @pl.when((s // 8 == h) & (t != NT - 1))
+        def _():
+            def finish(l, rows, v, stepped):
+                to = AT[h][rows.start // 8]
+                e_out[to, l - PAD] = v + ratio * (stepped - v) + (s0[1, l, rows] - wide[1, l, rows])
+
+            sweep(lambda l, rows: wide[0, l, rows], finish, coefficients, PAD, PAD + 4)
+            for l in range(4):
+                w_out[l] = wide[0, PAD + l]
+
+        @pl.when((s // 8 == h) & (t == NT - 1))
+        def _():
+            for l in range(4):
+                for r in range(16):
+                    e_out[AT[h][r], l] = s0[0, PAD + l, rows_at(r)]
+                w_out[l] = a[0, l]
+
+    leave(0)
+    leave(1)
+
+
+def region(cond, halo):
+    t, s = lax.axis_index("tm"), lax.axis_index("space")
+    chip, place = s // 2, place_of(t, s // 8)
     count = 8 + 2 * halo
     shape = (count, 24, 128)
     layer = lax.broadcasted_iota(jnp.int32, shape, 0) + (chip * 8 - halo)
@@ -323,8 +330,12 @@
     return (j - 1) % NT
 
 
-def chips_kernel(flags, own, other, chip, send):
-    def run(first, last, side):
+def chips_kernel(own, other, cond, cond_got, cond_swap, chip, send, tiles):
+    tiles[8:16] = cond[...]
+
+    def run(first, last, side, left, right):
+        tiles[0:8] = left[...]
+        tiles[16:24] = right[...]
         for j in range(NT):
             chip[j, 0:4] = first[slot(j)]
             chip[j, 4:8] = last[slot(j)]
@@ -333,16 +344,16 @@
                 a, b = STARTS[i], STARTS[i] + h
                 send[q, a:b] = chip[4 * q + i, side(h)]
 
-    @pl.when(flags[1] % 2 == 0)
-    def _():
-        run(own, other, lambda h: slice(0, h))
-
-    @pl.when(flags[1] % 2 == 1)
-    def _():
-        run(other, own, lambda h: slice(8 - h, 8))
-
-
-def rows_kernel(flags, chip, got, swap, send):
+    @pl.when(lax.axis_index("space") % 2 == 0)
+    def _():
+        run(own, other, lambda h: slice(0, h), cond_got, cond_swap)
+
+    @pl.when(lax.axis_index("space") % 2 == 1)
+    def _():
+        run(other, own, lambda h: slice(8 - h, 8), cond_swap, cond_got)
+
+
+def rows_kernel(chip, got, swap, send):
     def run(left, right, upward):
         for q in range(4):
             for i, l, rows, tile, first in PIECES:
@@ -356,19 +367,19 @@
                     value = right[q, a + l - h - 8, pick]
                 send[q, tile, first : first + rows] = value
 
-    @pl.when(flags[1] % 2 == 0)
+    @pl.when(lax.axis_index("space") % 2 == 0)
     def _():
         run(got, swap, False)
 
-    @pl.when(flags[1] % 2 == 1)
+    @pl.when(lax.axis_index("space") % 2 == 1)
     def _():
         run(swap, got, True)
 
 
-def quads_kernel(groups, flags, cond, chip, xg, xs, yg, ys, *refs):
+def quads_kernel(groups, cond, chip, xg, xs, yg, ys, *refs):
     outs, (b0, b1, b2), coef = refs[:-8], refs[-8:-5], refs[-5:]
-    core = flags[1] % 2
-    for value, ref in zip(region(flags, cond, 6), coef):
+    core = lax.axis_index("space") % 2
+    for value, ref in zip(region(cond, 6), coef):
         ref[...] = value
     for h, buf in zip(HALOS, (b0, b1, b2)):
         buf[...] = jnp.zeros((8 + 2 * h, 24, 128), jnp.float32)
@@ -421,9 +432,9 @@
                 zp_out[4 * q - 4 + i] = partial[i]
 
 
-def chain_kernel(q, flags, cond, c_in, p, zp, ends, xg, xs, yg, ys, last, done, buf, *coef):
-    core = flags[1] % 2
-    for value, ref in zip(region(flags, cond, 8), coef):
+def chain_kernel(q, cond, c_in, p, zp, ends, xg, xs, yg, ys, last, done, buf, *coef):
+    core = lax.axis_index("space") % 2
+    for value, ref in zip(region(cond, 8), coef):
         ref[...] = value
     buf[8:16, 8:16] = c_in[...]
 
@@ -455,11 +466,20 @@
 
 
 def final_kernel(got, w, out):
-    for src in range(NT):
-        rows = slice(8 * place_of(src), 8 * place_of(src) + 8)
-        for l in range(4):
-            out[0, l, rows] = got[src, 0, l] + w[l, rows]
-            out[1, l, rows] = got[src, 1, l]
+    def run(h):
+        for src in range(NT):
+            rows = rows_at(PLACE[h][src])
+            for l in range(4):
+                out[0, l, rows] = got[src, 0, l] + w[l, rows]
+                out[1, l, rows] = got[src, 1, l]
+
+    @pl.when(lax.axis_index("space") < 8)
+    def _():
+        run(0)
+
+    @pl.when(lax.axis_index("space") >= 8)
+    def _():
+        run(1)
 
 
 def coefficient_scratch(halo):
@@ -468,12 +488,11 @@
     return [pltpu.VMEM((count, 24, 128), jnp.float32) for count in counts]
 
 
-def call(kernel, outs, scratches, *args, smem=True, cost=None):
-    specs = [SMEM] + [VMEM] * (len(args) - 1) if smem else [VMEM] * len(args)
+def call(kernel, outs, scratches, *args, cost=None):
     return pl.pallas_call(
         kernel,
         out_shape=outs,
-        in_specs=specs,
+        in_specs=[VMEM] * len(args),
         out_specs=[VMEM] * len(outs),
         scratch_shapes=scratches,
         compiler_params=params(),
@@ -485,41 +504,49 @@
     t = lax.axis_index("tm")
     s = lax.axis_index("space")
     core = s % 2
-    place = t ^ ((t >> 1) & 1)
-    flags = jnp.stack([t, s, place, core]).astype(jnp.int32)
+    place = place_of(t, s // 8)
     swap = (jnp.arange(4) == 0)[:, None, None, None] & (t == NT - 1)
     pack = jnp.where(swap, initial[None], jnp.concatenate([guess, cond[None], source[None]]))
     ev = even(pack)
     od = odd(pack)
-    layers = pltpu.VMEM((EXT, 128, 128), jnp.float32)
-    fine_scratch = [pltpu.VMEM((2, EXT, 128, 128), jnp.float32)] * 2 + [layers] * 6
-    (a,) = call(first_kernel, [struct(2, 4, 128, 128)], fine_scratch, flags, pack, ev, od)
-
     start = 8 * place
     rows_of = lambda x: lax.dynamic_slice_in_dim(jnp.pad(x, ((0, 0), (8, 8), (0, 0))), start, 24, 1)
     mine, yours = rows_of(pack[2]), rows_of(ev[2])
     chip = jnp.where(core == 0, jnp.concatenate([mine, yours]), jnp.concatenate([yours, mine]))
-
+    c_got = xodd(chip)
+
+    layers = pltpu.VMEM((EXT, 128, 128), jnp.float32)
+    fine_scratch = [pltpu.VMEM((2, EXT, 128, 128), jnp.float32)] * 2 + [layers] * 6
+    (a,) = call(first_kernel, [struct(2, 4, 128, 128)], fine_scratch, pack, ev, od)
+
+    a, c_got = lax.optimization_barrier((a, c_got))
     ev2 = even(a)
     tail = lambda x: jnp.where(core == 0, x[0], x[3])
     nearest = lambda x: jnp.where(core == 0, x[3], x[0])
-    chip_rows = chip.reshape(192, 128)
-    od2 = odd(jnp.concatenate([a.reshape(1024, 128), tail(ev2[0]), tail(ev[2]), chip_rows]))
-    ev5 = even(jnp.concatenate([nearest(od2[:512].reshape(4, 128, 128)), nearest(od[2]), od2[1280:]]))
-    e, w, tiles = call(
+    od2 = odd(jnp.concatenate([a.reshape(1024, 128), tail(ev2[0]), tail(ev[2])]))
+    ev5 = even(jnp.concatenate([nearest(od2[:512].reshape(4, 128, 128)), nearest(od[2])]))
+    ev5, c_got = lax.optimization_barrier((ev5, c_got))
+    c_swap = even(c_got)
+    e, w = call(
         second_kernel,
-        [struct(NT, 4, 8, 128), struct(4, 128, 128), struct(24, 24, 128)],
+        [struct(NT, 4, 8, 128), struct(4, 128, 128)],
         fine_scratch + [pltpu.VMEM((2, EXT, 128, 128), jnp.float32)],
-        flags, a, pack, ev2, od2, ev, od, ev5, chip,
+        a, pack, ev2, od2, ev, od, ev5,
     )
+    e, w, c_swap = lax.optimization_barrier((e, w, c_swap))
     own = lax.all_to_all(e, "tm", 0, 0)
     own, w = lax.optimization_barrier((own, w))
     w_before = lax.ppermute(w, "tm", [(i, (i + 1) % NT) for i in range(NT)])
     other = even(own)
-    chips, send = call(chips_kernel, [struct(NT, 8, 8, 128), struct(4, 12, 8, 128)], [], flags, own, other)
-    xg = odd(send)
+    chips, send, tiles = call(
+        chips_kernel,
+        [struct(NT, 8, 8, 128), struct(4, 12, 8, 128), struct(24, 24, 128)],
+        [],
+        own, other, chip, c_got, c_swap,
+    )
+    xg = xodd(send)
     xs = even(xg)
-    (send,) = call(rows_kernel, [struct(4, Y_TILES, 8, 128)], [], flags, chips, xg, xs)
+    (send,) = call(rows_kernel, [struct(4, Y_TILES, 8, 128)], [], chips, xg, xs)
     send, w_before = lax.optimization_barrier((send, w_before))
     yg = yodd(send)
     ys = even(yg)
@@ -529,18 +556,18 @@
         functools.partial(quads_kernel, (0,)),
         [struct(8, 8, 128), struct(4, 2, 4, 8, 128)],
         quad_scratch,
-        flags, tiles, chips, xg, xs, yg, ys,
+        tiles, chips, xg, xs, yg, ys,
     )
     p, zp, ends = call(
         functools.partial(quads_kernel, (1, 2, 3)),
         [struct(12, 4, 8, 128), struct(12, 4, 8, 128), struct(3, 8, 8, 128)],
         quad_scratch,
-        flags, tiles, chips, xg, xs, yg, ys,
+        tiles, chips, xg, xs, yg, ys,
         cost=pl.CostEstimate(flops=30_000_000, bytes_accessed=4_000_000, transcendentals=0),
     )
     parts = [done]
     for q in (1, 2, 3):
-        xg = odd(last)
+        xg = xodd(last)
         if q == 1:
             xg, p, zp, ends = lax.optimization_barrier((xg, p, zp, ends))
         xs = even(xg)
@@ -552,11 +579,11 @@
             functools.partial(chain_kernel, q),
             [struct(8, 8, 128), struct(4, 2, 4, 8, 128)],
             [pltpu.VMEM((24, 24, 128), jnp.float32)] + coefficient_scratch(8),
-            flags, tiles, last, p, zp, ends, xg, xs, yg, ys,
+            tiles, last, p, zp, ends, xg, xs, yg, ys,
         )
         parts.append(done)
     back = lax.all_to_all(jnp.concatenate(parts), "tm", 0, 0)
-    (out,) = call(final_kernel, [struct(2, 4, 128, 128)], [], back, w_before, smem=False)
+    (out,) = call(final_kernel, [struct(2, 4, 128, 128)], [], back, w_before)
     return out
 
 

time: 166 us -> 162 us (0.976)
  waiting for transfers between devices: 83.9 us -> 63.7 us
  starting transfers between devices: 14.1 us -> 32.8 us
  Pallas kernels: 22.8 us -> 18.2 us
    ppermute x6 -> x2, waiting for transfers between devices: 45.5 us -> 25.4 us  [odd(): return lax.ppermute(x, ('tm', 'space'), ODD)]
    ppermute x0 -> x5, starting transfers between devices: none -> 13.5 us  [xodd(): return lax.ppermute(x, ('tm', 'space'), XODD)]
    ppermute x4, starting transfers between devices: 0.37 us -> 12.2 us  [yodd(): return lax.ppermute(x, ('tm', 'space'), YODD)]
    ppermute x4, waiting for transfers between devices: 23.1 us -> 13 us  [yodd(): return lax.ppermute(x, ('tm', 'space'), YODD)]
    ppermute x6 -> x2, starting transfers between devices: 12.3 us -> 4.48 us  [odd(): return lax.ppermute(x, ('tm', 'space'), ODD)]
    ppermute x0 -> x5, waiting for transfers between devices: none -> 7.68 us  [xodd(): return lax.ppermute(x, ('tm', 'space'), XODD)]
    pallas_call x10, Pallas kernels: 22.8 us -> 18.2 us  [call(): pl.pallas_call(kernel, out_shape=outs, in_specs=[VMEM] * len(args), out_s...]
    ppermute x1, waiting for transfers between devices: 0.01 us -> 2.34 us  [body(): w_before = lax.ppermute(w, 'tm', [(i, (i + 1) % NT) for i in range(NT)])]
  transfers between devices with their start and end apart: 23 -> 25, of which waited for: 21 -> 21; matrix products, arithmetic and copies ran while one was open for 0% -> 0% of each run, Pallas kernels for 3% -> 7%
where the time goes in v6:
time: 162 us; the launch traced here: 161 us
  waiting for transfers between devices  63.7 us (39%)
  blocking collectives  44 us (27%)
  starting transfers between devices  32.8 us (20%)
  Pallas kernels  18.2 us (11%)
  other arithmetic  1.63 us (1%)
    ppermute x2, waiting for transfers between devices, odd(): return lax.ppermute(x, ('tm', 'space'), ODD)  25.4 us
    all_to_all x1, blocking collectives, body(): back = lax.all_to_all(jnp.concatenate(parts), 'tm', 0, 0)  23.1 us
    all_to_all x1, blocking collectives, body(): own = lax.all_to_all(e, 'tm', 0, 0)  20.9 us
    pallas_call x10, Pallas kernels, call(): pl.pallas_call(kernel, out_shape=outs, in_specs=[VMEM] * len(args), out_s...  18.2 us
    ppermute x13, waiting for transfers between devices, even(): return lax.ppermute(x, 'space', EVEN)  15.3 us
    ppermute x5, starting transfers between devices, xodd(): return lax.ppermute(x, ('tm', 'space'), XODD)  13.5 us
    ppermute x4, waiting for transfers between devices, yodd(): return lax.ppermute(x, ('tm', 'space'), YODD)  13 us
    ppermute x4, starting transfers between devices, yodd(): return lax.ppermute(x, ('tm', 'space'), YODD)  12.2 us
  transfers between devices with their start and end apart: 25, of which 21 were waited for; matrix products, arithmetic and copies ran while one was open for 0% of the time, Pallas kernels for 7%

profile of v6, /device:TPU:16, one launch (start us, length us, event | category | flops | bytes accessed | tf_op | source)
XLA Modules:
  0.0 160.7 jit_solution(17994241614133719201)
XLA Ops:
  0.0 1.4 maximum_select_fusion.pack
  1.4 0.1 collective-permute-start
  1.6 2.6 %collective-permute-start.1 = (f32[4,4,128,128]{3,2,1,0:T(8,128)S(1)}, f32[4,4,128,128]{3,2,1,0:T(8,128)S(1)}, u32[]{:S(2)}, u32[]{:S(2)}) collective-permute-start(f32[4,4,128,128]{3,2,1,0:T(8,128)S(1)} %maximum_select_fusion.pack), channel_id=1, source_target_pairs={{0,32},{1,2},{2,1},{3,4},{4,3},{5,6},{6,5},{7,8},{8,7},{9,10},{10,... | collective-permute-start | bytes 3145736 | tf_op jit(solution)/shard_map/ppermute | solution.py:65
  4.2 0.0 collective-permute-done.ev.evc
  4.3 2.4 %collective-permute-start.2 = (f32[8,24,128]{2,1,0:T(8,128)S(1)}, f32[8,24,128]{2,1,0:T(8,128)S(1)}, u32[]{:S(2)}, u32[]{:S(2)}) collective-permute-start(f32[8,24,128]{2,1,0:T(8,128)S(1)} %maximum_select_fusion.1.cond), channel_id=1, source_target_pairs={{0,32},{1,2},{2,1},{3,4},{4,3},{5,6},{6,5},{7,24},{8,23},{9,10},{1... | collective-permute-start | bytes 294920 | tf_op jit(solution)/shard_map/ppermute | solution.py:69
  6.7 13.5 %collective-permute-done.1.od.odc = f32[4,4,128,128]{3,2,1,0:T(8,128)S(1)} collective-permute-done((f32[4,4,128,128]{3,2,1,0:T(8,128)S(1)}, f32[4,4,128,128]{3,2,1,0:T(8,128)S(1)}, u32[]{:S(2)}, u32[]{:S(2)}) %collective-permute-start.1) | collective-permute-done | bytes 1048608 | tf_op jit(solution)/shard_map/ppermute | solution.py:65
  20.3 3.4 %shard_map.46.a = f32[2,4,128,128]{3,2,1,0:T(8,128)S(1)} custom-call(f32[4,4,128,128]{3,2,1,0:T(8,128)S(1)} %maximum_select_fusion.pack, f32[4,4,128,128]{3,2,1,0:T(8,128)S(1)} %collective-permute-done.ev.evc, f32[4,4,128,128]{3,2,1,0:T(8,128)S(1)} %collective-permute-done.1.od.odc), custom_call_target="tpu_custom_call" | custom-call | tf_op jit(solution)/shard_map/pallas_call | solution.py:492
  23.6 0.0 collective-permute-done.2.cond_got
  23.6 0.1 collective-permute-start.3
  23.7 1.9 %collective-permute-done.3.ev = f32[2,4,128,128]{3,2,1,0:T(8,128)S(1)} collective-permute-done((f32[2,4,128,128]{3,2,1,0:T(8,128)S(1)}, f32[2,4,128,128]{3,2,1,0:T(8,128)S(1)}, u32[]{:S(2)}, u32[]{:S(2)}) %collective-permute-start.3) | collective-permute-done | bytes 524320 | tf_op jit(solution)/shard_map/ppermute | solution.py:61
  25.7 1.8 %collective-permute-start.4 = (f32[1280,128]{1,0:T(8,128)S(1)}, f32[1280,128]{1,0:T(8,128)S(1)}, u32[]{:S(2)}, u32[]{:S(2)}) collective-permute-start(f32[1280,128]{1,0:T(8,128)S(1)} %pad_maximum_fusion), channel_id=1, source_target_pairs={{0,32},{1,2},{2,1},{3,4},{4,3},{5,6},{6,5},{7,8},{8,7},{9,10},{10,... | collective-permute-start | bytes 1966088 | tf_op jit(solution)/shard_map/ppermute | solution.py:65
  27.5 11.9 %collective-permute-done.4.od = f32[1280,128]{1,0:T(8,128)S(1)} collective-permute-done((f32[1280,128]{1,0:T(8,128)S(1)}, f32[1280,128]{1,0:T(8,128)S(1)}, u32[]{:S(2)}, u32[]{:S(2)}) %collective-permute-start.4) | collective-permute-done | bytes 655392 | tf_op jit(solution)/shard_map/ppermute | solution.py:65
  39.4 0.1 collective-permute-start.5
  39.5 1.3 collective-permute-done.5.ev5
  40.9 0.1 collective-permute-start.6
  41.0 4.7 %shard_map.47 = (f32[16,4,8,128]{3,2,1,0:T(8,128)S(1)}, f32[4,128,128]{2,1,0:T(8,128)S(1)}) custom-call(f32[2,4,128,128]{3,2,1,0:T(8,128)S(1)} %shard_map.46.a, f32[4,4,128,128]{3,2,1,0:T(8,128)S(1)} %maximum_select_fusion.pack, f32[2,4,128,128]{3,2,1,0:T(8,128)S(1)} %collective-permute-done.3.ev, f32[1280,128]{1,0:T(8,128)S(1)} %collective-permute-done.4.od, ...), custom_call_target="tpu_custom_call" | custom-call | tf_op jit(solution)/shard_map/pallas_call | solution.py:492
  45.7 0.0 collective-permute-done.6.cond_swap
  45.7 20.9 %all_to_all.10.own = f32[16,4,8,128]{3,2,1,0:T(8,128)S(1)} all-to-all(f32[16,4,8,128]{3,2,1,0:T(8,128)S(1)} %get-tuple-element.41), channel_id=1, replica_groups=mesh['tm'=16,'space'=16] {'tm'}, dimensions={0} | all-to-all | bytes 524288 | tf_op jit(solution)/shard_map/all_to_all | solution.py:537
  66.6 0.0 collective-permute-start.7
  66.6 1.5 collective-permute-done.7.other
  68.2 0.1 shard_map.48
  68.2 2.7 %collective-permute-start.8 = (f32[4,12,8,128]{3,2,1,0:T(8,128)S(1)}, f32[4,12,8,128]{3,2,1,0:T(8,128)S(1)}, u32[]{:S(2)}, u32[]{:S(2)}) collective-permute-start(f32[4,12,8,128]{3,2,1,0:T(8,128)S(1)} %get-tuple-element.47), channel_id=1, source_target_pairs={{0,32},{1,2},{2,1},{3,4},{4,3},{5,6},{6,5},{7,24},{8,23},{9,10},{1... | collective-permute-start | bytes 589832 | tf_op jit(solution)/shard_map/ppermute | solution.py:69
  70.9 2.2 %collective-permute-start.10 = (f32[4,128,128]{2,1,0:T(8,128)S(1)}, f32[4,128,128]{2,1,0:T(8,128)S(1)}, u32[]{:S(2)}, u32[]{:S(2)}) collective-permute-start(f32[4,128,128]{2,1,0:T(8,128)S(1)} %get-tuple-element.48), channel_id=1, source_target_pairs={{0,16},{16,32},{32,48},{48,64},{64,80},{80,96},{96,112},{112,128},... | collective-permute-start | bytes 786440 | tf_op jit(solution)/shard_map/ppermute | solution.py:539
  73.1 2.5 %collective-permute-done.8.got.xg = f32[4,12,8,128]{3,2,1,0:T(8,128)S(1)} collective-permute-done((f32[4,12,8,128]{3,2,1,0:T(8,128)S(1)}, f32[4,12,8,128]{3,2,1,0:T(8,128)S(1)}, u32[]{:S(2)}, u32[]{:S(2)}) %collective-permute-start.8) | collective-permute-done | bytes 196640 | tf_op jit(solution)/shard_map/ppermute | solution.py:69
  75.5 0.0 collective-permute-start.9
  75.5 1.4 collective-permute-done.9.swap.xs
  77.0 0.1 shard_map.49
  77.0 2.3 %collective-permute-done.10.w = f32[4,128,128]{2,1,0:T(8,128)S(1)} collective-permute-done((f32[4,128,128]{2,1,0:T(8,128)S(1)}, f32[4,128,128]{2,1,0:T(8,128)S(1)}, u32[]{:S(2)}, u32[]{:S(2)}) %collective-permute-start.10) | collective-permute-done | bytes 262176 | tf_op jit(solution)/shard_map/ppermute | solution.py:539
  79.4 0.0 collective-permute-start.11
  79.4 6.1 %collective-permute-done.11.yg = f32[4,18,8,128]{3,2,1,0:T(8,128)S(1)} collective-permute-done((f32[4,18,8,128]{3,2,1,0:T(8,128)S(1)}, f32[4,18,8,128]{3,2,1,0:T(8,128)S(1)}, u32[]{:S(2)}, u32[]{:S(2)}) %collective-permute-start.11) | collective-permute-done | bytes 294944 | tf_op jit(solution)/shard_map/ppermute | solution.py:73
  85.5 0.0 collective-permute-start.12
  85.5 1.6 collective-permute-done.12.ys
  87.1 1.1 shard_map.50
  88.3 2.5 %collective-permute-start.13 = (f32[8,8,128]{2,1,0:T(8,128)S(1)}, f32[8,8,128]{2,1,0:T(8,128)S(1)}, u32[]{:S(2)}, u32[]{:S(2)}) collective-permute-start(f32[8,8,128]{2,1,0:T(8,128)S(1)} %get-tuple-element.51.c_in), channel_id=1, source_target_pairs={{0,32},{1,2},{2,1},{3,4},{4,3},{5,6},{6,5},{7,24},{8,23},{9,10},{1... | collective-permute-start | bytes 98312 | tf_op jit(solution)/shard_map/ppermute | solution.py:69
  90.7 3.0 %shard_map.51 = (f32[12,4,8,128]{3,2,1,0:T(8,128)S(1)}, f32[12,4,8,128]{3,2,1,0:T(8,128)S(1)}, f32[3,8,8,128]{3,2,1,0:T(8,128)S(1)}) custom-call(f32[24,24,128]{2,1,0:T(8,128)S(1)} %get-tuple-element.45.cond, f32[16,8,8,128]{3,2,1,0:T(8,128)S(1)} %get-tuple-element.46.chip, f32[4,12,8,128]{3,2,1,0:T(8,128)S(1)} %collective-permute-done.8.got.xg, ...), custom_call_target="tpu_custom_call" | custom-call | flops 30000000 | bytes 4000000 | tf_op jit(solution)/shard_map/pallas_call | solution.py:492
  93.7 0.0 collective-permute-done.13.xg
  93.8 0.1 collective-permute-start.14
  93.9 1.2 collective-permute-done.14.xs
  95.1 3.7 %collective-permute-start.15 = (f32[24,8,128]{2,1,0:T(8,128)S(1)}, f32[24,8,128]{2,1,0:T(8,128)S(1)}, u32[]{:S(2)}, u32[]{:S(2)}) collective-permute-start(f32[24,8,128]{2,1,0:T(8,128)S(1)} %pad_maximum_fusion.3), channel_id=1, source_target_pairs={{0,225},{1,16},{2,227},{3,18},{4,229},{5,20},{6,231},{7,22},{8,25}... | collective-permute-start | bytes 294920 | tf_op jit(solution)/shard_map/ppermute | solution.py:73
  98.8 2.3 %collective-permute-done.15.yg = f32[24,8,128]{2,1,0:T(8,128)S(1)} collective-permute-done((f32[24,8,128]{2,1,0:T(8,128)S(1)}, f32[24,8,128]{2,1,0:T(8,128)S(1)}, u32[]{:S(2)}, u32[]{:S(2)}) %collective-permute-start.15) | collective-permute-done | bytes 98336 | tf_op jit(solution)/shard_map/ppermute | solution.py:73
  101.1 0.0 collective-permute-start.16
  101.1 1.3 collective-permute-done.16.ys
  102.4 1.6 %shard_map.52 = (f32[8,8,128]{2,1,0:T(8,128)S(1)}, f32[4,2,4,8,128]{4,3,2,1,0:T(8,128)S(1)}) custom-call(f32[24,24,128]{2,1,0:T(8,128)S(1)} %get-tuple-element.45.cond, f32[8,8,128]{2,1,0:T(8,128)S(1)} %get-tuple-element.51.c_in, f32[12,4,8,128]{3,2,1,0:T(8,128)S(1)} %get-tuple-element.55.p, f32[12,4,8,128]{3,2,1,0:T(8,128)S(1)} %get-tuple-element.56.zp, ...), custom_call_target="tpu_custom_call" | custom-call | tf_op jit(solution)/shard_map/pallas_call | solution.py:492
  104.0 3.0 %collective-permute-start.17 = (f32[8,8,128]{2,1,0:T(8,128)S(1)}, f32[8,8,128]{2,1,0:T(8,128)S(1)}, u32[]{:S(2)}, u32[]{:S(2)}) collective-permute-start(f32[8,8,128]{2,1,0:T(8,128)S(1)} %get-tuple-element.60.c_in), channel_id=1, source_target_pairs={{0,32},{1,2},{2,1},{3,4},{4,3},{5,6},{6,5},{7,24},{8,23},{9,10},{1... | collective-permute-start | bytes 98312 | tf_op jit(solution)/shard_map/ppermute | solution.py:69
  107.1 2.5 %collective-permute-done.17.xg = f32[8,8,128]{2,1,0:T(8,128)S(1)} collective-permute-done((f32[8,8,128]{2,1,0:T(8,128)S(1)}, f32[8,8,128]{2,1,0:T(8,128)S(1)}, u32[]{:S(2)}, u32[]{:S(2)}) %collective-permute-start.17) | collective-permute-done | bytes 32800 | tf_op jit(solution)/shard_map/ppermute | solution.py:69
  109.6 0.0 collective-permute-start.18
  109.6 1.2 collective-permute-done.18.xs
  110.8 4.2 %collective-permute-start.19 = (f32[24,8,128]{2,1,0:T(8,128)S(1)}, f32[24,8,128]{2,1,0:T(8,128)S(1)}, u32[]{:S(2)}, u32[]{:S(2)}) collective-permute-start(f32[24,8,128]{2,1,0:T(8,128)S(1)} %pad_maximum_fusion.4), channel_id=1, source_target_pairs={{0,225},{1,16},{2,227},{3,18},{4,229},{5,20},{6,231},{7,22},{8,25}... | collective-permute-start | bytes 294920 | tf_op jit(solution)/shard_map/ppermute | solution.py:73
  115.0 2.3 %collective-permute-done.19.yg = f32[24,8,128]{2,1,0:T(8,128)S(1)} collective-permute-done((f32[24,8,128]{2,1,0:T(8,128)S(1)}, f32[24,8,128]{2,1,0:T(8,128)S(1)}, u32[]{:S(2)}, u32[]{:S(2)}) %collective-permute-start.19) | collective-permute-done | bytes 98336 | tf_op jit(solution)/shard_map/ppermute | solution.py:73
  117.3 0.0 collective-permute-start.20
  117.3 1.3 collective-permute-done.20.ys
  118.6 1.4 shard_map.53
  120.1 2.9 %collective-permute-start.21 = (f32[8,8,128]{2,1,0:T(8,128)S(1)}, f32[8,8,128]{2,1,0:T(8,128)S(1)}, u32[]{:S(2)}, u32[]{:S(2)}) collective-permute-start(f32[8,8,128]{2,1,0:T(8,128)S(1)} %get-tuple-element.62.c_in), channel_id=1, source_target_pairs={{0,32},{1,2},{2,1},{3,4},{4,3},{5,6},{6,5},{7,24},{8,23},{9,10},{1... | collective-permute-start | bytes 98312 | tf_op jit(solution)/shard_map/ppermute | solution.py:69
  122.9 2.7 %collective-permute-done.21.xg = f32[8,8,128]{2,1,0:T(8,128)S(1)} collective-permute-done((f32[8,8,128]{2,1,0:T(8,128)S(1)}, f32[8,8,128]{2,1,0:T(8,128)S(1)}, u32[]{:S(2)}, u32[]{:S(2)}) %collective-permute-start.21) | collective-permute-done | bytes 32800 | tf_op jit(solution)/shard_map/ppermute | solution.py:69
  125.6 0.0 collective-permute-start.22
  125.6 1.2 collective-permute-done.22.xs
  126.8 4.2 %collective-permute-start.23 = (f32[24,8,128]{2,1,0:T(8,128)S(1)}, f32[24,8,128]{2,1,0:T(8,128)S(1)}, u32[]{:S(2)}, u32[]{:S(2)}) collective-permute-start(f32[24,8,128]{2,1,0:T(8,128)S(1)} %pad_maximum_fusion.5), channel_id=1, source_target_pairs={{0,225},{1,16},{2,227},{3,18},{4,229},{5,20},{6,231},{7,22},{8,25}... | collective-permute-start | bytes 294920 | tf_op jit(solution)/shard_map/ppermute | solution.py:73
  131.1 2.3 %collective-permute-done.23.yg = f32[24,8,128]{2,1,0:T(8,128)S(1)} collective-permute-done((f32[24,8,128]{2,1,0:T(8,128)S(1)}, f32[24,8,128]{2,1,0:T(8,128)S(1)}, u32[]{:S(2)}, u32[]{:S(2)}) %collective-permute-start.23) | collective-permute-done | bytes 98336 | tf_op jit(solution)/shard_map/ppermute | solution.py:73
  133.4 0.0 collective-permute-start.24
  133.4 1.3 collective-permute-done.24.ys
  134.7 2.0 %shard_map.54 = (f32[8,8,128]{2,1,0:T(8,128)}, f32[4,2,4,8,128]{4,3,2,1,0:T(8,128)S(1)}) custom-call(f32[24,24,128]{2,1,0:T(8,128)S(1)} %get-tuple-element.45.cond, f32[8,8,128]{2,1,0:T(8,128)S(1)} %get-tuple-element.62.c_in, f32[12,4,8,128]{3,2,1,0:T(8,128)S(1)} %get-tuple-element.55.p, f32[12,4,8,128]{3,2,1,0:T(8,128)S(1)} %get-tuple-element.56.zp, ...), custom_call_target="tpu_custom_call" | custom-call | tf_op jit(solution)/shard_map/pallas_call | solution.py:492
  136.8 23.1 %all_to_all.11.got = f32[16,2,4,8,128]{4,3,2,1,0:T(8,128)S(1)} all-to-all(f32[16,2,4,8,128]{4,3,2,1,0:T(8,128)S(1)} %pad_maximum_fusion.1), channel_id=1, replica_groups=mesh['tm'=16,'space'=16] {'tm'}, dimensions={0} | all-to-all | bytes 1048576 | tf_op jit(solution)/shard_map/all_to_all | solution.py:585
  159.9 0.8 shard_map.55
  (19 shorter events, 0.3 us)
Async XLA Ops:
  1.4 2.8 %collective-permute-start = (f32[4,4,128,128]{3,2,1,0:T(8,128)S(1)}, f32[4,4,128,128]{3,2,1,0:T(8,128)S(1)}, u32[]{:S(2)}, u32[]{:S(2)}) collective-permute-start(f32[4,4,128,128]{3,2,1,0:T(8,128)S(1)} %maximum_select_fusion.pack), channel_id=1, source_target_pairs={{0,1},{1,0},{2,3},{3,2},{4,5},{5,4},{6,7},{7,6},{8,9},{9,8},{10,11... | collective-permute-start | bytes 3145736 | tf_op jit(solution)/shard_map/ppermute | solution.py:61
  1.6 18.7 %collective-permute-start.1 = (f32[4,4,128,128]{3,2,1,0:T(8,128)S(1)}, f32[4,4,128,128]{3,2,1,0:T(8,128)S(1)}, u32[]{:S(2)}, u32[]{:S(2)}) collective-permute-start(f32[4,4,128,128]{3,2,1,0:T(8,128)S(1)} %maximum_select_fusion.pack), channel_id=1, source_target_pairs={{0,32},{1,2},{2,1},{3,4},{4,3},{5,6},{6,5},{7,8},{8,7},{9,10},{10,... | collective-permute-start | bytes 3145736 | tf_op jit(solution)/shard_map/ppermute | solution.py:65
  4.3 19.3 %collective-permute-start.2 = (f32[8,24,128]{2,1,0:T(8,128)S(1)}, f32[8,24,128]{2,1,0:T(8,128)S(1)}, u32[]{:S(2)}, u32[]{:S(2)}) collective-permute-start(f32[8,24,128]{2,1,0:T(8,128)S(1)} %maximum_select_fusion.1.cond), channel_id=1, source_target_pairs={{0,32},{1,2},{2,1},{3,4},{4,3},{5,6},{6,5},{7,24},{8,23},{9,10},{1... | collective-permute-start | bytes 294920 | tf_op jit(solution)/shard_map/ppermute | solution.py:69
  23.6 2.0 %collective-permute-start.3 = (f32[2,4,128,128]{3,2,1,0:T(8,128)S(1)}, f32[2,4,128,128]{3,2,1,0:T(8,128)S(1)}, u32[]{:S(2)}, u32[]{:S(2)}) collective-permute-start(f32[2,4,128,128]{3,2,1,0:T(8,128)S(1)} %shard_map.46.a), channel_id=1, source_target_pairs={{0,1},{1,0},{2,3},{3,2},{4,5},{5,4},{6,7},{7,6},{8,9},{9,8},{10,11... | collective-permute-start | bytes 1572872 | tf_op jit(solution)/shard_map/ppermute | solution.py:61
  25.7 13.7 %collective-permute-start.4 = (f32[1280,128]{1,0:T(8,128)S(1)}, f32[1280,128]{1,0:T(8,128)S(1)}, u32[]{:S(2)}, u32[]{:S(2)}) collective-permute-start(f32[1280,128]{1,0:T(8,128)S(1)} %pad_maximum_fusion), channel_id=1, source_target_pairs={{0,32},{1,2},{2,1},{3,4},{4,3},{5,6},{6,5},{7,8},{8,7},{9,10},{10,... | collective-permute-start | bytes 1966088 | tf_op jit(solution)/shard_map/ppermute | solution.py:65
  39.4 1.4 collective-permute-start.5
  40.9 4.9 %collective-permute-start.6 = (f32[8,24,128]{2,1,0:T(8,128)S(1)}, f32[8,24,128]{2,1,0:T(8,128)S(1)}, u32[]{:S(2)}, u32[]{:S(2)}) collective-permute-start(f32[8,24,128]{2,1,0:T(8,128)S(1)} %collective-permute-done.2.cond_got), channel_id=1, source_target_pairs={{0,1},{1,0},{2,3},{3,2},{4,5},{5,4},{6,7},{7,6},{8,9},{9,8},{10,11... | collective-permute-start | bytes 294920 | tf_op jit(solution)/shard_map/ppermute | solution.py:61
  66.6 1.5 collective-permute-start.7
  68.2 7.3 %collective-permute-start.8 = (f32[4,12,8,128]{3,2,1,0:T(8,128)S(1)}, f32[4,12,8,128]{3,2,1,0:T(8,128)S(1)}, u32[]{:S(2)}, u32[]{:S(2)}) collective-permute-start(f32[4,12,8,128]{3,2,1,0:T(8,128)S(1)} %get-tuple-element.47), channel_id=1, source_target_pairs={{0,32},{1,2},{2,1},{3,4},{4,3},{5,6},{6,5},{7,24},{8,23},{9,10},{1... | collective-permute-start | bytes 589832 | tf_op jit(solution)/shard_map/ppermute | solution.py:69
  70.9 8.5 %collective-permute-start.10 = (f32[4,128,128]{2,1,0:T(8,128)S(1)}, f32[4,128,128]{2,1,0:T(8,128)S(1)}, u32[]{:S(2)}, u32[]{:S(2)}) collective-permute-start(f32[4,128,128]{2,1,0:T(8,128)S(1)} %get-tuple-element.48), channel_id=1, source_target_pairs={{0,16},{16,32},{32,48},{48,64},{64,80},{80,96},{96,112},{112,128},... | collective-permute-start | bytes 786440 | tf_op jit(solution)/shard_map/ppermute | solution.py:539
  75.5 1.4 collective-permute-start.9
  79.4 6.1 %collective-permute-start.11 = (f32[4,18,8,128]{3,2,1,0:T(8,128)S(1)}, f32[4,18,8,128]{3,2,1,0:T(8,128)S(1)}, u32[]{:S(2)}, u32[]{:S(2)}) collective-permute-start(f32[4,18,8,128]{3,2,1,0:T(8,128)S(1)} %shard_map.49), channel_id=1, source_target_pairs={{0,225},{1,16},{2,227},{3,18},{4,229},{5,20},{6,231},{7,22},{8,25}... | collective-permute-start | bytes 884744 | tf_op jit(solution)/shard_map/ppermute | solution.py:73
  85.5 1.6 collective-permute-start.12
  88.3 5.5 %collective-permute-start.13 = (f32[8,8,128]{2,1,0:T(8,128)S(1)}, f32[8,8,128]{2,1,0:T(8,128)S(1)}, u32[]{:S(2)}, u32[]{:S(2)}) collective-permute-start(f32[8,8,128]{2,1,0:T(8,128)S(1)} %get-tuple-element.51.c_in), channel_id=1, source_target_pairs={{0,32},{1,2},{2,1},{3,4},{4,3},{5,6},{6,5},{7,24},{8,23},{9,10},{1... | collective-permute-start | bytes 98312 | tf_op jit(solution)/shard_map/ppermute | solution.py:69
  93.8 1.3 collective-permute-start.14
  95.1 6.0 %collective-permute-start.15 = (f32[24,8,128]{2,1,0:T(8,128)S(1)}, f32[24,8,128]{2,1,0:T(8,128)S(1)}, u32[]{:S(2)}, u32[]{:S(2)}) collective-permute-start(f32[24,8,128]{2,1,0:T(8,128)S(1)} %pad_maximum_fusion.3), channel_id=1, source_target_pairs={{0,225},{1,16},{2,227},{3,18},{4,229},{5,20},{6,231},{7,22},{8,25}... | collective-permute-start | bytes 294920 | tf_op jit(solution)/shard_map/ppermute | solution.py:73
  101.1 1.3 collective-permute-start.16
  104.0 5.5 %collective-permute-start.17 = (f32[8,8,128]{2,1,0:T(8,128)S(1)}, f32[8,8,128]{2,1,0:T(8,128)S(1)}, u32[]{:S(2)}, u32[]{:S(2)}) collective-permute-start(f32[8,8,128]{2,1,0:T(8,128)S(1)} %get-tuple-element.60.c_in), channel_id=1, source_target_pairs={{0,32},{1,2},{2,1},{3,4},{4,3},{5,6},{6,5},{7,24},{8,23},{9,10},{1... | collective-permute-start | bytes 98312 | tf_op jit(solution)/shard_map/ppermute | solution.py:69
  109.6 1.2 collective-permute-start.18
  110.8 6.5 %collective-permute-start.19 = (f32[24,8,128]{2,1,0:T(8,128)S(1)}, f32[24,8,128]{2,1,0:T(8,128)S(1)}, u32[]{:S(2)}, u32[]{:S(2)}) collective-permute-start(f32[24,8,128]{2,1,0:T(8,128)S(1)} %pad_maximum_fusion.4), channel_id=1, source_target_pairs={{0,225},{1,16},{2,227},{3,18},{4,229},{5,20},{6,231},{7,22},{8,25}... | collective-permute-start | bytes 294920 | tf_op jit(solution)/shard_map/ppermute | solution.py:73
  117.3 1.3 collective-permute-start.20
  120.1 5.5 %collective-permute-start.21 = (f32[8,8,128]{2,1,0:T(8,128)S(1)}, f32[8,8,128]{2,1,0:T(8,128)S(1)}, u32[]{:S(2)}, u32[]{:S(2)}) collective-permute-start(f32[8,8,128]{2,1,0:T(8,128)S(1)} %get-tuple-element.62.c_in), channel_id=1, source_target_pairs={{0,32},{1,2},{2,1},{3,4},{4,3},{5,6},{6,5},{7,24},{8,23},{9,10},{1... | collective-permute-start | bytes 98312 | tf_op jit(solution)/shard_map/ppermute | solution.py:69
  125.6 1.2 collective-permute-start.22
  126.8 6.5 %collective-permute-start.23 = (f32[24,8,128]{2,1,0:T(8,128)S(1)}, f32[24,8,128]{2,1,0:T(8,128)S(1)}, u32[]{:S(2)}, u32[]{:S(2)}) collective-permute-start(f32[24,8,128]{2,1,0:T(8,128)S(1)} %pad_maximum_fusion.5), channel_id=1, source_target_pairs={{0,225},{1,16},{2,227},{3,18},{4,229},{5,20},{6,231},{7,22},{8,25}... | collective-permute-start | bytes 294920 | tf_op jit(solution)/shard_map/ppermute | solution.py:73
  133.4 1.3 collective-permute-start.24

commit v7 on v6

--- a/solution.py
+++ b/solution.py
@@ -196,41 +196,43 @@
 
 
 def second_kernel(
-    a, pack, ev, od, evc, odc, ev5, e_out, w_out, s0, s1, cnd, heat, *rest
+    a, pack, ev, od, evc, odc, low, high, e_out, w_out, s0, s1, cnd, heat, *rest
 ):
     coefficients, wide = rest[:4], rest[4]
     t, s = lax.axis_index("tm"), lax.axis_index("space")
     core = s % 2
-    od_at = lambda i: od[128 * i : 128 * i + 128]
     for l in range(4):
         for f in range(2):
             s0[f, PAD + l] = a[f, l]
         cnd[PAD + l] = pack[2, l]
         heat[PAD + l] = pack[3, l]
 
-    def sides(even, odd, even5, odd5):
+    def sides(even, odd):
         for l in range(4):
             for f in range(2):
                 s0[f, even + l] = ev[f, l]
-                s0[f, odd + l] = od_at(4 * f + l)
+                s0[f, odd + l] = od[f, l]
             cnd[even + l] = evc[2, l]
             cnd[odd + l] = odc[2, l]
             heat[even + l] = evc[3, l]
             heat[odd + l] = odc[3, l]
-        s0[0, even5] = ev5[0:128]
-        s0[0, odd5] = od_at(8)
-        cnd[even5] = ev5[128:256]
-        cnd[odd5] = od_at(9)
 
     @pl.when(core == 0)
     def _():
-        sides(PAD + 4, 1, EXT - 1, 0)
+        sides(PAD + 4, 1)
 
     @pl.when(core == 1)
     def _():
-        sides(1, PAD + 4, 0, EXT - 1)
-
-    clear_outside(s, [s0.at[0], s0.at[1], cnd], 0, EXT)
+        sides(1, PAD + 4)
+
+    clear_outside(s, [s0.at[0], s0.at[1], cnd], 1, EXT - 1)
+    zero = jnp.zeros((128, 128), jnp.float32)
+    inside = s > 1
+    s0[0, 0] = jnp.where(inside, low[0], zero)
+    cnd[0] = jnp.where(inside, low[1], zero)
+    inside = s < NS - 2
+    s0[0, EXT - 1] = jnp.where(inside, high[0], zero)
+    cnd[EXT - 1] = jnp.where(inside, high[1], zero)
     set_coefficients(cnd, *coefficients, 0, EXT - 1)
     ratio = COARSE / FINE
     for f, h in ((0, 1), (1, 0)):
@@ -521,17 +523,16 @@
 
     a, c_got = lax.optimization_barrier((a, c_got))
     ev2 = even(a)
-    tail = lambda x: jnp.where(core == 0, x[0], x[3])
-    nearest = lambda x: jnp.where(core == 0, x[3], x[0])
-    od2 = odd(jnp.concatenate([a.reshape(1024, 128), tail(ev2[0]), tail(ev[2])]))
-    ev5 = even(jnp.concatenate([nearest(od2[:512].reshape(4, 128, 128)), nearest(od[2])]))
-    ev5, c_got = lax.optimization_barrier((ev5, c_got))
+    od2 = odd(a)
+    low = lax.ppermute(jnp.stack([a[0, 3], pack[2, 3]]), "space", [(i, (i + 2) % NS) for i in range(NS)])
+    high = lax.ppermute(jnp.stack([a[0, 0], pack[2, 0]]), "space", [(i, (i - 2) % NS) for i in range(NS)])
+    od2, c_got = lax.optimization_barrier((od2, c_got))
     c_swap = even(c_got)
     e, w = call(
         second_kernel,
         [struct(NT, 4, 8, 128), struct(4, 128, 128)],
         fine_scratch + [pltpu.VMEM((2, EXT, 128, 128), jnp.float32)],
-        a, pack, ev2, od2, ev, od, ev5,
+        a, pack, ev2, od2, ev, od, low, high,
     )
     e, w, c_swap = lax.optimization_barrier((e, w, c_swap))
     own = lax.all_to_all(e, "tm", 0, 0)

time: 162 us -> 159 us (0.981)
  waiting for transfers between devices: 63.7 us -> 55.7 us
  starting transfers between devices: 32.8 us -> 37.4 us
    ppermute x2, waiting for transfers between devices: 25.4 us -> 19.4 us  [odd(): return lax.ppermute(x, ('tm', 'space'), ODD)]
    ppermute x0 -> x2, starting transfers between devices: none -> 5.78 us  [the longest x1 5.7 us: body(): lax.ppermute(jnp.stack([a[0, 0], pack[2, 0]]), 'space', [(i, (i - 2) % NS...]
    ppermute x13 -> x12, waiting for transfers between devices: 15.3 us -> 12.1 us  [even(): return lax.ppermute(x, 'space', EVEN)]
  transfers between devices with their start and end apart: 25 -> 26, of which waited for: 21 -> 20; matrix products, arithmetic and copies ran while one was open for 0% -> 0% of each run, Pallas kernels for 7% -> 7%
where the time goes in v7:
time: 159 us; the launch traced here: 158 us
  waiting for transfers between devices  55.7 us (35%)
  blocking collectives  44.9 us (28%)
  starting transfers between devices  37.4 us (24%)
  Pallas kernels  18 us (11%)
    all_to_all x1, blocking collectives, body(): back = lax.all_to_all(jnp.concatenate(parts), 'tm', 0, 0)  23.1 us
    all_to_all x1, blocking collectives, body(): own = lax.all_to_all(e, 'tm', 0, 0)  21.8 us
    ppermute x2, waiting for transfers between devices, odd(): return lax.ppermute(x, ('tm', 'space'), ODD)  19.4 us
    pallas_call x10, Pallas kernels, call(): pl.pallas_call(kernel, out_shape=outs, in_specs=[VMEM] * len(args), out_s...  18 us
    ppermute x4, waiting for transfers between devices, yodd(): return lax.ppermute(x, ('tm', 'space'), YODD)  13.1 us
    ppermute x5, starting transfers between devices, xodd(): return lax.ppermute(x, ('tm', 'space'), XODD)  12.8 us
    ppermute x12, waiting for transfers between devices, even(): return lax.ppermute(x, 'space', EVEN)  12.1 us
    ppermute x4, starting transfers between devices, yodd(): return lax.ppermute(x, ('tm', 'space'), YODD)  11.9 us
  transfers between devices with their start and end apart: 26, of which 20 were waited for; matrix products, arithmetic and copies ran while one was open for 0% of the time, Pallas kernels for 7%

profile of v7, /device:TPU:16, one launch (start us, length us, event | category | flops | bytes accessed | tf_op | source)
XLA Modules:
  0.0 157.9 jit_solution(17718106233273378848)
XLA Ops:
  0.0 1.4 maximum_select_fusion.pack
  1.4 0.1 collective-permute-start
  1.6 2.6 %collective-permute-start.1 = (f32[4,4,128,128]{3,2,1,0:T(8,128)S(1)}, f32[4,4,128,128]{3,2,1,0:T(8,128)S(1)}, u32[]{:S(2)}, u32[]{:S(2)}) collective-permute-start(f32[4,4,128,128]{3,2,1,0:T(8,128)S(1)} %maximum_select_fusion.pack), channel_id=1, source_target_pairs={{0,32},{1,2},{2,1},{3,4},{4,3},{5,6},{6,5},{7,8},{8,7},{9,10},{10,... | collective-permute-start | bytes 3145736 | tf_op jit(solution)/shard_map/ppermute | solution.py:65
  4.2 0.0 collective-permute-done.ev.evc
  4.3 2.4 %collective-permute-start.2 = (f32[8,24,128]{2,1,0:T(8,128)S(1)}, f32[8,24,128]{2,1,0:T(8,128)S(1)}, u32[]{:S(2)}, u32[]{:S(2)}) collective-permute-start(f32[8,24,128]{2,1,0:T(8,128)S(1)} %maximum_select_fusion.1.cond), channel_id=1, source_target_pairs={{0,32},{1,2},{2,1},{3,4},{4,3},{5,6},{6,5},{7,24},{8,23},{9,10},{1... | collective-permute-start | bytes 294920 | tf_op jit(solution)/shard_map/ppermute | solution.py:69
  6.7 13.5 %collective-permute-done.1.od.odc = f32[4,4,128,128]{3,2,1,0:T(8,128)S(1)} collective-permute-done((f32[4,4,128,128]{3,2,1,0:T(8,128)S(1)}, f32[4,4,128,128]{3,2,1,0:T(8,128)S(1)}, u32[]{:S(2)}, u32[]{:S(2)}) %collective-permute-start.1) | collective-permute-done | bytes 1048608 | tf_op jit(solution)/shard_map/ppermute | solution.py:65
  20.3 3.4 %shard_map.46.a = f32[2,4,128,128]{3,2,1,0:T(8,128)S(1)} custom-call(f32[4,4,128,128]{3,2,1,0:T(8,128)S(1)} %maximum_select_fusion.pack, f32[4,4,128,128]{3,2,1,0:T(8,128)S(1)} %collective-permute-done.ev.evc, f32[4,4,128,128]{3,2,1,0:T(8,128)S(1)} %collective-permute-done.1.od.odc), custom_call_target="tpu_custom_call" | custom-call | tf_op jit(solution)/shard_map/pallas_call | solution.py:494
  23.6 0.0 collective-permute-done.2.cond_got
  23.6 1.8 %collective-permute-start.4 = (f32[2,4,128,128]{3,2,1,0:T(8,128)S(1)}, f32[2,4,128,128]{3,2,1,0:T(8,128)S(1)}, u32[]{:S(2)}, u32[]{:S(2)}) collective-permute-start(f32[2,4,128,128]{3,2,1,0:T(8,128)S(1)} %shard_map.46.a), channel_id=1, source_target_pairs={{0,32},{1,2},{2,1},{3,4},{4,3},{5,6},{6,5},{7,8},{8,7},{9,10},{10,... | collective-permute-start | bytes 1572872 | tf_op jit(solution)/shard_map/ppermute | solution.py:65
  25.5 0.1 collective-permute-start.3
  25.6 0.1 collective-permute-start.5
  25.7 5.7 %collective-permute-start.6 = (f32[2,128,128]{2,1,0:T(8,128)S(1)}, f32[2,128,128]{2,1,0:T(8,128)S(1)}, u32[]{:S(2)}, u32[]{:S(2)}) collective-permute-start(f32[2,128,128]{2,1,0:T(8,128)S(1)} %pad_maximum_fusion.2), channel_id=1, source_target_pairs={{0,14},{1,15},{2,0},{3,1},{4,2},{5,3},{6,4},{7,5},{8,6},{9,7},{10,... | collective-permute-start | bytes 393224 | tf_op jit(solution)/shard_map/ppermute | solution.py:528
  31.4 5.9 %collective-permute-done.4.od = f32[2,4,128,128]{3,2,1,0:T(8,128)S(1)} collective-permute-done((f32[2,4,128,128]{3,2,1,0:T(8,128)S(1)}, f32[2,4,128,128]{3,2,1,0:T(8,128)S(1)}, u32[]{:S(2)}, u32[]{:S(2)}) %collective-permute-start.4) | collective-permute-done | bytes 524320 | tf_op jit(solution)/shard_map/ppermute | solution.py:65
  37.3 0.0 collective-permute-start.7
  37.3 0.0 collective-permute-done.5.low
  37.3 0.0 collective-permute-done.6.high
  37.4 0.0 collective-permute-done.3.ev
  37.4 4.7 %shard_map.47 = (f32[16,4,8,128]{3,2,1,0:T(8,128)S(1)}, f32[4,128,128]{2,1,0:T(8,128)S(1)}) custom-call(f32[2,4,128,128]{3,2,1,0:T(8,128)S(1)} %shard_map.46.a, f32[4,4,128,128]{3,2,1,0:T(8,128)S(1)} %maximum_select_fusion.pack, f32[2,4,128,128]{3,2,1,0:T(8,128)S(1)} %collective-permute-done.3.ev, f32[2,4,128,128]{3,2,1,0:T(8,128)S(1)} %collective-permute-done.4.od, ...), custom_call_target="tpu_custom_call" | custom-call | tf_op jit(solution)/shard_map/pallas_call | solution.py:494
  42.1 0.0 collective-permute-done.7.cond_swap
  42.1 21.8 %all_to_all.10.own = f32[16,4,8,128]{3,2,1,0:T(8,128)S(1)} all-to-all(f32[16,4,8,128]{3,2,1,0:T(8,128)S(1)} %get-tuple-element.41), channel_id=1, replica_groups=mesh['tm'=16,'space'=16] {'tm'}, dimensions={0} | all-to-all | bytes 524288 | tf_op jit(solution)/shard_map/all_to_all | solution.py:538
  63.8 0.0 collective-permute-start.8
  63.8 1.5 collective-permute-done.8.other
  65.4 0.1 shard_map.48
  65.5 3.2 %collective-permute-start.9 = (f32[4,12,8,128]{3,2,1,0:T(8,128)S(1)}, f32[4,12,8,128]{3,2,1,0:T(8,128)S(1)}, u32[]{:S(2)}, u32[]{:S(2)}) collective-permute-start(f32[4,12,8,128]{3,2,1,0:T(8,128)S(1)} %get-tuple-element.47), channel_id=1, source_target_pairs={{0,32},{1,2},{2,1},{3,4},{4,3},{5,6},{6,5},{7,24},{8,23},{9,10},{1... | collective-permute-start | bytes 589832 | tf_op jit(solution)/shard_map/ppermute | solution.py:69
  68.6 2.3 %collective-permute-start.11 = (f32[4,128,128]{2,1,0:T(8,128)S(1)}, f32[4,128,128]{2,1,0:T(8,128)S(1)}, u32[]{:S(2)}, u32[]{:S(2)}) collective-permute-start(f32[4,128,128]{2,1,0:T(8,128)S(1)} %get-tuple-element.48), channel_id=1, source_target_pairs={{0,16},{16,32},{32,48},{48,64},{64,80},{80,96},{96,112},{112,128},... | collective-permute-start | bytes 786440 | tf_op jit(solution)/shard_map/ppermute | solution.py:540
  70.9 1.9 %collective-permute-done.9.got.xg = f32[4,12,8,128]{3,2,1,0:T(8,128)S(1)} collective-permute-done((f32[4,12,8,128]{3,2,1,0:T(8,128)S(1)}, f32[4,12,8,128]{3,2,1,0:T(8,128)S(1)}, u32[]{:S(2)}, u32[]{:S(2)}) %collective-permute-start.9) | collective-permute-done | bytes 196640 | tf_op jit(solution)/shard_map/ppermute | solution.py:69
  72.7 0.0 collective-permute-start.10
  72.7 1.4 collective-permute-done.10.swap.xs
  74.2 0.1 shard_map.49
  74.3 2.8 %collective-permute-done.11.w = f32[4,128,128]{2,1,0:T(8,128)S(1)} collective-permute-done((f32[4,128,128]{2,1,0:T(8,128)S(1)}, f32[4,128,128]{2,1,0:T(8,128)S(1)}, u32[]{:S(2)}, u32[]{:S(2)}) %collective-permute-start.11) | collective-permute-done | bytes 262176 | tf_op jit(solution)/shard_map/ppermute | solution.py:540
  77.1 0.0 collective-permute-start.12
  77.1 6.1 %collective-permute-done.12.yg = f32[4,18,8,128]{3,2,1,0:T(8,128)S(1)} collective-permute-done((f32[4,18,8,128]{3,2,1,0:T(8,128)S(1)}, f32[4,18,8,128]{3,2,1,0:T(8,128)S(1)}, u32[]{:S(2)}, u32[]{:S(2)}) %collective-permute-start.12) | collective-permute-done | bytes 294944 | tf_op jit(solution)/shard_map/ppermute | solution.py:73
  83.3 0.0 collective-permute-start.13
  83.3 1.6 %collective-permute-done.13.ys = f32[4,18,8,128]{3,2,1,0:T(8,128)S(1)} collective-permute-done((f32[4,18,8,128]{3,2,1,0:T(8,128)S(1)}, f32[4,18,8,128]{3,2,1,0:T(8,128)S(1)}, u32[]{:S(2)}, u32[]{:S(2)}) %collective-permute-start.13) | collective-permute-done | bytes 294944 | tf_op jit(solution)/shard_map/ppermute | solution.py:61
  84.8 1.1 shard_map.50
  86.0 1.3 collective-permute-start.14
  87.3 3.0 %shard_map.51 = (f32[12,4,8,128]{3,2,1,0:T(8,128)S(1)}, f32[12,4,8,128]{3,2,1,0:T(8,128)S(1)}, f32[3,8,8,128]{3,2,1,0:T(8,128)S(1)}) custom-call(f32[24,24,128]{2,1,0:T(8,128)S(1)} %get-tuple-element.45.cond, f32[16,8,8,128]{3,2,1,0:T(8,128)S(1)} %get-tuple-element.46.chip, f32[4,12,8,128]{3,2,1,0:T(8,128)S(1)} %collective-permute-done.9.got.xg, ...), custom_call_target="tpu_custom_call" | custom-call | flops 30000000 | bytes 4000000 | tf_op jit(solution)/shard_map/pallas_call | solution.py:494
  90.3 1.2 collective-permute-done.14.xg
  91.5 0.0 collective-permute-start.15
  91.5 1.2 collective-permute-done.15.xs
  92.7 3.4 %collective-permute-start.16 = (f32[24,8,128]{2,1,0:T(8,128)S(1)}, f32[24,8,128]{2,1,0:T(8,128)S(1)}, u32[]{:S(2)}, u32[]{:S(2)}) collective-permute-start(f32[24,8,128]{2,1,0:T(8,128)S(1)} %pad_maximum_fusion.3), channel_id=1, source_target_pairs={{0,225},{1,16},{2,227},{3,18},{4,229},{5,20},{6,231},{7,22},{8,25}... | collective-permute-start | bytes 294920 | tf_op jit(solution)/shard_map/ppermute | solution.py:73
  96.1 2.3 %collective-permute-done.16.yg = f32[24,8,128]{2,1,0:T(8,128)S(1)} collective-permute-done((f32[24,8,128]{2,1,0:T(8,128)S(1)}, f32[24,8,128]{2,1,0:T(8,128)S(1)}, u32[]{:S(2)}, u32[]{:S(2)}) %collective-permute-start.16) | collective-permute-done | bytes 98336 | tf_op jit(solution)/shard_map/ppermute | solution.py:73
  98.4 0.0 collective-permute-start.17
  98.4 1.3 collective-permute-done.17.ys
  99.7 1.4 shard_map.52
  101.1 3.0 %collective-permute-start.18 = (f32[8,8,128]{2,1,0:T(8,128)S(1)}, f32[8,8,128]{2,1,0:T(8,128)S(1)}, u32[]{:S(2)}, u32[]{:S(2)}) collective-permute-start(f32[8,8,128]{2,1,0:T(8,128)S(1)} %get-tuple-element.60.c_in), channel_id=1, source_target_pairs={{0,32},{1,2},{2,1},{3,4},{4,3},{5,6},{6,5},{7,24},{8,23},{9,10},{1... | collective-permute-start | bytes 98312 | tf_op jit(solution)/shard_map/ppermute | solution.py:69
  104.2 2.5 %collective-permute-done.18.xg = f32[8,8,128]{2,1,0:T(8,128)S(1)} collective-permute-done((f32[8,8,128]{2,1,0:T(8,128)S(1)}, f32[8,8,128]{2,1,0:T(8,128)S(1)}, u32[]{:S(2)}, u32[]{:S(2)}) %collective-permute-start.18) | collective-permute-done | bytes 32800 | tf_op jit(solution)/shard_map/ppermute | solution.py:69
  106.7 0.0 collective-permute-start.19
  106.7 1.2 collective-permute-done.19.xs
  107.9 4.2 %collective-permute-start.20 = (f32[24,8,128]{2,1,0:T(8,128)S(1)}, f32[24,8,128]{2,1,0:T(8,128)S(1)}, u32[]{:S(2)}, u32[]{:S(2)}) collective-permute-start(f32[24,8,128]{2,1,0:T(8,128)S(1)} %pad_maximum_fusion.4), channel_id=1, source_target_pairs={{0,225},{1,16},{2,227},{3,18},{4,229},{5,20},{6,231},{7,22},{8,25}... | collective-permute-start | bytes 294920 | tf_op jit(solution)/shard_map/ppermute | solution.py:73
  112.2 2.3 %collective-permute-done.20.yg = f32[24,8,128]{2,1,0:T(8,128)S(1)} collective-permute-done((f32[24,8,128]{2,1,0:T(8,128)S(1)}, f32[24,8,128]{2,1,0:T(8,128)S(1)}, u32[]{:S(2)}, u32[]{:S(2)}) %collective-permute-start.20) | collective-permute-done | bytes 98336 | tf_op jit(solution)/shard_map/ppermute | solution.py:73
  114.5 1.3 collective-permute-done.21.ys
  115.8 1.4 shard_map.53
  117.2 2.9 %collective-permute-start.22 = (f32[8,8,128]{2,1,0:T(8,128)S(1)}, f32[8,8,128]{2,1,0:T(8,128)S(1)}, u32[]{:S(2)}, u32[]{:S(2)}) collective-permute-start(f32[8,8,128]{2,1,0:T(8,128)S(1)} %get-tuple-element.62.c_in), channel_id=1, source_target_pairs={{0,32},{1,2},{2,1},{3,4},{4,3},{5,6},{6,5},{7,24},{8,23},{9,10},{1... | collective-permute-start | bytes 98312 | tf_op jit(solution)/shard_map/ppermute | solution.py:69
  120.0 2.7 %collective-permute-done.22.xg = f32[8,8,128]{2,1,0:T(8,128)S(1)} collective-permute-done((f32[8,8,128]{2,1,0:T(8,128)S(1)}, f32[8,8,128]{2,1,0:T(8,128)S(1)}, u32[]{:S(2)}, u32[]{:S(2)}) %collective-permute-start.22) | collective-permute-done | bytes 32800 | tf_op jit(solution)/shard_map/ppermute | solution.py:69
  122.7 0.0 collective-permute-start.23
  122.7 1.2 collective-permute-done.23.xs
  124.0 4.2 %collective-permute-start.24 = (f32[24,8,128]{2,1,0:T(8,128)S(1)}, f32[24,8,128]{2,1,0:T(8,128)S(1)}, u32[]{:S(2)}, u32[]{:S(2)}) collective-permute-start(f32[24,8,128]{2,1,0:T(8,128)S(1)} %pad_maximum_fusion.5), channel_id=1, source_target_pairs={{0,225},{1,16},{2,227},{3,18},{4,229},{5,20},{6,231},{7,22},{8,25}... | collective-permute-start | bytes 294920 | tf_op jit(solution)/shard_map/ppermute | solution.py:73
  128.2 2.3 %collective-permute-done.24.yg = f32[24,8,128]{2,1,0:T(8,128)S(1)} collective-permute-done((f32[24,8,128]{2,1,0:T(8,128)S(1)}, f32[24,8,128]{2,1,0:T(8,128)S(1)}, u32[]{:S(2)}, u32[]{:S(2)}) %collective-permute-start.24) | collective-permute-done | bytes 98336 | tf_op jit(solution)/shard_map/ppermute | solution.py:73
  130.5 0.0 collective-permute-start.25
  130.5 1.3 collective-permute-done.25.ys
  131.8 2.0 %shard_map.54 = (f32[8,8,128]{2,1,0:T(8,128)}, f32[4,2,4,8,128]{4,3,2,1,0:T(8,128)S(1)}) custom-call(f32[24,24,128]{2,1,0:T(8,128)S(1)} %get-tuple-element.45.cond, f32[8,8,128]{2,1,0:T(8,128)S(1)} %get-tuple-element.62.c_in, f32[12,4,8,128]{3,2,1,0:T(8,128)S(1)} %get-tuple-element.55.p, f32[12,4,8,128]{3,2,1,0:T(8,128)S(1)} %get-tuple-element.56.zp, ...), custom_call_target="tpu_custom_call" | custom-call | tf_op jit(solution)/shard_map/pallas_call | solution.py:494
  133.9 23.1 %all_to_all.11.got = f32[16,2,4,8,128]{4,3,2,1,0:T(8,128)S(1)} all-to-all(f32[16,2,4,8,128]{4,3,2,1,0:T(8,128)S(1)} %pad_maximum_fusion), channel_id=1, replica_groups=mesh['tm'=16,'space'=16] {'tm'}, dimensions={0} | all-to-all | bytes 1048576 | tf_op jit(solution)/shard_map/all_to_all | solution.py:586
  157.0 0.8 shard_map.55
  (18 shorter events, 0.2 us)
Async XLA Ops:
  1.4 2.8 %collective-permute-start = (f32[4,4,128,128]{3,2,1,0:T(8,128)S(1)}, f32[4,4,128,128]{3,2,1,0:T(8,128)S(1)}, u32[]{:S(2)}, u32[]{:S(2)}) collective-permute-start(f32[4,4,128,128]{3,2,1,0:T(8,128)S(1)} %maximum_select_fusion.pack), channel_id=1, source_target_pairs={{0,1},{1,0},{2,3},{3,2},{4,5},{5,4},{6,7},{7,6},{8,9},{9,8},{10,11... | collective-permute-start | bytes 3145736 | tf_op jit(solution)/shard_map/ppermute | solution.py:61
  1.6 18.7 %collective-permute-start.1 = (f32[4,4,128,128]{3,2,1,0:T(8,128)S(1)}, f32[4,4,128,128]{3,2,1,0:T(8,128)S(1)}, u32[]{:S(2)}, u32[]{:S(2)}) collective-permute-start(f32[4,4,128,128]{3,2,1,0:T(8,128)S(1)} %maximum_select_fusion.pack), channel_id=1, source_target_pairs={{0,32},{1,2},{2,1},{3,4},{4,3},{5,6},{6,5},{7,8},{8,7},{9,10},{10,... | collective-permute-start | bytes 3145736 | tf_op jit(solution)/shard_map/ppermute | solution.py:65
  4.3 19.3 %collective-permute-start.2 = (f32[8,24,128]{2,1,0:T(8,128)S(1)}, f32[8,24,128]{2,1,0:T(8,128)S(1)}, u32[]{:S(2)}, u32[]{:S(2)}) collective-permute-start(f32[8,24,128]{2,1,0:T(8,128)S(1)} %maximum_select_fusion.1.cond), channel_id=1, source_target_pairs={{0,32},{1,2},{2,1},{3,4},{4,3},{5,6},{6,5},{7,24},{8,23},{9,10},{1... | collective-permute-start | bytes 294920 | tf_op jit(solution)/shard_map/ppermute | solution.py:69
  23.6 13.7 %collective-permute-start.4 = (f32[2,4,128,128]{3,2,1,0:T(8,128)S(1)}, f32[2,4,128,128]{3,2,1,0:T(8,128)S(1)}, u32[]{:S(2)}, u32[]{:S(2)}) collective-permute-start(f32[2,4,128,128]{3,2,1,0:T(8,128)S(1)} %shard_map.46.a), channel_id=1, source_target_pairs={{0,32},{1,2},{2,1},{3,4},{4,3},{5,6},{6,5},{7,8},{8,7},{9,10},{10,... | collective-permute-start | bytes 1572872 | tf_op jit(solution)/shard_map/ppermute | solution.py:65
  25.5 11.9 %collective-permute-start.3 = (f32[2,4,128,128]{3,2,1,0:T(8,128)S(1)}, f32[2,4,128,128]{3,2,1,0:T(8,128)S(1)}, u32[]{:S(2)}, u32[]{:S(2)}) collective-permute-start(f32[2,4,128,128]{3,2,1,0:T(8,128)S(1)} %shard_map.46.a), channel_id=1, source_target_pairs={{0,1},{1,0},{2,3},{3,2},{4,5},{5,4},{6,7},{7,6},{8,9},{9,8},{10,11... | collective-permute-start | bytes 1572872 | tf_op jit(solution)/shard_map/ppermute | solution.py:61
  25.6 11.7 %collective-permute-start.5 = (f32[2,128,128]{2,1,0:T(8,128)S(1)}, f32[2,128,128]{2,1,0:T(8,128)S(1)}, u32[]{:S(2)}, u32[]{:S(2)}) collective-permute-start(f32[2,128,128]{2,1,0:T(8,128)S(1)} %pad_maximum_fusion.1), channel_id=1, source_target_pairs={{0,2},{1,3},{2,4},{3,5},{4,6},{5,7},{6,8},{7,9},{8,10},{9,11},{10,... | collective-permute-start | bytes 393224 | tf_op jit(solution)/shard_map/ppermute | solution.py:527
  25.7 11.6 %collective-permute-start.6 = (f32[2,128,128]{2,1,0:T(8,128)S(1)}, f32[2,128,128]{2,1,0:T(8,128)S(1)}, u32[]{:S(2)}, u32[]{:S(2)}) collective-permute-start(f32[2,128,128]{2,1,0:T(8,128)S(1)} %pad_maximum_fusion.2), channel_id=1, source_target_pairs={{0,14},{1,15},{2,0},{3,1},{4,2},{5,3},{6,4},{7,5},{8,6},{9,7},{10,... | collective-permute-start | bytes 393224 | tf_op jit(solution)/shard_map/ppermute | solution.py:528
  37.3 4.7 %collective-permute-start.7 = (f32[8,24,128]{2,1,0:T(8,128)S(1)}, f32[8,24,128]{2,1,0:T(8,128)S(1)}, u32[]{:S(2)}, u32[]{:S(2)}) collective-permute-start(f32[8,24,128]{2,1,0:T(8,128)S(1)} %collective-permute-done.2.cond_got), channel_id=1, source_target_pairs={{0,1},{1,0},{2,3},{3,2},{4,5},{5,4},{6,7},{7,6},{8,9},{9,8},{10,11... | collective-permute-start | bytes 294920 | tf_op jit(solution)/shard_map/ppermute | solution.py:61
  63.8 1.5 collective-permute-start.8
  65.5 7.3 %collective-permute-start.9 = (f32[4,12,8,128]{3,2,1,0:T(8,128)S(1)}, f32[4,12,8,128]{3,2,1,0:T(8,128)S(1)}, u32[]{:S(2)}, u32[]{:S(2)}) collective-permute-start(f32[4,12,8,128]{3,2,1,0:T(8,128)S(1)} %get-tuple-element.47), channel_id=1, source_target_pairs={{0,32},{1,2},{2,1},{3,4},{4,3},{5,6},{6,5},{7,24},{8,23},{9,10},{1... | collective-permute-start | bytes 589832 | tf_op jit(solution)/shard_map/ppermute | solution.py:69
  68.6 8.5 %collective-permute-start.11 = (f32[4,128,128]{2,1,0:T(8,128)S(1)}, f32[4,128,128]{2,1,0:T(8,128)S(1)}, u32[]{:S(2)}, u32[]{:S(2)}) collective-permute-start(f32[4,128,128]{2,1,0:T(8,128)S(1)} %get-tuple-element.48), channel_id=1, source_target_pairs={{0,16},{16,32},{32,48},{48,64},{64,80},{80,96},{96,112},{112,128},... | collective-permute-start | bytes 786440 | tf_op jit(solution)/shard_map/ppermute | solution.py:540
  72.7 1.4 collective-permute-start.10
  77.1 6.1 %collective-permute-start.12 = (f32[4,18,8,128]{3,2,1,0:T(8,128)S(1)}, f32[4,18,8,128]{3,2,1,0:T(8,128)S(1)}, u32[]{:S(2)}, u32[]{:S(2)}) collective-permute-start(f32[4,18,8,128]{3,2,1,0:T(8,128)S(1)} %shard_map.49), channel_id=1, source_target_pairs={{0,225},{1,16},{2,227},{3,18},{4,229},{5,20},{6,231},{7,22},{8,25}... | collective-permute-start | bytes 884744 | tf_op jit(solution)/shard_map/ppermute | solution.py:73
  83.3 1.6 %collective-permute-start.13 = (f32[4,18,8,128]{3,2,1,0:T(8,128)S(1)}, f32[4,18,8,128]{3,2,1,0:T(8,128)S(1)}, u32[]{:S(2)}, u32[]{:S(2)}) collective-permute-start(f32[4,18,8,128]{3,2,1,0:T(8,128)S(1)} %collective-permute-done.12.yg), channel_id=1, source_target_pairs={{0,1},{1,0},{2,3},{3,2},{4,5},{5,4},{6,7},{7,6},{8,9},{9,8},{10,11... | collective-permute-start | bytes 884744 | tf_op jit(solution)/shard_map/ppermute | solution.py:61
  86.0 5.5 %collective-permute-start.14 = (f32[8,8,128]{2,1,0:T(8,128)S(1)}, f32[8,8,128]{2,1,0:T(8,128)S(1)}, u32[]{:S(2)}, u32[]{:S(2)}) collective-permute-start(f32[8,8,128]{2,1,0:T(8,128)S(1)} %get-tuple-element.51.c_in), channel_id=1, source_target_pairs={{0,32},{1,2},{2,1},{3,4},{4,3},{5,6},{6,5},{7,24},{8,23},{9,10},{1... | collective-permute-start | bytes 98312 | tf_op jit(solution)/shard_map/ppermute | solution.py:69
  91.5 1.2 collective-permute-start.15
  92.7 5.7 %collective-permute-start.16 = (f32[24,8,128]{2,1,0:T(8,128)S(1)}, f32[24,8,128]{2,1,0:T(8,128)S(1)}, u32[]{:S(2)}, u32[]{:S(2)}) collective-permute-start(f32[24,8,128]{2,1,0:T(8,128)S(1)} %pad_maximum_fusion.3), channel_id=1, source_target_pairs={{0,225},{1,16},{2,227},{3,18},{4,229},{5,20},{6,231},{7,22},{8,25}... | collective-permute-start | bytes 294920 | tf_op jit(solution)/shard_map/ppermute | solution.py:73
  98.4 1.3 collective-permute-start.17
  101.1 5.5 %collective-permute-start.18 = (f32[8,8,128]{2,1,0:T(8,128)S(1)}, f32[8,8,128]{2,1,0:T(8,128)S(1)}, u32[]{:S(2)}, u32[]{:S(2)}) collective-permute-start(f32[8,8,128]{2,1,0:T(8,128)S(1)} %get-tuple-element.60.c_in), channel_id=1, source_target_pairs={{0,32},{1,2},{2,1},{3,4},{4,3},{5,6},{6,5},{7,24},{8,23},{9,10},{1... | collective-permute-start | bytes 98312 | tf_op jit(solution)/shard_map/ppermute | solution.py:69
  106.7 1.2 collective-permute-start.19
  107.9 6.5 %collective-permute-start.20 = (f32[24,8,128]{2,1,0:T(8,128)S(1)}, f32[24,8,128]{2,1,0:T(8,128)S(1)}, u32[]{:S(2)}, u32[]{:S(2)}) collective-permute-start(f32[24,8,128]{2,1,0:T(8,128)S(1)} %pad_maximum_fusion.4), channel_id=1, source_target_pairs={{0,225},{1,16},{2,227},{3,18},{4,229},{5,20},{6,231},{7,22},{8,25}... | collective-permute-start | bytes 294920 | tf_op jit(solution)/shard_map/ppermute | solution.py:73
  114.5 1.3 collective-permute-start.21
  117.2 5.5 %collective-permute-start.22 = (f32[8,8,128]{2,1,0:T(8,128)S(1)}, f32[8,8,128]{2,1,0:T(8,128)S(1)}, u32[]{:S(2)}, u32[]{:S(2)}) collective-permute-start(f32[8,8,128]{2,1,0:T(8,128)S(1)} %get-tuple-element.62.c_in), channel_id=1, source_target_pairs={{0,32},{1,2},{2,1},{3,4},{4,3},{5,6},{6,5},{7,24},{8,23},{9,10},{1... | collective-permute-start | bytes 98312 | tf_op jit(solution)/shard_map/ppermute | solution.py:69
  122.7 1.2 collective-permute-start.23
  124.0 6.5 %collective-permute-start.24 = (f32[24,8,128]{2,1,0:T(8,128)S(1)}, f32[24,8,128]{2,1,0:T(8,128)S(1)}, u32[]{:S(2)}, u32[]{:S(2)}) collective-permute-start(f32[24,8,128]{2,1,0:T(8,128)S(1)} %pad_maximum_fusion.5), channel_id=1, source_target_pairs={{0,225},{1,16},{2,227},{3,18},{4,229},{5,20},{6,231},{7,22},{8,25}... | collective-permute-start | bytes 294920 | tf_op jit(solution)/shard_map/ppermute | solution.py:73
  130.5 1.3 collective-permute-start.25

commit v8 on v7

--- a/solution.py
+++ b/solution.py
@@ -383,6 +383,9 @@
     core = lax.axis_index("space") % 2
     for value, ref in zip(region(cond, 6), coef):
         ref[...] = value
+    if 0 not in groups:
+        for value, ref in zip(region(cond, 8), outs[3:]):
+            ref[...] = value
     for h, buf in zip(HALOS, (b0, b1, b2)):
         buf[...] = jnp.zeros((8 + 2 * h, 24, 128), jnp.float32)
     c = tuple(r[...] for r in coef)
@@ -427,17 +430,16 @@
                 done[i, 0] = partial[i]
                 done[i, 1] = half(core, values[i])
         else:
-            p_out, zp_out, ends = outs
+            p_out, zp_out, ends = outs[:3]
             ends[q - 1] = values[3]
             for i in range(4):
                 p_out[4 * q - 4 + i] = half(core, values[i])
                 zp_out[4 * q - 4 + i] = partial[i]
 
 
-def chain_kernel(q, cond, c_in, p, zp, ends, xg, xs, yg, ys, last, done, buf, *coef):
+def chain_kernel(q, c_in, p, zp, ends, xg, xs, yg, ys, mask, kx, ky, kz, bb, done, *rest):
+    buf = rest[-1]
     core = lax.axis_index("space") % 2
-    for value, ref in zip(region(cond, 8), coef):
-        ref[...] = value
     buf[8:16, 8:16] = c_in[...]
 
     def put(left, right, below, above):
@@ -454,7 +456,7 @@
     def _():
         put(xs, xg, ys, yg)
 
-    c = tuple(r[...] for r in coef)
+    c = tuple(r[...] for r in (mask, kx, ky, kz, bb))
     v = buf[...] * c[0]
     for turn in range(8):
         v = coarse_step(v, c, 8, 8 - turn)
@@ -464,7 +466,8 @@
             done[i, 0] = zp[4 * q - 4 + i] + half(core, tile)
         else:
             done[i, 1] = p[4 * q - 4 + i] + half(core, tile)
-    last[...] = ends[q - 1] + tile
+    if q < 3:
+        rest[0][...] = ends[q - 1] + tile
 
 
 def final_kernel(got, w, out):
@@ -559,9 +562,10 @@
         quad_scratch,
         tiles, chips, xg, xs, yg, ys,
     )
-    p, zp, ends = call(
+    p, zp, ends, *chain_coefficients = call(
         functools.partial(quads_kernel, (1, 2, 3)),
-        [struct(12, 4, 8, 128), struct(12, 4, 8, 128), struct(3, 8, 8, 128)],
+        [struct(12, 4, 8, 128), struct(12, 4, 8, 128), struct(3, 8, 8, 128)]
+        + [struct(24 - (k == 1), 24, 128) for k in range(5)],
         quad_scratch,
         tiles, chips, xg, xs, yg, ys,
         cost=pl.CostEstimate(flops=30_000_000, bytes_accessed=4_000_000, transcendentals=0),
@@ -576,13 +580,14 @@
         right = jnp.where(core == 0, xs, xg)
         yg = yodd(jnp.concatenate([left, last, right]))
         ys = even(yg)
-        last, done = call(
+        done, *last = call(
             functools.partial(chain_kernel, q),
-            [struct(8, 8, 128), struct(4, 2, 4, 8, 128)],
-            [pltpu.VMEM((24, 24, 128), jnp.float32)] + coefficient_scratch(8),
-            tiles, last, p, zp, ends, xg, xs, yg, ys,
+            [struct(4, 2, 4, 8, 128)] + [struct(8, 8, 128)] * (q < 3),
+            [pltpu.VMEM((24, 24, 128), jnp.float32)],
+            last, p, zp, ends, xg, xs, yg, ys, *chain_coefficients,
         )
         parts.append(done)
+        last = last[0] if last else None
     back = lax.all_to_all(jnp.concatenate(parts), "tm", 0, 0)
     (out,) = call(final_kernel, [struct(2, 4, 128, 128)], [], back, w_before)
     return out

time: 159 us -> 158 us (level)
  no operation moved by 1% of the time
where the time goes in v8:
time: 158 us; the launch traced here: 157 us
  waiting for transfers between devices  56.3 us (36%)
  blocking collectives  44.9 us (28%)
  starting transfers between devices  36.8 us (23%)
  Pallas kernels  17.4 us (11%)
    all_to_all x1, blocking collectives, body(): back = lax.all_to_all(jnp.concatenate(parts), 'tm', 0, 0)  23.1 us
    all_to_all x1, blocking collectives, body(): own = lax.all_to_all(e, 'tm', 0, 0)  21.8 us
    ppermute x2, waiting for transfers between devices, odd(): return lax.ppermute(x, ('tm', 'space'), ODD)  19.4 us
    pallas_call x10, Pallas kernels, call(): pl.pallas_call(kernel, out_shape=outs, in_specs=[VMEM] * len(args), out_s...  17.4 us
    ppermute x4, waiting for transfers between devices, yodd(): return lax.ppermute(x, ('tm', 'space'), YODD)  13.1 us
    ppermute x12, waiting for transfers between devices, even(): return lax.ppermute(x, 'space', EVEN)  12.1 us
    ppermute x5, starting transfers between devices, xodd(): return lax.ppermute(x, ('tm', 'space'), XODD)  12 us
    ppermute x4, starting transfers between devices, yodd(): return lax.ppermute(x, ('tm', 'space'), YODD)  12 us
  transfers between devices with their start and end apart: 26, of which 20 were waited for; matrix products, arithmetic and copies ran while one was open for 0% of the time, Pallas kernels for 7%

profile of v8, /device:TPU:16, one launch (start us, length us, event | category | flops | bytes accessed | tf_op | source)
XLA Modules:
  0.0 157.2 jit_solution(7204191930392276666)
XLA Ops:
  0.0 1.4 maximum_select_fusion.pack
  1.4 0.1 collective-permute-start
  1.6 2.6 %collective-permute-start.1 = (f32[4,4,128,128]{3,2,1,0:T(8,128)S(1)}, f32[4,4,128,128]{3,2,1,0:T(8,128)S(1)}, u32[]{:S(2)}, u32[]{:S(2)}) collective-permute-start(f32[4,4,128,128]{3,2,1,0:T(8,128)S(1)} %maximum_select_fusion.pack), channel_id=1, source_target_pairs={{0,32},{1,2},{2,1},{3,4},{4,3},{5,6},{6,5},{7,8},{8,7},{9,10},{10,... | collective-permute-start | bytes 3145736 | tf_op jit(solution)/shard_map/ppermute | solution.py:65
  4.2 0.0 collective-permute-done.ev.evc
  4.3 2.4 %collective-permute-start.2 = (f32[8,24,128]{2,1,0:T(8,128)S(1)}, f32[8,24,128]{2,1,0:T(8,128)S(1)}, u32[]{:S(2)}, u32[]{:S(2)}) collective-permute-start(f32[8,24,128]{2,1,0:T(8,128)S(1)} %maximum_select_fusion.1.cond), channel_id=1, source_target_pairs={{0,32},{1,2},{2,1},{3,4},{4,3},{5,6},{6,5},{7,24},{8,23},{9,10},{1... | collective-permute-start | bytes 294920 | tf_op jit(solution)/shard_map/ppermute | solution.py:69
  6.7 13.5 %collective-permute-done.1.od.odc = f32[4,4,128,128]{3,2,1,0:T(8,128)S(1)} collective-permute-done((f32[4,4,128,128]{3,2,1,0:T(8,128)S(1)}, f32[4,4,128,128]{3,2,1,0:T(8,128)S(1)}, u32[]{:S(2)}, u32[]{:S(2)}) %collective-permute-start.1) | collective-permute-done | bytes 1048608 | tf_op jit(solution)/shard_map/ppermute | solution.py:65
  20.3 3.4 %shard_map.46.a = f32[2,4,128,128]{3,2,1,0:T(8,128)S(1)} custom-call(f32[4,4,128,128]{3,2,1,0:T(8,128)S(1)} %maximum_select_fusion.pack, f32[4,4,128,128]{3,2,1,0:T(8,128)S(1)} %collective-permute-done.ev.evc, f32[4,4,128,128]{3,2,1,0:T(8,128)S(1)} %collective-permute-done.1.od.odc), custom_call_target="tpu_custom_call" | custom-call | tf_op jit(solution)/shard_map/pallas_call | solution.py:497
  23.6 0.0 collective-permute-done.2.cond_got
  23.6 1.8 %collective-permute-start.4 = (f32[2,4,128,128]{3,2,1,0:T(8,128)S(1)}, f32[2,4,128,128]{3,2,1,0:T(8,128)S(1)}, u32[]{:S(2)}, u32[]{:S(2)}) collective-permute-start(f32[2,4,128,128]{3,2,1,0:T(8,128)S(1)} %shard_map.46.a), channel_id=1, source_target_pairs={{0,32},{1,2},{2,1},{3,4},{4,3},{5,6},{6,5},{7,8},{8,7},{9,10},{10,... | collective-permute-start | bytes 1572872 | tf_op jit(solution)/shard_map/ppermute | solution.py:65
  25.5 0.1 collective-permute-start.3
  25.6 0.1 collective-permute-start.5
  25.7 5.7 %collective-permute-start.6 = (f32[2,128,128]{2,1,0:T(8,128)S(1)}, f32[2,128,128]{2,1,0:T(8,128)S(1)}, u32[]{:S(2)}, u32[]{:S(2)}) collective-permute-start(f32[2,128,128]{2,1,0:T(8,128)S(1)} %pad_maximum_fusion.2), channel_id=1, source_target_pairs={{0,14},{1,15},{2,0},{3,1},{4,2},{5,3},{6,4},{7,5},{8,6},{9,7},{10,... | collective-permute-start | bytes 393224 | tf_op jit(solution)/shard_map/ppermute | solution.py:531
  31.4 5.9 %collective-permute-done.4.od = f32[2,4,128,128]{3,2,1,0:T(8,128)S(1)} collective-permute-done((f32[2,4,128,128]{3,2,1,0:T(8,128)S(1)}, f32[2,4,128,128]{3,2,1,0:T(8,128)S(1)}, u32[]{:S(2)}, u32[]{:S(2)}) %collective-permute-start.4) | collective-permute-done | bytes 524320 | tf_op jit(solution)/shard_map/ppermute | solution.py:65
  37.3 0.0 collective-permute-start.7
  37.3 0.0 collective-permute-done.5.low
  37.3 0.0 collective-permute-done.6.high
  37.4 0.0 collective-permute-done.3.ev
  37.4 4.7 %shard_map.47 = (f32[16,4,8,128]{3,2,1,0:T(8,128)S(1)}, f32[4,128,128]{2,1,0:T(8,128)S(1)}) custom-call(f32[2,4,128,128]{3,2,1,0:T(8,128)S(1)} %shard_map.46.a, f32[4,4,128,128]{3,2,1,0:T(8,128)S(1)} %maximum_select_fusion.pack, f32[2,4,128,128]{3,2,1,0:T(8,128)S(1)} %collective-permute-done.3.ev, f32[2,4,128,128]{3,2,1,0:T(8,128)S(1)} %collective-permute-done.4.od, ...), custom_call_target="tpu_custom_call" | custom-call | tf_op jit(solution)/shard_map/pallas_call | solution.py:497
  42.1 0.0 collective-permute-done.7.cond_swap
  42.1 21.8 %all_to_all.10.own = f32[16,4,8,128]{3,2,1,0:T(8,128)S(1)} all-to-all(f32[16,4,8,128]{3,2,1,0:T(8,128)S(1)} %get-tuple-element.45), channel_id=1, replica_groups=mesh['tm'=16,'space'=16] {'tm'}, dimensions={0} | all-to-all | bytes 524288 | tf_op jit(solution)/shard_map/all_to_all | solution.py:541
  63.8 0.0 collective-permute-start.8
  63.8 1.5 collective-permute-done.8.other
  65.4 0.1 shard_map.48
  65.5 3.2 %collective-permute-start.9 = (f32[4,12,8,128]{3,2,1,0:T(8,128)S(1)}, f32[4,12,8,128]{3,2,1,0:T(8,128)S(1)}, u32[]{:S(2)}, u32[]{:S(2)}) collective-permute-start(f32[4,12,8,128]{3,2,1,0:T(8,128)S(1)} %get-tuple-element.51), channel_id=1, source_target_pairs={{0,32},{1,2},{2,1},{3,4},{4,3},{5,6},{6,5},{7,24},{8,23},{9,10},{1... | collective-permute-start | bytes 589832 | tf_op jit(solution)/shard_map/ppermute | solution.py:69
  68.6 2.3 %collective-permute-start.11 = (f32[4,128,128]{2,1,0:T(8,128)S(1)}, f32[4,128,128]{2,1,0:T(8,128)S(1)}, u32[]{:S(2)}, u32[]{:S(2)}) collective-permute-start(f32[4,128,128]{2,1,0:T(8,128)S(1)} %get-tuple-element.52), channel_id=1, source_target_pairs={{0,16},{16,32},{32,48},{48,64},{64,80},{80,96},{96,112},{112,128},... | collective-permute-start | bytes 786440 | tf_op jit(solution)/shard_map/ppermute | solution.py:543
  70.9 1.9 %collective-permute-done.9.got.xg = f32[4,12,8,128]{3,2,1,0:T(8,128)S(1)} collective-permute-done((f32[4,12,8,128]{3,2,1,0:T(8,128)S(1)}, f32[4,12,8,128]{3,2,1,0:T(8,128)S(1)}, u32[]{:S(2)}, u32[]{:S(2)}) %collective-permute-start.9) | collective-permute-done | bytes 196640 | tf_op jit(solution)/shard_map/ppermute | solution.py:69
  72.7 0.0 collective-permute-start.10
  72.7 1.4 collective-permute-done.10.swap.xs
  74.2 0.1 shard_map.49
  74.3 2.8 %collective-permute-done.11.w = f32[4,128,128]{2,1,0:T(8,128)S(1)} collective-permute-done((f32[4,128,128]{2,1,0:T(8,128)S(1)}, f32[4,128,128]{2,1,0:T(8,128)S(1)}, u32[]{:S(2)}, u32[]{:S(2)}) %collective-permute-start.11) | collective-permute-done | bytes 262176 | tf_op jit(solution)/shard_map/ppermute | solution.py:543
  77.1 0.0 collective-permute-start.12
  77.1 6.1 %collective-permute-done.12.yg = f32[4,18,8,128]{3,2,1,0:T(8,128)S(1)} collective-permute-done((f32[4,18,8,128]{3,2,1,0:T(8,128)S(1)}, f32[4,18,8,128]{3,2,1,0:T(8,128)S(1)}, u32[]{:S(2)}, u32[]{:S(2)}) %collective-permute-start.12) | collective-permute-done | bytes 294944 | tf_op jit(solution)/shard_map/ppermute | solution.py:73
  83.3 0.0 collective-permute-start.13
  83.3 1.6 %collective-permute-done.13.ys = f32[4,18,8,128]{3,2,1,0:T(8,128)S(1)} collective-permute-done((f32[4,18,8,128]{3,2,1,0:T(8,128)S(1)}, f32[4,18,8,128]{3,2,1,0:T(8,128)S(1)}, u32[]{:S(2)}, u32[]{:S(2)}) %collective-permute-start.13) | collective-permute-done | bytes 294944 | tf_op jit(solution)/shard_map/ppermute | solution.py:61
  84.8 1.1 shard_map.50
  86.0 1.3 collective-permute-start.14
  87.3 3.1 %shard_map.51 = (f32[12,4,8,128]{3,2,1,0:T(8,128)S(1)}, f32[12,4,8,128]{3,2,1,0:T(8,128)S(1)}, f32[3,8,8,128]{3,2,1,0:T(8,128)S(1)}, f32[24,24,128]{2,1,0:T(8,12...) custom-call(f32[24,24,128]{2,1,0:T(8,128)S(1)} %get-tuple-element.49, ...), custom_call_target="tpu_custom_call" | custom-call | flops 30000000 | bytes 4000000 | tf_op jit(solution)/shard_map/pallas_call | solution.py:497
  90.4 1.1 collective-permute-done.14.xg
  91.5 0.0 collective-permute-start.15
  91.5 1.2 collective-permute-done.15.xs
  92.7 3.5 %collective-permute-start.16 = (f32[24,8,128]{2,1,0:T(8,128)S(1)}, f32[24,8,128]{2,1,0:T(8,128)S(1)}, u32[]{:S(2)}, u32[]{:S(2)}) collective-permute-start(f32[24,8,128]{2,1,0:T(8,128)S(1)} %pad_maximum_fusion.3), channel_id=1, source_target_pairs={{0,225},{1,16},{2,227},{3,18},{4,229},{5,20},{6,231},{7,22},{8,25}... | collective-permute-start | bytes 294920 | tf_op jit(solution)/shard_map/ppermute | solution.py:73
  96.3 2.3 %collective-permute-done.16.yg = f32[24,8,128]{2,1,0:T(8,128)S(1)} collective-permute-done((f32[24,8,128]{2,1,0:T(8,128)S(1)}, f32[24,8,128]{2,1,0:T(8,128)S(1)}, u32[]{:S(2)}, u32[]{:S(2)}) %collective-permute-start.16) | collective-permute-done | bytes 98336 | tf_op jit(solution)/shard_map/ppermute | solution.py:73
  98.6 0.0 collective-permute-start.17
  98.6 1.3 collective-permute-done.17.ys
  99.9 1.4 shard_map.52
  101.2 2.7 %collective-permute-start.18 = (f32[8,8,128]{2,1,0:T(8,128)S(1)}, f32[8,8,128]{2,1,0:T(8,128)S(1)}, u32[]{:S(2)}, u32[]{:S(2)}) collective-permute-start(f32[8,8,128]{2,1,0:T(8,128)S(1)} %get-tuple-element.69.c_in), channel_id=1, source_target_pairs={{0,32},{1,2},{2,1},{3,4},{4,3},{5,6},{6,5},{7,24},{8,23},{9,10},{1... | collective-permute-start | bytes 98312 | tf_op jit(solution)/shard_map/ppermute | solution.py:69
  103.9 2.9 %collective-permute-done.18.xg = f32[8,8,128]{2,1,0:T(8,128)S(1)} collective-permute-done((f32[8,8,128]{2,1,0:T(8,128)S(1)}, f32[8,8,128]{2,1,0:T(8,128)S(1)}, u32[]{:S(2)}, u32[]{:S(2)}) %collective-permute-start.18) | collective-permute-done | bytes 32800 | tf_op jit(solution)/shard_map/ppermute | solution.py:69
  106.8 1.2 collective-permute-done.19.xs
  108.0 4.2 %collective-permute-start.20 = (f32[24,8,128]{2,1,0:T(8,128)S(1)}, f32[24,8,128]{2,1,0:T(8,128)S(1)}, u32[]{:S(2)}, u32[]{:S(2)}) collective-permute-start(f32[24,8,128]{2,1,0:T(8,128)S(1)} %pad_maximum_fusion.4), channel_id=1, source_target_pairs={{0,225},{1,16},{2,227},{3,18},{4,229},{5,20},{6,231},{7,22},{8,25}... | collective-permute-start | bytes 294920 | tf_op jit(solution)/shard_map/ppermute | solution.py:73
  112.3 2.3 %collective-permute-done.20.yg = f32[24,8,128]{2,1,0:T(8,128)S(1)} collective-permute-done((f32[24,8,128]{2,1,0:T(8,128)S(1)}, f32[24,8,128]{2,1,0:T(8,128)S(1)}, u32[]{:S(2)}, u32[]{:S(2)}) %collective-permute-start.20) | collective-permute-done | bytes 98336 | tf_op jit(solution)/shard_map/ppermute | solution.py:73
  114.6 0.0 collective-permute-start.21
  114.6 1.3 collective-permute-done.21.ys
  115.9 1.4 shard_map.53
  117.2 2.5 %collective-permute-start.22 = (f32[8,8,128]{2,1,0:T(8,128)S(1)}, f32[8,8,128]{2,1,0:T(8,128)S(1)}, u32[]{:S(2)}, u32[]{:S(2)}) collective-permute-start(f32[8,8,128]{2,1,0:T(8,128)S(1)} %get-tuple-element.71.c_in), channel_id=1, source_target_pairs={{0,32},{1,2},{2,1},{3,4},{4,3},{5,6},{6,5},{7,24},{8,23},{9,10},{1... | collective-permute-start | bytes 98312 | tf_op jit(solution)/shard_map/ppermute | solution.py:69
  119.7 3.1 %collective-permute-done.22.xg = f32[8,8,128]{2,1,0:T(8,128)S(1)} collective-permute-done((f32[8,8,128]{2,1,0:T(8,128)S(1)}, f32[8,8,128]{2,1,0:T(8,128)S(1)}, u32[]{:S(2)}, u32[]{:S(2)}) %collective-permute-start.22) | collective-permute-done | bytes 32800 | tf_op jit(solution)/shard_map/ppermute | solution.py:69
  122.8 0.0 collective-permute-start.23
  122.8 1.2 collective-permute-done.23.xs
  124.0 4.2 %collective-permute-start.24 = (f32[24,8,128]{2,1,0:T(8,128)S(1)}, f32[24,8,128]{2,1,0:T(8,128)S(1)}, u32[]{:S(2)}, u32[]{:S(2)}) collective-permute-start(f32[24,8,128]{2,1,0:T(8,128)S(1)} %pad_maximum_fusion.5), channel_id=1, source_target_pairs={{0,225},{1,16},{2,227},{3,18},{4,229},{5,20},{6,231},{7,22},{8,25}... | collective-permute-start | bytes 294920 | tf_op jit(solution)/shard_map/ppermute | solution.py:73
  128.3 2.3 %collective-permute-done.24.yg = f32[24,8,128]{2,1,0:T(8,128)S(1)} collective-permute-done((f32[24,8,128]{2,1,0:T(8,128)S(1)}, f32[24,8,128]{2,1,0:T(8,128)S(1)}, u32[]{:S(2)}, u32[]{:S(2)}) %collective-permute-start.24) | collective-permute-done | bytes 98336 | tf_op jit(solution)/shard_map/ppermute | solution.py:73
  130.6 0.0 collective-permute-start.25
  130.6 1.3 collective-permute-done.25.ys
  131.9 1.4 shard_map.54
  133.3 23.1 %all_to_all.11.got = f32[16,2,4,8,128]{4,3,2,1,0:T(8,128)S(1)} all-to-all(f32[16,2,4,8,128]{4,3,2,1,0:T(8,128)S(1)} %pad_maximum_fusion), channel_id=1, replica_groups=mesh['tm'=16,'space'=16] {'tm'}, dimensions={0} | all-to-all | bytes 1048576 | tf_op jit(solution)/shard_map/all_to_all | solution.py:591
  156.4 0.8 shard_map.55
  (18 shorter events, 0.2 us)
Async XLA Ops:
  1.4 2.8 %collective-permute-start = (f32[4,4,128,128]{3,2,1,0:T(8,128)S(1)}, f32[4,4,128,128]{3,2,1,0:T(8,128)S(1)}, u32[]{:S(2)}, u32[]{:S(2)}) collective-permute-start(f32[4,4,128,128]{3,2,1,0:T(8,128)S(1)} %maximum_select_fusion.pack), channel_id=1, source_target_pairs={{0,1},{1,0},{2,3},{3,2},{4,5},{5,4},{6,7},{7,6},{8,9},{9,8},{10,11... | collective-permute-start | bytes 3145736 | tf_op jit(solution)/shard_map/ppermute | solution.py:61
  1.6 18.7 %collective-permute-start.1 = (f32[4,4,128,128]{3,2,1,0:T(8,128)S(1)}, f32[4,4,128,128]{3,2,1,0:T(8,128)S(1)}, u32[]{:S(2)}, u32[]{:S(2)}) collective-permute-start(f32[4,4,128,128]{3,2,1,0:T(8,128)S(1)} %maximum_select_fusion.pack), channel_id=1, source_target_pairs={{0,32},{1,2},{2,1},{3,4},{4,3},{5,6},{6,5},{7,8},{8,7},{9,10},{10,... | collective-permute-start | bytes 3145736 | tf_op jit(solution)/shard_map/ppermute | solution.py:65
  4.3 19.3 %collective-permute-start.2 = (f32[8,24,128]{2,1,0:T(8,128)S(1)}, f32[8,24,128]{2,1,0:T(8,128)S(1)}, u32[]{:S(2)}, u32[]{:S(2)}) collective-permute-start(f32[8,24,128]{2,1,0:T(8,128)S(1)} %maximum_select_fusion.1.cond), channel_id=1, source_target_pairs={{0,32},{1,2},{2,1},{3,4},{4,3},{5,6},{6,5},{7,24},{8,23},{9,10},{1... | collective-permute-start | bytes 294920 | tf_op jit(solution)/shard_map/ppermute | solution.py:69
  23.6 13.7 %collective-permute-start.4 = (f32[2,4,128,128]{3,2,1,0:T(8,128)S(1)}, f32[2,4,128,128]{3,2,1,0:T(8,128)S(1)}, u32[]{:S(2)}, u32[]{:S(2)}) collective-permute-start(f32[2,4,128,128]{3,2,1,0:T(8,128)S(1)} %shard_map.46.a), channel_id=1, source_target_pairs={{0,32},{1,2},{2,1},{3,4},{4,3},{5,6},{6,5},{7,8},{8,7},{9,10},{10,... | collective-permute-start | bytes 1572872 | tf_op jit(solution)/shard_map/ppermute | solution.py:65
  25.5 11.9 %collective-permute-start.3 = (f32[2,4,128,128]{3,2,1,0:T(8,128)S(1)}, f32[2,4,128,128]{3,2,1,0:T(8,128)S(1)}, u32[]{:S(2)}, u32[]{:S(2)}) collective-permute-start(f32[2,4,128,128]{3,2,1,0:T(8,128)S(1)} %shard_map.46.a), channel_id=1, source_target_pairs={{0,1},{1,0},{2,3},{3,2},{4,5},{5,4},{6,7},{7,6},{8,9},{9,8},{10,11... | collective-permute-start | bytes 1572872 | tf_op jit(solution)/shard_map/ppermute | solution.py:61
  25.6 11.7 %collective-permute-start.5 = (f32[2,128,128]{2,1,0:T(8,128)S(1)}, f32[2,128,128]{2,1,0:T(8,128)S(1)}, u32[]{:S(2)}, u32[]{:S(2)}) collective-permute-start(f32[2,128,128]{2,1,0:T(8,128)S(1)} %pad_maximum_fusion.1), channel_id=1, source_target_pairs={{0,2},{1,3},{2,4},{3,5},{4,6},{5,7},{6,8},{7,9},{8,10},{9,11},{10,... | collective-permute-start | bytes 393224 | tf_op jit(solution)/shard_map/ppermute | solution.py:530
  25.7 11.6 %collective-permute-start.6 = (f32[2,128,128]{2,1,0:T(8,128)S(1)}, f32[2,128,128]{2,1,0:T(8,128)S(1)}, u32[]{:S(2)}, u32[]{:S(2)}) collective-permute-start(f32[2,128,128]{2,1,0:T(8,128)S(1)} %pad_maximum_fusion.2), channel_id=1, source_target_pairs={{0,14},{1,15},{2,0},{3,1},{4,2},{5,3},{6,4},{7,5},{8,6},{9,7},{10,... | collective-permute-start | bytes 393224 | tf_op jit(solution)/shard_map/ppermute | solution.py:531
  37.3 4.7 %collective-permute-start.7 = (f32[8,24,128]{2,1,0:T(8,128)S(1)}, f32[8,24,128]{2,1,0:T(8,128)S(1)}, u32[]{:S(2)}, u32[]{:S(2)}) collective-permute-start(f32[8,24,128]{2,1,0:T(8,128)S(1)} %collective-permute-done.2.cond_got), channel_id=1, source_target_pairs={{0,1},{1,0},{2,3},{3,2},{4,5},{5,4},{6,7},{7,6},{8,9},{9,8},{10,11... | collective-permute-start | bytes 294920 | tf_op jit(solution)/shard_map/ppermute | solution.py:61
  63.8 1.5 collective-permute-start.8
  65.5 7.3 %collective-permute-start.9 = (f32[4,12,8,128]{3,2,1,0:T(8,128)S(1)}, f32[4,12,8,128]{3,2,1,0:T(8,128)S(1)}, u32[]{:S(2)}, u32[]{:S(2)}) collective-permute-start(f32[4,12,8,128]{3,2,1,0:T(8,128)S(1)} %get-tuple-element.51), channel_id=1, source_target_pairs={{0,32},{1,2},{2,1},{3,4},{4,3},{5,6},{6,5},{7,24},{8,23},{9,10},{1... | collective-permute-start | bytes 589832 | tf_op jit(solution)/shard_map/ppermute | solution.py:69
  68.6 8.5 %collective-permute-start.11 = (f32[4,128,128]{2,1,0:T(8,128)S(1)}, f32[4,128,128]{2,1,0:T(8,128)S(1)}, u32[]{:S(2)}, u32[]{:S(2)}) collective-permute-start(f32[4,128,128]{2,1,0:T(8,128)S(1)} %get-tuple-element.52), channel_id=1, source_target_pairs={{0,16},{16,32},{32,48},{48,64},{64,80},{80,96},{96,112},{112,128},... | collective-permute-start | bytes 786440 | tf_op jit(solution)/shard_map/ppermute | solution.py:543
  72.7 1.4 collective-permute-start.10
  77.1 6.1 %collective-permute-start.12 = (f32[4,18,8,128]{3,2,1,0:T(8,128)S(1)}, f32[4,18,8,128]{3,2,1,0:T(8,128)S(1)}, u32[]{:S(2)}, u32[]{:S(2)}) collective-permute-start(f32[4,18,8,128]{3,2,1,0:T(8,128)S(1)} %shard_map.49), channel_id=1, source_target_pairs={{0,225},{1,16},{2,227},{3,18},{4,229},{5,20},{6,231},{7,22},{8,25}... | collective-permute-start | bytes 884744 | tf_op jit(solution)/shard_map/ppermute | solution.py:73
  83.3 1.6 %collective-permute-start.13 = (f32[4,18,8,128]{3,2,1,0:T(8,128)S(1)}, f32[4,18,8,128]{3,2,1,0:T(8,128)S(1)}, u32[]{:S(2)}, u32[]{:S(2)}) collective-permute-start(f32[4,18,8,128]{3,2,1,0:T(8,128)S(1)} %collective-permute-done.12.yg), channel_id=1, source_target_pairs={{0,1},{1,0},{2,3},{3,2},{4,5},{5,4},{6,7},{7,6},{8,9},{9,8},{10,11... | collective-permute-start | bytes 884744 | tf_op jit(solution)/shard_map/ppermute | solution.py:61
  86.0 5.5 %collective-permute-start.14 = (f32[8,8,128]{2,1,0:T(8,128)S(1)}, f32[8,8,128]{2,1,0:T(8,128)S(1)}, u32[]{:S(2)}, u32[]{:S(2)}) collective-permute-start(f32[8,8,128]{2,1,0:T(8,128)S(1)} %get-tuple-element.55.c_in), channel_id=1, source_target_pairs={{0,32},{1,2},{2,1},{3,4},{4,3},{5,6},{6,5},{7,24},{8,23},{9,10},{1... | collective-permute-start | bytes 98312 | tf_op jit(solution)/shard_map/ppermute | solution.py:69
  91.5 1.2 collective-permute-start.15
  92.7 5.8 %collective-permute-start.16 = (f32[24,8,128]{2,1,0:T(8,128)S(1)}, f32[24,8,128]{2,1,0:T(8,128)S(1)}, u32[]{:S(2)}, u32[]{:S(2)}) collective-permute-start(f32[24,8,128]{2,1,0:T(8,128)S(1)} %pad_maximum_fusion.3), channel_id=1, source_target_pairs={{0,225},{1,16},{2,227},{3,18},{4,229},{5,20},{6,231},{7,22},{8,25}... | collective-permute-start | bytes 294920 | tf_op jit(solution)/shard_map/ppermute | solution.py:73
  98.6 1.3 collective-permute-start.17
  101.2 5.5 %collective-permute-start.18 = (f32[8,8,128]{2,1,0:T(8,128)S(1)}, f32[8,8,128]{2,1,0:T(8,128)S(1)}, u32[]{:S(2)}, u32[]{:S(2)}) collective-permute-start(f32[8,8,128]{2,1,0:T(8,128)S(1)} %get-tuple-element.69.c_in), channel_id=1, source_target_pairs={{0,32},{1,2},{2,1},{3,4},{4,3},{5,6},{6,5},{7,24},{8,23},{9,10},{1... | collective-permute-start | bytes 98312 | tf_op jit(solution)/shard_map/ppermute | solution.py:69
  106.8 1.2 collective-permute-start.19
  108.0 6.5 %collective-permute-start.20 = (f32[24,8,128]{2,1,0:T(8,128)S(1)}, f32[24,8,128]{2,1,0:T(8,128)S(1)}, u32[]{:S(2)}, u32[]{:S(2)}) collective-permute-start(f32[24,8,128]{2,1,0:T(8,128)S(1)} %pad_maximum_fusion.4), channel_id=1, source_target_pairs={{0,225},{1,16},{2,227},{3,18},{4,229},{5,20},{6,231},{7,22},{8,25}... | collective-permute-start | bytes 294920 | tf_op jit(solution)/shard_map/ppermute | solution.py:73
  114.6 1.3 collective-permute-start.21
  117.2 5.5 %collective-permute-start.22 = (f32[8,8,128]{2,1,0:T(8,128)S(1)}, f32[8,8,128]{2,1,0:T(8,128)S(1)}, u32[]{:S(2)}, u32[]{:S(2)}) collective-permute-start(f32[8,8,128]{2,1,0:T(8,128)S(1)} %get-tuple-element.71.c_in), channel_id=1, source_target_pairs={{0,32},{1,2},{2,1},{3,4},{4,3},{5,6},{6,5},{7,24},{8,23},{9,10},{1... | collective-permute-start | bytes 98312 | tf_op jit(solution)/shard_map/ppermute | solution.py:69
  122.8 1.2 collective-permute-start.23
  124.0 6.5 %collective-permute-start.24 = (f32[24,8,128]{2,1,0:T(8,128)S(1)}, f32[24,8,128]{2,1,0:T(8,128)S(1)}, u32[]{:S(2)}, u32[]{:S(2)}) collective-permute-start(f32[24,8,128]{2,1,0:T(8,128)S(1)} %pad_maximum_fusion.5), channel_id=1, source_target_pairs={{0,225},{1,16},{2,227},{3,18},{4,229},{5,20},{6,231},{7,22},{8,25}... | collective-permute-start | bytes 294920 | tf_op jit(solution)/shard_map/ppermute | solution.py:73
  130.6 1.3 collective-permute-start.25
